TPU v7x, 32 devices: a whole 2x2x4 slice. The times are simulated.
32 devices in a mesh: dp: 4 (over z), pair: 8 (over y, x, core).
Axes of the slice: x: 2, y: 2, z: 4, core: 2. Of those that a mesh axis runs over, the one named last changes fastest.
Arguments:
- embeddings: bfloat16 [128, 512, 256], P('pair', 'dp'), may hold values from -6 to 6
- field_width: int32 [128], replicated, may hold values from 64 to 256, as said below
- pair_fields: int32 [384, 2], replicated, may hold values from 0 to 127, as said below
- pair_mats: bfloat16 [384, 256, 256], P('pair'), may hold values from -0.0048828125 to 0.0048828125
- labels: int32 [512], P('dp'), may hold values 0 or 1
Outputs:
- logits: float32 [512], P('dp')
- mat_grad: bfloat16 [384, 256, 256], P('pair', 'dp')
- emb_grad: float32 [128, 512, 256], P('pair', 'dp')
Inputs may be any that keep to these rules, and one draw needn't show every extreme that they name: `field_width`: each is 64, 128 or 256. `pair_fields`: the two fields of a pair differ. The 48 pairs of one owner read at most 3 different fields from the 16 fields of any one owner (field f is owned by index f // 16), and exactly 3 from some owner.
All inputs are finite; a program needn't handle non-finite values. No bound on the sum of `labels` on one device may be relied on, other than what follows from the above.
Results may differ from a plain program's by a relative error of at most 0.017.
Values may be sent and summed in bfloat16 or wider, within the bound.
No kernel may reach another device: no remote copies, remote signals or barrier semaphores. Data moves between devices by JAX's collectives and lax.ppermute only.
A program may use at most 128 MiB of HBM per device.

v0:
```python
import jax
import jax.numpy as jnp
from jax import lax
from jax.sharding import PartitionSpec as P

CAP = 3


def shards(embeddings, field_width, pair_fields, pair_mats, labels):
    owners = lax.axis_size("pair")
    owner_index = lax.axis_index("pair")
    field_count = embeddings.shape[0]
    sample_count = embeddings.shape[1]
    padded_width = embeddings.shape[2]
    pair_count = pair_mats.shape[0]
    column_ids = jnp.arange(padded_width, dtype=jnp.int32)
    width_mask = (column_ids[None, :] < field_width[:, None]).astype(jnp.bfloat16)
    own_mask = lax.dynamic_slice_in_dim(width_mask, owner_index * field_count, field_count, 0)
    masked = embeddings * own_mask[:, None, :]
    my_fields = owner_index * field_count + jnp.arange(field_count, dtype=jnp.int32)
    grouped = pair_fields.reshape(owners, pair_count * 2)
    needed = jnp.any(grouped[:, :, None] == my_fields[None, None, :], axis=1)
    slot_rank = jnp.cumsum(needed.astype(jnp.int32), axis=1) - 1
    slot_ids = jnp.arange(CAP, dtype=jnp.int32)
    selector = (needed[:, None, :] & (slot_rank[:, None, :] == slot_ids[None, :, None])).astype(
        jnp.bfloat16
    )
    outgoing = jnp.einsum("dcf,fsk->dcsk", selector, masked, preferred_element_type=jnp.bfloat16)
    incoming = lax.all_to_all(outgoing, "pair", split_axis=0, concat_axis=0, tiled=True)
    received = incoming.reshape(owners * CAP, sample_count, padded_width)
    my_pairs = lax.dynamic_slice_in_dim(pair_fields, owner_index * pair_count, pair_count, 0)
    every_field = jnp.arange(owners * field_count, dtype=jnp.int32)
    wanted = jnp.any(my_pairs.reshape(-1)[:, None] == every_field[None, :], axis=0).reshape(
        owners, field_count
    )
    slot_table = (jnp.cumsum(wanted.astype(jnp.int32), axis=1) - 1).reshape(-1)
    slot_index = my_pairs // field_count * CAP + slot_table[my_pairs]
    left_rows = received[slot_index[:, 0]]
    right_rows = received[slot_index[:, 1]]
    projected = jnp.einsum("psk,pkl->psl", left_rows, pair_mats, preferred_element_type=jnp.float32)
    partial_value = jnp.sum(projected * right_rows, axis=(0, 2))
    logits = lax.psum(partial_value, "pair")
    grad_out = jax.nn.sigmoid(logits) - labels.astype(jnp.float32)
    toward_left = grad_out[None, :, None] * jnp.einsum(
        "psl,pkl->psk", right_rows, pair_mats, preferred_element_type=jnp.float32
    )
    toward_right = grad_out[None, :, None] * projected
    slot_grads = jnp.zeros((owners * CAP, sample_count, padded_width), jnp.float32)
    slot_grads = (
        slot_grads.at[slot_index[:, 0]].add(toward_left).at[slot_index[:, 1]].add(toward_right)
    )
    slot_grads = slot_grads.astype(jnp.bfloat16).reshape(owners, CAP, sample_count, padded_width)
    returned = lax.all_to_all(slot_grads, "pair", split_axis=0, concat_axis=0, tiled=True)
    emb_grad = jnp.einsum("dcf,dcsk->fsk", selector, returned, preferred_element_type=jnp.float32)
    emb_grad = emb_grad * own_mask[:, None, :].astype(jnp.float32)
    scaled = (grad_out[None, :, None] * left_rows).astype(jnp.bfloat16)
    mat_term = jnp.einsum("psk,psl->pkl", scaled, right_rows, preferred_element_type=jnp.float32)
    mat_grad = lax.psum_scatter(
        mat_term.astype(jnp.bfloat16), "dp", scatter_dimension=1, tiled=True
    )
    return (logits, mat_grad, emb_grad)


def solution(mesh):
    in_specs = (P("pair", "dp", None), P(), P(), P("pair", None, None), P("dp"))
    out_specs = (P("dp"), P("pair", "dp", None), P("pair", "dp", None))
    return jax.shard_map(shards, mesh=mesh, in_specs=in_specs, out_specs=out_specs, check_vma=False)
```

profile of v0, /device:TPU:0, one launch (start us, length us, event | category | flops | bytes accessed | tf_op | source)
XLA Modules:
  0.0 190.4 jit_solution(742963178127088369)
XLA Ops:
  7.2 0.7 dynamic-slice
  8.0 0.8 copy.34
  8.8 0.1 eq.43
  9.0 0.3 compare_reduce_fusion
  9.2 0.2 reduce_window_sum.17
  9.4 1.3 broadcast_multiply_fusion.2
  10.7 0.7 fusion.2
  11.5 1.5 copy.36
  13.0 5.2 %all-to-all-start = ((bf16[8,3,128,256]{3,2,1,0:T(8,128)(2,1)}), bf16[8,3,128,256]{3,2,1,0:T(8,128)(2,1)S(1)}, u32[]{:S(2)}, u32[]{:S(2)}) async-start(bf16[8,3,128,256]{3,2,1,0:T(8,128)(2,1)} %copy.36), calls=%async_computation | async-start | bytes 3145728 | tf_op jit(solution)/shard_map/all_to_all | solution.py:29
  18.2 0.1 eq.50
  18.5 0.2 reduce_window_sum.18
  18.8 0.1 reshape.45
  18.9 1.2 gather_fusion
  20.2 0.1 reshape.44
  20.3 0.2 fusion.10
  20.5 18.7 %all-to-all-done = bf16[8,3,128,256]{3,2,1,0:T(8,128)(2,1)S(1)} async-done(((bf16[8,3,128,256]{3,2,1,0:T(8,128)(2,1)}), bf16[8,3,128,256]{3,2,1,0:T(8,128)(2,1)S(1)}, u32[]{:S(2)}, u32[]{:S(2)}) %all-to-all-start) | async-done | bytes 1572896 | tf_op jit(solution)/shard_map/all_to_all | solution.py:29
  39.2 1.1 copy-done
  40.3 2.2 %gather_fusion.2 = bf16[48,128,256]{2,1,0:T(8,128)(2,1)S(1)} fusion(bf16[24,128,256]{2,1,0:T(8,128)(2,1)} %bitcast.20, s32[1024]{0:T(1024)S(1)} %get-tuple-element.26), kind=kCustom, calls=%fused_computation.2 | custom fusion | bytes 6291648 | tf_op jit(solution)/shard_map/gather | solution.py:39
  42.5 3.9 %gather_fusion.1 = bf16[48,128,256]{2,1,0:T(8,128)(2,1)} fusion(bf16[24,128,256]{2,1,0:T(8,128)(2,1)} %bitcast.21, s32[1024]{0:T(1024)S(1)} %get-tuple-element.27), kind=kCustom, calls=%fused_computation.1 | custom fusion | bytes 6291648 | tf_op jit(solution)/shard_map/gather | solution.py:38
  46.4 7.4 %multiply_reduce_fusion = (f32[128]{0:T(128)S(1)}, f32[48,128,256]{2,1,0:T(8,128)}) fusion(bf16[48,128,256]{2,1,0:T(8,128)(2,1)S(1)} %gather_fusion.2, bf16[48,128,256]{2,1,0:T(8,128)(2,1)} %gather_fusion.1, bf16[48,256,256]{2,1,0:T(8,128)(2,1)} %param.8), kind=kOutput, calls=%fused_computation.6 | convolution fusion | flops 810024832 | bytes 18874880 | tf_op jit(solution)/shard_map/psk,pkl->psl/dot_general | solution.py:40
  53.8 11.8 %psum.7 = f32[128]{0:T(128)S(1)} all-reduce(f32[128]{0:T(128)S(1)} %get-tuple-element.24), channel_id=1, replica_groups=mesh['dp'=4,'pair'=8] {'pair'}, use_global_device_ids=true, to_apply=%region_5.6 | all-reduce | flops 128 | bytes 1024 | tf_op jit(solution)/shard_map/psum | solution.py:42
  65.6 6.5 %convolution_convert_fusion = bf16[48,256,256]{2,1,0:T(8,128)(2,1)} fusion(bf16[48,128,256]{2,1,0:T(8,128)(2,1)S(1)} %gather_fusion.2, bf16[48,128,256]{2,1,0:T(8,128)(2,1)} %gather_fusion.1, f32[128]{0:T(128)S(1)} %divide_subtract_fusion), kind=kOutput, calls=%fused_computation.7 | convolution fusion | flops 813170688 | bytes 12583424 | tf_op jit(solution)/shard_map/psk,psl->pkl/dot_general | solution.py:57
  72.2 8.2 %broadcast_multiply_fusion.1 = f32[48,128,256]{2,1,0:T(8,128)} fusion(f32[128]{0:T(128)S(1)} %divide_subtract_fusion, bf16[48,128,256]{2,1,0:T(8,128)(2,1)S(1)} %gather_fusion.2, bf16[48,256,256]{2,1,0:T(8,128)(2,1)} %param.8), kind=kOutput, calls=%fused_computation.9 | convolution fusion | flops 806879232 | bytes 15729152 | tf_op jit(solution)/shard_map/psl,pkl->psk/dot_general | solution.py:44
  80.4 0.3 broadcast_in_dim.5
  80.8 9.5 %scatter_fusion = f32[24,128,256]{2,1,0:T(8,128)S(1)} fusion(f32[24,128,256]{2,1,0:T(8,128)S(1)} %broadcast_in_dim.5, s32[48]{0:T(128)S(1)} %get-tuple-element.19, f32[48,128,256]{2,1,0:T(8,128)} %broadcast_multiply_fusion.1), kind=kCustom, calls=%fused_computation.3 | custom fusion | flops 1572864 | bytes 18874560 | tf_op jit(solution)/shard_map/scatter-add | solution.py:50
  90.3 6.5 %broadcast_multiply_fusion = f32[48,128,256]{2,1,0:T(8,128)} fusion(f32[48,128,256]{2,1,0:T(8,128)} %get-tuple-element.25, f32[128]{0:T(128)S(1)} %divide_subtract_fusion), kind=kLoop, calls=%fused_computation.8 | loop fusion | flops 1572864 | bytes 12583424 | tf_op jit(solution)/shard_map/mul | solution.py:47
  96.8 9.5 %scatter_fusion.1 = f32[24,128,256]{2,1,0:T(8,128)S(1)} fusion(f32[24,128,256]{2,1,0:T(8,128)S(1)} %scatter_fusion, s32[48]{0:T(128)S(1)} %get-tuple-element.18, f32[48,128,256]{2,1,0:T(8,128)} %broadcast_multiply_fusion), kind=kCustom, calls=%fused_computation.4 | custom fusion | flops 1572864 | bytes 18874560 | tf_op jit(solution)/shard_map/scatter-add | solution.py:50
  106.2 0.2 convert_element_type.48
  106.5 23.7 %all_to_all.10 = bf16[8,3,128,256]{3,2,1,0:T(8,128)(2,1)S(1)} all-to-all(bf16[8,3,128,256]{3,2,1,0:T(8,128)(2,1)S(1)} %bitcast.22), channel_id=1, replica_groups=mesh['dp'=4,'pair'=8] {'pair'}, dimensions={0} | all-to-all | bytes 3145728 | tf_op jit(solution)/shard_map/all_to_all | solution.py:53
  130.1 1.0 bitcast_multiply_fusion
  131.1 2.5 %copy.40 = f32[16,128,256]{2,1,0:T(8,128)} copy(f32[16,128,256]{2,0,1:T(8,128)S(1)} %bitcast_multiply_fusion) | data formatting | bytes 4194304
  133.7 49.9 %reduce-scatter.2.cloned.1.call-done = bf16[48,64,256]{2,1,0:T(8,128)(2,1)} async-done(((bf16[48,256,256]{2,1,0:T(8,128)(2,1)}), bf16[48,64,256]{2,1,0:T(8,128)(2,1)}) %reduce-scatter.2.cloned.1.call-update) | async-done | bytes 1572880 | tf_op jit(solution)/shard_map/reduce_scatter | solution.py:58
  (21 shorter events, 0.5 us)
Async XLA Ops:
  13.0 26.2 %all-to-all-start = ((bf16[8,3,128,256]{3,2,1,0:T(8,128)(2,1)}), bf16[8,3,128,256]{3,2,1,0:T(8,128)(2,1)S(1)}, u32[]{:S(2)}, u32[]{:S(2)}) async-start(bf16[8,3,128,256]{3,2,1,0:T(8,128)(2,1)} %copy.36), calls=%async_computation | async-start | bytes 3145728 | tf_op jit(solution)/shard_map/all_to_all | solution.py:29
  18.2 165.4 %reduce-scatter.2.cloned.1.call-start = ((), (), s32[]{:S(2)}) async-start(), calls=%async_computation.3 | async-start | bytes 7864320 | tf_op jit(solution)/shard_map/reduce_scatter | solution.py:58
  39.2 1.1 copy-start
  46.4 19.2 %copy-start.1 = (s32[128]{0:T(128)S(1)}, s32[128]{0:T(128)}, u32[]{:S(2)}) copy-start(s32[128]{0:T(128)} %param.9) | copy-start | bytes 1540
  65.6 6.6 %copy-start.2 = (f32[128]{0:T(128)}, f32[128]{0:T(128)S(1)}, u32[]{:S(2)}) copy-start(f32[128]{0:T(128)S(1)} %psum.7) | copy-start | bytes 1540
Sparse Core Ops, SparseCore 0:
  72.3 111.1 reduce-scatter.1
where the time goes:
time: 191 us; the launch traced here: 190 us
  waiting for transfers between devices  68.6 us (36%)
  blocking collectives  35.4 us (19%)
  other arithmetic  28 us (15%)
  matrix products  23.9 us (13%)
  local copies, waits for them, and re-layouts  15 us (8%)
  between operations  14.2 us (7%)
  starting transfers between devices  5.21 us (3%)
    reduce_scatter x1, waiting for transfers between devices, shards(): lax.psum_scatter(mat_term.astype(jnp.bfloat16), 'dp', scatter_dimension=1...  49.9 us
    all_to_all x1, blocking collectives, shards(): lax.all_to_all(slot_grads, 'pair', split_axis=0, concat_axis=0, tiled=True)  23.7 us
    scatter-add x2, other arithmetic, shards(): slot_grads.at[slot_index[:, 0]].add(toward_left).at[slot_index[:, 1]]  19 us
    all_to_all x1, waiting for transfers between devices, shards(): lax.all_to_all(outgoing, 'pair', split_axis=0, concat_axis=0, tiled=True)  18.7 us
    psum x1, blocking collectives, shards(): logits = lax.psum(partial_value, 'pair')  11.8 us
    dot_general x1, matrix products, shards(): jnp.einsum('psl,pkl->psk', right_rows, pair_mats, preferred_element_type=...  8.23 us
    dot_general x1, matrix products, shards(): jnp.einsum('psk,pkl->psl', left_rows, pair_mats, preferred_element_type=j...  7.41 us
    dot_general x1, matrix products, shards(): jnp.einsum('psk,psl->pkl', scaled, right_rows, preferred_element_type=jnp...  6.53 us
  transfers between devices with their start and end apart: 2, of which 2 were waited for; matrix products, arithmetic and copies ran while one was open for 21% of the time, Pallas kernels for 0%

commit v1 on v0

v1 whole, which is shorter than its diff:
```python
import functools

import jax
import jax.numpy as jnp
from jax import lax
from jax.experimental import pallas as pl
from jax.experimental.pallas import tpu as pltpu
from jax.sharding import PartitionSpec as P

CAP = 3
VMEM = pl.BlockSpec(memory_space=pltpu.VMEM)
SMEM = pl.BlockSpec(memory_space=pltpu.SMEM)
HBM = pl.BlockSpec(memory_space=pl.ANY)
F32 = jnp.float32
BF16 = jnp.bfloat16


def pick_rows_kernel(which_ref, table_ref, *refs):
    *sources, out_ref, sems = refs
    slots = out_ref.shape[0]
    for at, source in enumerate(sources):

        @pl.when(which_ref[0] == at)
        def _(source=source):
            @pl.loop(0, slots)
            def _(j):
                pltpu.make_async_copy(source.at[table_ref[j]], out_ref.at[j], sems.at[j]).start()

    @pl.loop(0, slots)
    def _(j):
        pltpu.make_async_copy(sources[0].at[0], out_ref.at[j], sems.at[j]).wait()


def pick_rows(which, table, sources):
    shape = (table.shape[0],) + sources[0].shape[1:]
    size = shape[0] * shape[1] * shape[2] * 2
    return pl.pallas_call(
        pick_rows_kernel,
        out_shape=jax.ShapeDtypeStruct(shape, BF16),
        in_specs=[SMEM, SMEM] + [HBM] * len(sources),
        out_specs=HBM,
        scratch_shapes=[pltpu.SemaphoreType.DMA((shape[0],))],
        cost_estimate=pl.CostEstimate(flops=0, bytes_accessed=2 * size, transcendentals=0),
    )(which, table, *sources)


def forward_kernel(group, slot_ref, width_ref, rows_ref, mats_ref, part_ref, sums_ref, x_ref, u_ref, acc_ref):
    step = pl.program_id(0)
    slots, samples, width = x_ref.shape

    @pl.when(step == 0)
    def _():
        columns = lax.broadcasted_iota(jnp.int32, (samples, width), 1)

        @pl.loop(0, slots)
        def _(j):
            x_ref[j] = jnp.where(columns < width_ref[j], rows_ref[j], jnp.zeros_like(rows_ref[j]))
            u_ref[j] = jnp.zeros((samples, width), F32)

        acc_ref[...] = jnp.zeros_like(acc_ref)

    for k in range(group):
        p = step * group + k
        a, b = slot_ref[2 * p], slot_ref[2 * p + 1]
        left, right, mat = x_ref[a], x_ref[b], mats_ref[k]
        projected = jnp.dot(left, mat, preferred_element_type=F32)
        back = lax.dot_general(right, mat, (((1,), (1,)), ((), ())), preferred_element_type=F32)
        acc_ref[...] += projected * right.astype(F32)
        u_ref[b] += projected
        u_ref[a] += back

    @pl.when(step == pl.num_programs(0) - 1)
    def _():
        @pl.loop(0, slots)
        def _(j):
            sums_ref[j] = u_ref[j].astype(BF16)

        total = acc_ref[:, 0:128]
        for at in range(128, width, 128):
            total = total + acc_ref[:, at : at + 128]
        part_ref[...] = jnp.sum(total.T, axis=0, keepdims=True)


def forward(slot_index, slot_width, rows, mats, group=4):
    slots, samples, width = rows.shape
    pairs = mats.shape[0]
    whole = lambda *shape: pl.BlockSpec(shape, lambda i: (0,) * len(shape))
    return pl.pallas_call(
        functools.partial(forward_kernel, group),
        grid=(pairs // group,),
        out_shape=(
            jax.ShapeDtypeStruct((1, samples), F32),
            jax.ShapeDtypeStruct(rows.shape, BF16),
        ),
        in_specs=[SMEM, SMEM, whole(*rows.shape), pl.BlockSpec((group, width, width), lambda i: (i, 0, 0))],
        out_specs=(whole(1, samples), whole(*rows.shape)),
        scratch_shapes=[
            pltpu.VMEM(rows.shape, BF16),
            pltpu.VMEM(rows.shape, F32),
            pltpu.VMEM((samples, width), F32),
        ],
        compiler_params=pltpu.CompilerParams(vmem_limit_bytes=60 * 2**20),
        cost_estimate=pl.CostEstimate(
            flops=4 * pairs * samples * width * width, bytes_accessed=2 * pairs * width * width, transcendentals=0
        ),
    )(slot_index, slot_width, rows, mats)


def emb_grad_kernel(table_ref, width_ref, back_ref, grad_ref, out_ref):
    fields, samples, width = out_ref.shape

    @pl.loop(0, fields)
    def _(f):
        out_ref[f] = jnp.zeros((samples, width), F32)

    @pl.loop(0, back_ref.shape[0])
    def _(j):
        f = table_ref[j]
        out_ref[f] += back_ref[j].astype(F32)

    grad = jnp.broadcast_to(grad_ref[...], (128, samples)).T
    grad = jnp.concatenate([grad] * (width // 128), axis=1)
    columns = lax.broadcasted_iota(jnp.int32, (samples, width), 1)

    @pl.loop(0, fields)
    def _(f):
        out_ref[f] = jnp.where(columns < width_ref[f], out_ref[f] * grad, 0.0)


def emb_grad_of(table, own_width, back, grad, fields):
    slots, samples, width = back.shape
    return pl.pallas_call(
        emb_grad_kernel,
        out_shape=jax.ShapeDtypeStruct((fields, samples, width), F32),
        in_specs=[SMEM, SMEM, VMEM, VMEM],
        out_specs=VMEM,
        compiler_params=pltpu.CompilerParams(vmem_limit_bytes=60 * 2**20),
        cost_estimate=pl.CostEstimate(
            flops=slots * samples * width, bytes_accessed=fields * samples * width * 6, transcendentals=0
        ),
    )(table, own_width, back, grad)


def mat_grad_kernel(count, slot_ref, width_ref, source_ref, first_ref, grads_ref, *refs):
    blocks = refs[:count]
    out_ref, x_ref, t_ref, acc_ref, sems = refs[count:]
    _, slots, samples, width = x_ref.shape
    pairs, rows, _ = acc_ref.shape
    columns = lax.broadcasted_iota(jnp.int32, (samples, width), 1)
    own_row = lax.broadcasted_iota(jnp.int32, (rows, width), 0) + first_ref[0]
    pick = (lax.broadcasted_iota(jnp.int32, (rows, width), 1) == own_row).astype(BF16)

    def load(at):
        return pltpu.make_async_copy(blocks[at], x_ref.at[at % 2], sems.at[at % 2])

    load(0).start()
    for at in range(count):
        if at + 1 < count:
            load(at + 1).start()
        load(at).wait()
        now = at % 2
        grad = grads_ref[source_ref[at]]

        @pl.loop(0, slots)
        def _(j):
            x = jnp.where(columns < width_ref[j], x_ref[now, j], jnp.zeros((samples, width), BF16))
            x_ref[now, j] = x
            turned = lax.dot_general(pick, x, (((1,), (1,)), ((), ())), preferred_element_type=F32)
            t_ref[j] = (turned * grad).astype(BF16)

        @pl.loop(0, pairs, unroll=4)
        def _(p):
            a, b = slot_ref[2 * p], slot_ref[2 * p + 1]
            term = jnp.dot(t_ref[a], x_ref[now, b], preferred_element_type=F32)
            if at == 0:
                acc_ref[p] = term
            elif at < count - 1:
                acc_ref[p] += term
            else:
                out_ref[p] = (acc_ref[p] + term).astype(BF16)


def mat_grad_of(slot_index, slot_width, sources, first, grads, blocks, rows):
    slots, samples, width = blocks[0].shape
    pairs = slot_index.shape[0] // 2
    return pl.pallas_call(
        functools.partial(mat_grad_kernel, len(blocks)),
        out_shape=jax.ShapeDtypeStruct((pairs, rows, width), BF16),
        in_specs=[SMEM, SMEM, SMEM, SMEM, VMEM] + [HBM] * len(blocks),
        out_specs=VMEM,
        scratch_shapes=[
            pltpu.VMEM((2, slots, samples, width), BF16),
            pltpu.VMEM((slots, rows, samples), BF16),
            pltpu.VMEM((pairs, rows, width), F32),
            pltpu.SemaphoreType.DMA((2,)),
        ],
        compiler_params=pltpu.CompilerParams(vmem_limit_bytes=60 * 2**20),
        cost_estimate=pl.CostEstimate(
            flops=2 * len(blocks) * pairs * rows * samples * width,
            bytes_accessed=2 * len(blocks) * slots * samples * width,
            transcendentals=0,
        ),
    )(slot_index, slot_width, sources, first, grads, *blocks)


def line_rounds(n):
    order = []
    for i in range(n):
        order.append([(up, k) for k in range(1, n) for up in (True, False) if (i - k >= 0 if up else i + k < n)])
    return order


def shards(embeddings, field_width, pair_fields, pair_mats, labels):
    owners = lax.axis_size("pair")
    groups = lax.axis_size("dp")
    owner = lax.axis_index("pair")
    group = lax.axis_index("dp")
    fields, samples, width = embeddings.shape
    pairs = pair_mats.shape[0]
    every = owners * fields

    pair_list = pair_fields.T
    field_ids = jnp.arange(fields, dtype=jnp.int32)
    slot_ids = jnp.arange(CAP, dtype=jnp.int32)
    local = pair_list.reshape(2, owners, 1, pairs) - owner * fields
    needed = jnp.any(local == field_ids[None, None, :, None], axis=(0, 3)).astype(jnp.int32)
    rank = jnp.sum(jnp.where(field_ids[:, None] > field_ids[None, :], needed[:, None, :], 0), axis=2)
    chosen = (needed[:, None, :] > 0) & (rank[:, None, :] == slot_ids[None, :, None])
    table = jnp.sum(jnp.where(chosen, field_ids[None, None, :], 0), axis=2).reshape(-1)

    mine = lax.dynamic_slice_in_dim(pair_list, owner * pairs, pairs, 1)
    all_ids = jnp.arange(every, dtype=jnp.int32)
    hit = mine.T.reshape(-1)[:, None] == all_ids[None, :]
    wanted = jnp.any(hit, axis=0).astype(jnp.int32).reshape(owners, fields)
    place = jnp.sum(jnp.where(field_ids[:, None] > field_ids[None, :], wanted[:, None, :], 0), axis=2)
    slot_of = jnp.arange(owners, dtype=jnp.int32)[:, None] * CAP + place
    slot_index = jnp.sum(jnp.where(hit, slot_of.reshape(-1)[None, :], 0), axis=1)
    taken = (wanted[:, None, :] > 0) & (place[:, None, :] == slot_ids[None, :, None])
    slot_width = jnp.sum(jnp.where(taken, field_width.reshape(owners, 1, fields), 0), axis=2).reshape(-1)
    own_width = lax.dynamic_slice_in_dim(field_width, owner * fields, fields, 0)

    up, down = [embeddings], [embeddings]
    for k in range(1, groups):
        up.append(lax.ppermute(up[-1], "dp", [(i, i + 1) for i in range(k - 1, groups - 1)]))
        down.append(lax.ppermute(down[-1], "dp", [(i, i - 1) for i in range(1, groups - k + 1)]))

    def exchange(rows):
        return lax.all_to_all(
            rows.reshape(owners, CAP, samples, width), "pair", split_axis=0, concat_axis=0, tiled=True
        ).reshape(owners * CAP, samples, width)

    zero = jnp.zeros((1,), jnp.int32)
    received = exchange(pick_rows(zero, table, [embeddings]))

    part, sums = forward(slot_index, slot_width, received, pair_mats)
    back = exchange(sums)
    note = jnp.concatenate([part, labels.astype(F32)[None, :]], axis=0)
    notes = lax.all_gather(note, ("dp", "pair"), axis=0).reshape(groups, owners, 2, samples)
    every_logit = jnp.sum(notes[:, :, 0], axis=1)
    grads = (jax.nn.sigmoid(every_logit) - notes[:, 0, 1])[:, None, :]
    logits = lax.dynamic_index_in_dim(every_logit, group, 0, keepdims=False)
    own_grad = lax.dynamic_index_in_dim(grads, group, 0, keepdims=False)

    emb_grad = emb_grad_of(table, own_width, back, own_grad, fields)

    order = line_rounds(groups)
    blocks, sources = [received], [group]
    for r in range(groups - 1):
        ways = sorted({order[i][r] for i in range(groups)})
        which = jnp.array([[ways.index(order[i][r])] for i in range(groups)], jnp.int32)
        origin = jnp.array([i - k if u else i + k for i, (u, k) in ((i, order[i][r]) for i in range(groups))], jnp.int32)
        candidates = [(up if u else down)[k] for u, k in ways]
        which = lax.dynamic_index_in_dim(which, group, 0, keepdims=False)
        sources.append(lax.dynamic_index_in_dim(origin, group, 0, keepdims=False))
        blocks.append(exchange(pick_rows(which, table, candidates)))
    rows = width // groups
    mat_grad = mat_grad_of(
        slot_index, slot_width, jnp.stack(sources).astype(jnp.int32), (group * rows).reshape(1), grads, blocks, rows
    )
    return (logits, mat_grad, emb_grad)


def solution(mesh):
    in_specs = (P("pair", "dp", None), P(), P(), P("pair", None, None), P("dp"))
    out_specs = (P("dp"), P("pair", "dp", None), P("pair", "dp", None))
    return jax.shard_map(shards, mesh=mesh, in_specs=in_specs, out_specs=out_specs, check_vma=False)
```

time: 191 us -> 427 us (2.24)
  Pallas kernels: 0 us -> 243 us
  starting transfers between devices: 5.21 us -> 30.1 us
  matrix products: 23.9 us -> 0 us
  other arithmetic: 28 us -> 5.53 us
  waiting for transfers between devices: 68.6 us -> 84 us
  between operations: 14.2 us -> 0.88 us
  blocking collectives: 35.4 us -> 45.3 us
    pallas_call x0 -> x7, Pallas kernels: none -> 243 us  [the longest x4 200 us: pick_rows(): pl.pallas_call(pick_rows_kernel, out_shape=jax.ShapeDtypeStruct(shape, BF...]
    ppermute x0 -> x6, waiting for transfers between devices: none -> 76.7 us  [the longest x3 56.8 us: shards(): lax.ppermute(down[-1], 'dp', [(i, i - 1) for i in range(1, groups - k + 1)])]
    reduce_scatter x1 -> x0, waiting for transfers between devices: 49.9 us -> none  [shards(): lax.psum_scatter(mat_term.astype(jnp.bfloat16), 'dp', scatter_dimension=1...]
    all_gather x0 -> x1, blocking collectives: none -> 45.3 us  [shards(): lax.all_gather(note, ('dp', 'pair'), axis=0)]
    dot_general x5 -> x0, matrix products: 23.9 us -> none  [the longest x1 8.23 us: shards(): jnp.einsum('psl,pkl->psk', right_rows, pair_mats, preferred_element_type=...]
    all_to_all x1 -> x0, blocking collectives: 23.7 us -> none  [shards(): lax.all_to_all(slot_grads, 'pair', split_axis=0, concat_axis=0, tiled=True)]
    scatter-add x2 -> x0, other arithmetic: 19 us -> none  [shards(): slot_grads.at[slot_index[:, 0]].add(toward_left).at[slot_index[:, 1]]]
    all_to_all x1 -> x5, starting transfers between devices: 5.17 us -> 20.3 us  [exchange(): lax.all_to_all(rows.reshape(owners, CAP, samples, width), 'pair', split_a...]
  transfers between devices with their start and end apart: 2 -> 11, of which waited for: 2 -> 5; matrix products, arithmetic and copies ran while one was open for 21% -> 3% of each run, Pallas kernels for 0% -> 39%
where the time goes in v1:
time: 427 us; the launch traced here: 426 us
  Pallas kernels  243 us (57%)
  waiting for transfers between devices  84 us (20%)
  blocking collectives  45.3 us (11%)
  starting transfers between devices  30.1 us (7%)
  local copies, waits for them, and re-layouts  17.3 us (4%)
  other arithmetic  5.53 us (1%)
    pallas_call x4, Pallas kernels, pick_rows(): pl.pallas_call(pick_rows_kernel, out_shape=jax.ShapeDtypeStruct(shape, BF...  200 us
    ppermute x3, waiting for transfers between devices, shards(): lax.ppermute(down[-1], 'dp', [(i, i - 1) for i in range(1, groups - k + 1)])  56.8 us
    all_gather x1, blocking collectives, shards(): lax.all_gather(note, ('dp', 'pair'), axis=0)  45.3 us
    pallas_call x1, Pallas kernels, mat_grad_of(): pl.pallas_call(functools.partial(mat_grad_kernel, len(blocks)), out_shape...  27.2 us
    all_to_all x5, starting transfers between devices, exchange(): lax.all_to_all(rows.reshape(owners, CAP, samples, width), 'pair', split_a...  20.3 us
    ppermute x3, waiting for transfers between devices, shards(): lax.ppermute(up[-1], 'dp', [(i, i + 1) for i in range(k - 1, groups - 1)])  19.9 us
    pallas_call x1, Pallas kernels, forward(): pl.pallas_call(functools.partial(forward_kernel, group), grid=(pairs // g...  12.1 us
  transfers between devices with their start and end apart: 11, of which 5 were waited for; matrix products, arithmetic and copies ran while one was open for 3% of the time, Pallas kernels for 39%

profile of v1, /device:TPU:0, one launch (start us, length us, event | category | flops | bytes accessed | tf_op | source)
XLA Modules:
  0.0 426.3 jit_solution(4372173369911876900)
XLA Ops:
  4.8 49.6 %shard_map.130 = bf16[24,128,256]{2,1,0:T(8,128)(2,1)} custom-call(s32[1]{0:T(128)} %constant.60.clone.1.which_ref, s32[24]{0:T(128)} %reshape.136.table_ref, bf16[16,128,256]{2,1,0:T(8,128)(2,1)} %refs_0_.1), custom_call_target="tpu_custom_call" | custom-call | bytes 3145728 | tf_op jit(solution)/shard_map/pallas_call | solution.py:37
  54.5 5.2 %all-to-all-start = ((bf16[8,3,128,256]{3,2,1,0:T(8,128)(2,1)}), bf16[8,3,128,256]{3,2,1,0:T(8,128)(2,1)S(1)}, u32[]{:S(2)}, u32[]{:S(2)}) async-start(bf16[8,3,128,256]{3,2,1,0:T(8,128)(2,1)} %bitcast.40), calls=%async_computation | async-start | bytes 3145728 | tf_op jit(solution)/shard_map/all_to_all | solution.py:248
  59.6 4.5 %collective-permute-start.1 = (bf16[16,128,256]{2,1,0:T(8,128)(2,1)}, bf16[16,128,256]{2,1,0:T(8,128)(2,1)}, u32[]{:S(2)}, u32[]{:S(2)}) collective-permute-start(bf16[16,128,256]{2,1,0:T(8,128)(2,1)} %refs_0_.1), channel_id=1, source_target_pairs={{0,8},{8,16},{16,24},{1,9},{9,17},{17,25},{2,10},{10,18},{18,26},{... | collective-permute-start | bytes 3145736 | tf_op jit(solution)/shard_map/ppermute | solution.py:244
  64.1 1.3 collective-permute-start
  65.4 1.2 constant_dynamic-slice_fusion.3
  66.6 19.9 %collective-permute-done.1.refs_1_ = bf16[16,128,256]{2,1,0:T(8,128)(2,1)} collective-permute-done((bf16[16,128,256]{2,1,0:T(8,128)(2,1)}, bf16[16,128,256]{2,1,0:T(8,128)(2,1)}, u32[]{:S(2)}, u32[]{:S(2)}) %collective-permute-start.1) | collective-permute-done | bytes 1048608 | tf_op jit(solution)/shard_map/ppermute | solution.py:244
  86.5 5.0 %collective-permute-done.refs_0_ = bf16[16,128,256]{2,1,0:T(8,128)(2,1)S(1)} collective-permute-done((bf16[16,128,256]{2,1,0:T(8,128)(2,1)}, bf16[16,128,256]{2,1,0:T(8,128)(2,1)S(1)}, u32[]{:S(2)}, u32[]{:S(2)}) %collective-permute-start) | collective-permute-done | bytes 1048608 | tf_op jit(solution)/shard_map/ppermute | solution.py:245
  91.5 1.0 copy-done.5
  92.5 50.3 %shard_map.132 = bf16[24,128,256]{2,1,0:T(8,128)(2,1)} custom-call(s32[1]{0:T(128)} %bitcast.12.which_ref, s32[24]{0:T(128)} %reshape.136.table_ref, bf16[16,128,256]{2,1,0:T(8,128)(2,1)} %copy-done.5, bf16[16,128,256]{2,1,0:T(8,128)(2,1)} %collective-permute-done.1.refs_1_), custom_call_target="tpu_custom_call" | custom-call | bytes 3145728 | tf_op jit(solution)/shard_map/pallas_call | solution.py:37
  142.8 1.1 copy-done
  143.9 3.8 all-to-all-start.1
  149.4 12.1 %shard_map.131 = (f32[1,128]{1,0:T(1,128)}, bf16[24,128,256]{2,1,0:T(8,128)(2,1)}) custom-call(s32[96]{0:T(128)} %select_reduce_fusion.2.slot_ref, s32[24]{0:T(128)} %reshape.135.width_ref, bf16[24,128,256]{2,1,0:T(8,128)(2,1)} %bitcast.34, bf16[48,256,256]{2,1,0:T(8,128)(2,1)} %mats_ref.1), custom_call_target="tpu_custom_call" | custom-call | flops 1610612736 | bytes 6291456 | tf_op jit(solution)/shard_map/pallas_call | solution.py:88
  161.5 7.3 %all-to-all-done.1 = bf16[8,3,128,256]{3,2,1,0:T(8,128)(2,1)S(1)} async-done(((bf16[8,3,128,256]{3,2,1,0:T(8,128)(2,1)}), bf16[8,3,128,256]{3,2,1,0:T(8,128)(2,1)S(1)}, u32[]{:S(2)}, u32[]{:S(2)}) %all-to-all-start.1) | async-done | bytes 1572896 | tf_op jit(solution)/shard_map/all_to_all | solution.py:248
  168.8 1.2 copy-done.1
  170.0 3.6 all-to-all-start.4
  174.3 1.3 collective-permute-start.2
  175.6 1.3 constant_dynamic-slice_fusion.2
  176.9 26.5 %collective-permute-done.2.refs_1_.refs_0_ = bf16[16,128,256]{2,1,0:T(8,128)(2,1)} collective-permute-done((bf16[16,128,256]{2,1,0:T(8,128)(2,1)}, bf16[16,128,256]{2,1,0:T(8,128)(2,1)}, u32[]{:S(2)}, u32[]{:S(2)}) %collective-permute-start.2) | collective-permute-done | bytes 1048608 | tf_op jit(solution)/shard_map/ppermute | solution.py:245
  203.4 50.3 %shard_map.133 = bf16[24,128,256]{2,1,0:T(8,128)(2,1)} custom-call(s32[1]{0:T(128)} %bitcast.15.which_ref, s32[24]{0:T(128)} %reshape.136.table_ref, bf16[16,128,256]{2,1,0:T(8,128)(2,1)} %copy-done.5, bf16[16,128,256]{2,1,0:T(8,128)(2,1)} %collective-permute-done.2.refs_1_.refs_0_, bf16[16,128,256]{2,1,0:T(8,128)(2,1)} %copy-done.6), custom_call_target="tpu_custom_call" | custom-call | bytes 3145728 | tf_op jit(solution)/shard_map/pallas_call | solution.py:37
  253.7 1.1 copy-done.2
  254.9 3.9 all-to-all-start.2
  259.5 1.3 collective-permute-start.4
  260.8 1.2 constant_dynamic-slice_fusion.1
  262.0 25.3 %collective-permute-done.4.refs_1_ = bf16[16,128,256]{2,1,0:T(8,128)(2,1)} collective-permute-done((bf16[16,128,256]{2,1,0:T(8,128)(2,1)}, bf16[16,128,256]{2,1,0:T(8,128)(2,1)}, u32[]{:S(2)}, u32[]{:S(2)}) %collective-permute-start.4) | collective-permute-done | bytes 1048608 | tf_op jit(solution)/shard_map/ppermute | solution.py:245
  287.2 50.3 %shard_map.134 = bf16[24,128,256]{2,1,0:T(8,128)(2,1)} custom-call(s32[1]{0:T(128)} %bitcast.18.which_ref, s32[24]{0:T(128)} %reshape.136.table_ref, bf16[16,128,256]{2,1,0:T(8,128)(2,1)} %collective-permute-done.2.refs_1_.refs_0_, bf16[16,128,256]{2,1,0:T(8,128)(2,1)} %collective-permute-done.4.refs_1_, bf16[16,128,256]{2,1,0:T(8,128)(2,1)} %copy-done.6, ...), custom_call_target="tpu_custom_call" | custom-call | bytes 3145728 | tf_op jit(solution)/shard_map/pallas_call | solution.py:37
  337.6 1.1 copy-done.3
  338.7 3.8 all-to-all-start.3
  345.0 2.5 pad_add_fusion.source_ref
  347.5 45.3 %all-gather.1 = f32[32,2,128]{2,1,0:T(2,128)S(1)} all-gather(f32[1,2,128]{2,1,0:T(2,128)S(1)} %maximum_bitcast_fusion), channel_id=2, replica_groups=mesh['dp'=4,'pair'=8] {'dp','pair'}, dimensions={0}, use_global_device_ids=true | all-gather | bytes 33792 | tf_op jit(solution)/shard_map/all_gather | solution.py:258
  394.4 3.6 shard_map.136
  398.0 1.2 copy-done.4
  399.1 27.2 %shard_map.135 = bf16[48,64,256]{2,1,0:T(8,128)(2,1)} custom-call(s32[96]{0:T(128)} %select_reduce_fusion.2.slot_ref, s32[24]{0:T(128)} %reshape.135.width_ref, s32[4]{0:T(128)} %pad_add_fusion.source_ref, s32[1]{0:T(128)} %bitcast.8.first_ref, f32[4,1,128]{2,1,0:T(1,128)} %bitcast.49, bf16[24,128,256]{2,1,0:T(8,128)(2,1)} %bitcast.35, ...), custom_call_target="tpu_custom_call" | custom-call | flops 805306368 | bytes 6291456 | tf_op jit(solution)/shard_map/pallas_call | solution.py:186
  (66 shorter events, 11.4 us)
Async XLA Ops:
  54.5 88.3 %all-to-all-start = ((bf16[8,3,128,256]{3,2,1,0:T(8,128)(2,1)}), bf16[8,3,128,256]{3,2,1,0:T(8,128)(2,1)S(1)}, u32[]{:S(2)}, u32[]{:S(2)}) async-start(bf16[8,3,128,256]{3,2,1,0:T(8,128)(2,1)} %bitcast.40), calls=%async_computation | async-start | bytes 3145728 | tf_op jit(solution)/shard_map/all_to_all | solution.py:248
  59.6 26.9 %collective-permute-start.1 = (bf16[16,128,256]{2,1,0:T(8,128)(2,1)}, bf16[16,128,256]{2,1,0:T(8,128)(2,1)}, u32[]{:S(2)}, u32[]{:S(2)}) collective-permute-start(bf16[16,128,256]{2,1,0:T(8,128)(2,1)} %refs_0_.1), channel_id=1, source_target_pairs={{0,8},{8,16},{16,24},{1,9},{9,17},{17,25},{2,10},{10,18},{18,26},{... | collective-permute-start | bytes 3145736 | tf_op jit(solution)/shard_map/ppermute | solution.py:244
  64.1 27.4 %collective-permute-start = (bf16[16,128,256]{2,1,0:T(8,128)(2,1)}, bf16[16,128,256]{2,1,0:T(8,128)(2,1)S(1)}, u32[]{:S(2)}, u32[]{:S(2)}) collective-permute-start(bf16[16,128,256]{2,1,0:T(8,128)(2,1)} %refs_0_.1), channel_id=1, source_target_pairs={{8,0},{16,8},{24,16},{9,1},{17,9},{25,17},{10,2},{18,10},{26,18},{... | collective-permute-start | bytes 3145736 | tf_op jit(solution)/shard_map/ppermute | solution.py:245
  91.5 1.0 copy-start.5
  142.8 1.2 copy-start
  143.9 24.9 %all-to-all-start.1 = ((bf16[8,3,128,256]{3,2,1,0:T(8,128)(2,1)}), bf16[8,3,128,256]{3,2,1,0:T(8,128)(2,1)S(1)}, u32[]{:S(2)}, u32[]{:S(2)}) async-start(bf16[8,3,128,256]{3,2,1,0:T(8,128)(2,1)} %bitcast.42), calls=%async_computation.1 | async-start | bytes 3145728 | tf_op jit(solution)/shard_map/all_to_all | solution.py:248
  168.8 1.2 copy-start.1
  170.0 83.7 %all-to-all-start.4 = ((bf16[8,3,128,256]{3,2,1,0:T(8,128)(2,1)}), bf16[8,3,128,256]{3,2,1,0:T(8,128)(2,1)S(1)}, u32[]{:S(2)}, u32[]{:S(2)}) async-start(bf16[8,3,128,256]{3,2,1,0:T(8,128)(2,1)} %bitcast.44), calls=%async_computation.4 | async-start | bytes 3145728 | tf_op jit(solution)/shard_map/all_to_all | solution.py:248
  173.6 3.3 collective-permute-start.3
  174.3 29.1 %collective-permute-start.2 = (bf16[16,128,256]{2,1,0:T(8,128)(2,1)}, bf16[16,128,256]{2,1,0:T(8,128)(2,1)}, u32[]{:S(2)}, u32[]{:S(2)}) collective-permute-start(bf16[16,128,256]{2,1,0:T(8,128)(2,1)} %copy-done.5), channel_id=1, source_target_pairs={{8,0},{16,8},{9,1},{17,9},{10,2},{18,10},{11,3},{19,11},{12,4},{20... | collective-permute-start | bytes 3145736 | tf_op jit(solution)/shard_map/ppermute | solution.py:245
  176.9 26.5 %copy-start.6 = (bf16[16,128,256]{2,1,0:T(8,128)(2,1)}, bf16[16,128,256]{2,1,0:T(8,128)(2,1)S(1)}, u32[]{:S(2)}) copy-start(bf16[16,128,256]{2,1,0:T(8,128)(2,1)S(1)} %collective-permute-done.3.refs_2_) | copy-start | bytes 3145732
  253.7 1.2 copy-start.2
  254.9 82.7 %all-to-all-start.2 = ((bf16[8,3,128,256]{3,2,1,0:T(8,128)(2,1)}), bf16[8,3,128,256]{3,2,1,0:T(8,128)(2,1)S(1)}, u32[]{:S(2)}, u32[]{:S(2)}) async-start(bf16[8,3,128,256]{3,2,1,0:T(8,128)(2,1)} %bitcast.41), calls=%async_computation.2 | async-start | bytes 3145728 | tf_op jit(solution)/shard_map/all_to_all | solution.py:248
  258.7 3.2 collective-permute-start.5
  259.5 27.8 %collective-permute-start.4 = (bf16[16,128,256]{2,1,0:T(8,128)(2,1)}, bf16[16,128,256]{2,1,0:T(8,128)(2,1)}, u32[]{:S(2)}, u32[]{:S(2)}) collective-permute-start(bf16[16,128,256]{2,1,0:T(8,128)(2,1)} %collective-permute-done.2.refs_1_.refs_0_), channel_id=1, source_target_pairs={{8,0},{9,1},{10,2},{11,3},{12,4},{13,5},{14,6},{15,7}} | collective-permute-start | bytes 3145736 | tf_op jit(solution)/shard_map/ppermute | solution.py:245
  262.0 25.3 %copy-start.7 = (bf16[16,128,256]{2,1,0:T(8,128)(2,1)}, bf16[16,128,256]{2,1,0:T(8,128)(2,1)S(1)}, u32[]{:S(2)}) copy-start(bf16[16,128,256]{2,1,0:T(8,128)(2,1)S(1)} %collective-permute-done.5.refs_3_) | copy-start | bytes 3145732
  337.5 1.2 copy-start.3
  337.5 5.0 %copy-start.8 = (s32[128]{0:T(128)S(1)}, s32[128]{0:T(128)}, u32[]{:S(2)}) copy-start(s32[128]{0:T(128)} %param.12) | copy-start | bytes 1540
  337.5 5.7 %copy-start.13 = (s32[4]{0:T(128)S(1)}, s32[4]{0:T(128)}, u32[]{:S(2)}) copy-start(s32[4]{0:T(128)} %constant.73.clone) | copy-start | bytes 52
  337.6 6.2 %copy-start.12 = (s32[4]{0:T(128)S(1)}, s32[4]{0:T(128)}, u32[]{:S(2)}) copy-start(s32[4]{0:T(128)} %constant.71.clone) | copy-start | bytes 52
  337.6 6.8 %copy-start.11 = (s32[4]{0:T(128)S(1)}, s32[4]{0:T(128)}, u32[]{:S(2)}) copy-start(s32[4]{0:T(128)} %constant.69.clone) | copy-start | bytes 52
  337.6 9.9 %copy-start.10 = (s32[128]{0:T(128)S(1)}, s32[128]{0:T(128)}, u32[]{:S(2)}) copy-start(s32[128]{0:T(128)} %param.15) | copy-start | bytes 1540
  337.6 9.9 %copy-start.9 = (f32[1,128]{1,0:T(1,128)S(1)}, f32[1,128]{1,0:T(1,128)}, u32[]{:S(2)}) copy-start(f32[1,128]{1,0:T(1,128)} %get-tuple-element.5) | copy-start | bytes 1540
  338.7 59.3 %all-to-all-start.3 = ((bf16[8,3,128,256]{3,2,1,0:T(8,128)(2,1)}), bf16[8,3,128,256]{3,2,1,0:T(8,128)(2,1)S(1)}, u32[]{:S(2)}, u32[]{:S(2)}) async-start(bf16[8,3,128,256]{3,2,1,0:T(8,128)(2,1)} %bitcast.43), calls=%async_computation.3 | async-start | bytes 3145728 | tf_op jit(solution)/shard_map/all_to_all | solution.py:248
  398.0 1.2 copy-start.4

commit v2 on v1

v2 whole, which is shorter than its diff:
```python
import functools
import math

import jax
import jax.numpy as jnp
from jax import lax
from jax.experimental import pallas as pl
from jax.experimental.pallas import tpu as pltpu
from jax.sharding import PartitionSpec as P

CAP = 3
NOTE = 16
RAW = 64
VMEM = pl.BlockSpec(memory_space=pltpu.VMEM)
SMEM = pl.BlockSpec(memory_space=pltpu.SMEM)
HBM = pl.BlockSpec(memory_space=pl.ANY)
F32 = jnp.float32
BF16 = jnp.bfloat16
CHEAP = pl.CostEstimate(flops=0, bytes_accessed=1 << 20, transcendentals=0)


def limit(size):
    return pltpu.CompilerParams(vmem_limit_bytes=size + (4 << 20))


def pick_rows_kernel(ways, which_ref, table_ref, *refs):
    *sources, out_ref, sems = refs
    slots = out_ref.shape[0]
    lines = sources[0].shape[1]
    for r, choices in enumerate(ways):
        for at, source in enumerate(choices):

            @pl.when(which_ref[r] == at)
            def _(r=r, source=source):
                @pl.loop(0, slots)
                def _(j):
                    place = out_ref.at[j, pl.ds(r * lines, lines), :]
                    pltpu.make_async_copy(sources[source].at[table_ref[j]], place, sems.at[r, j]).start()

    for r in range(len(ways)):

        @pl.loop(0, slots)
        def _(j, r=r):
            place = out_ref.at[j, pl.ds(r * lines, lines), :]
            pltpu.make_async_copy(sources[0].at[0], place, sems.at[r, j]).wait()


def pick_rows(ways, which, table, sources):
    _, lines, width = sources[0].shape
    shape = (table.shape[0], len(ways) * lines, width)
    return pl.pallas_call(
        functools.partial(pick_rows_kernel, ways),
        out_shape=jax.ShapeDtypeStruct(shape, BF16),
        in_specs=[SMEM, SMEM] + [HBM] * len(sources),
        out_specs=VMEM,
        scratch_shapes=[pltpu.SemaphoreType.DMA((len(ways), shape[0]))],
        compiler_params=limit(math.prod(shape) * 2),
        cost_estimate=CHEAP,
    )(which, table, *sources)


def forward_kernel(group, slot_ref, width_ref, rows_ref, mats_ref, sums_ref, x_ref, u_ref, acc_ref):
    step = pl.program_id(0)
    slots, samples, width = x_ref.shape

    @pl.when(step == 0)
    def _():
        columns = lax.broadcasted_iota(jnp.int32, (samples, width), 1)

        @pl.loop(0, slots)
        def _(j):
            x_ref[j] = jnp.where(columns < width_ref[j], rows_ref[j], jnp.zeros_like(rows_ref[j]))
            u_ref[j] = jnp.zeros((samples, width), F32)

        acc_ref[...] = jnp.zeros_like(acc_ref)

    acc = jnp.zeros((samples, width), F32)
    for k in range(group):
        p = step * group + k
        a, b = slot_ref[2 * p], slot_ref[2 * p + 1]
        left, right, mat = x_ref[a], x_ref[b], mats_ref[k]
        projected = jnp.dot(left, mat, preferred_element_type=F32)
        back = lax.dot_general(right, mat, (((1,), (1,)), ((), ())), preferred_element_type=F32)
        acc += projected * right.astype(F32)
        u_ref[b] += projected
        u_ref[a] += back
    acc_ref[...] += acc

    @pl.when(step == pl.num_programs(0) - 1)
    def _():
        total = acc_ref[:, 0:128]
        for at in range(128, width, 128):
            total = total + acc_ref[:, at : at + 128]
        part = jnp.sum(total.T, axis=0, keepdims=True)
        note = jnp.zeros((NOTE, width), F32)
        for row in range(3):
            piece = part.astype(BF16).astype(F32)
            part = part - piece
            at = lax.broadcasted_iota(jnp.int32, (NOTE, width), 0) == row
            note = jnp.where(at, jnp.concatenate([piece] * (width // samples), axis=1), note)
        lines = CAP * samples

        @pl.loop(0, slots // CAP)
        def _(o):
            for c in range(CAP):
                sums_ref[o, c * samples : (c + 1) * samples, :] = u_ref[o * CAP + c].astype(BF16)
            sums_ref[o, lines : lines + NOTE, :] = note.astype(BF16)


def forward(slot_index, slot_width, rows, mats, group=8):
    slots, samples, width = rows.shape
    pairs = mats.shape[0]
    whole = lambda *shape: pl.BlockSpec(shape, lambda i: (0,) * len(shape))
    sums = (slots // CAP, CAP * samples + NOTE, width)
    return pl.pallas_call(
        functools.partial(forward_kernel, group),
        grid=(pairs // group,),
        out_shape=jax.ShapeDtypeStruct(sums, BF16),
        in_specs=[SMEM, SMEM, whole(*rows.shape), pl.BlockSpec((group, width, width), lambda i: (i, 0, 0))],
        out_specs=whole(*sums),
        scratch_shapes=[
            pltpu.VMEM(rows.shape, BF16),
            pltpu.VMEM(rows.shape, F32),
            pltpu.VMEM((samples, width), F32),
        ],
        compiler_params=limit(14 * math.prod(rows.shape) + 4 * group * width * width),
        cost_estimate=CHEAP,
    )(slot_index, slot_width, rows, mats)


def emb_grad_kernel(table_ref, width_ref, back_ref, labels_ref, out_ref, logit_ref, grad_ref):
    fields, samples, width = out_ref.shape
    owners = back_ref.shape[0]
    lines = CAP * samples

    @pl.loop(0, fields)
    def _(f):
        out_ref[f] = jnp.zeros((samples, width), F32)

    @pl.loop(0, owners)
    def _(o):
        for c in range(CAP):
            f = table_ref[o * CAP + c]
            out_ref[f] += back_ref[o, c * samples : (c + 1) * samples, :].astype(F32)

    note = back_ref[0, lines : lines + NOTE, 0:samples].astype(F32)
    for o in range(1, owners):
        note += back_ref[o, lines : lines + NOTE, 0:samples].astype(F32)
    logit = note[0:1] + note[1:2] + note[2:3]
    grad = jax.nn.sigmoid(logit) - labels_ref[...].astype(F32)
    logit_ref[...] = logit
    grad_ref[...] = grad
    factor = jnp.broadcast_to(grad, (128, samples)).T
    factor = jnp.concatenate([factor] * (width // 128), axis=1)
    columns = lax.broadcasted_iota(jnp.int32, (samples, width), 1)

    @pl.loop(0, fields)
    def _(f):
        out_ref[f] = jnp.where(columns < width_ref[f], out_ref[f] * factor, 0.0)


def emb_grad_of(table, own_width, back, labels, fields):
    samples, width = labels.shape[1], back.shape[2]
    return pl.pallas_call(
        emb_grad_kernel,
        out_shape=(
            jax.ShapeDtypeStruct((fields, samples, width), F32),
            jax.ShapeDtypeStruct((1, samples), F32),
            jax.ShapeDtypeStruct((1, samples), F32),
        ),
        in_specs=[SMEM, SMEM, VMEM, VMEM],
        out_specs=(VMEM, VMEM, VMEM),
        compiler_params=limit(math.prod(back.shape) * 2 + fields * samples * width * 4),
        cost_estimate=CHEAP,
    )(table, own_width, back, labels)


def mat_grad_kernel(ways, chunk, slot_ref, width_ref, which_ref, source_ref, first_ref, grads_ref, own_ref, raw_ref, *refs):
    *links, out_ref, x_ref, t_ref, acc_ref, sems = refs
    count = len(ways) + 1
    width = x_ref.shape[2]
    slots, samples, _ = own_ref.shape
    kept_lines = links[0].shape[1]
    raw_lines = samples - kept_lines
    pairs, rows, _ = acc_ref.shape
    own_row = lax.broadcasted_iota(jnp.int32, (rows, width), 0) + first_ref[0]
    columns = lax.broadcasted_iota(jnp.int32, (rows, width), 1)
    pick = (columns == own_row).astype(BF16)

    def place(k, low, size):
        return x_ref.at[:, pl.ds(k * samples + low, size), :]

    for start in range(0, count, chunk):
        waits = []
        for k in range(chunk):
            if start + k == 0:
                waits.append(pltpu.make_async_copy(own_ref, place(k, 0, samples), sems.at[k, 0]))
                waits[-1].start()
                continue
            r = start + k - 1
            raw = raw_ref.at[:, pl.ds(r * raw_lines, raw_lines), :]
            waits.append(pltpu.make_async_copy(raw, place(k, 0, raw_lines), sems.at[k, 0]))
            waits[-1].start()
            for at, link in enumerate(ways[r]):

                @pl.when(which_ref[r] == at)
                def _(k=k, link=link):
                    pltpu.make_async_copy(links[link], place(k, raw_lines, kept_lines), sems.at[k, 1]).start()

            waits.append(pltpu.make_async_copy(links[0], place(k, raw_lines, kept_lines), sems.at[k, 1]))
        for copy in waits:
            copy.wait()
        grad = jnp.concatenate([grads_ref[source_ref[start + k]] for k in range(chunk)], axis=1)

        @pl.loop(0, slots, unroll=4)
        def _(j, grad=grad):
            turned = lax.dot_general(pick, x_ref[j], (((1,), (1,)), ((), ())), preferred_element_type=F32)
            t_ref[j] = (turned * grad).astype(BF16)

        @pl.loop(0, pairs, unroll=4)
        def _(p, start=start):
            a, b = slot_ref[2 * p], slot_ref[2 * p + 1]
            term = jnp.dot(t_ref[a], x_ref[b], preferred_element_type=F32)
            if start > 0:
                term += acc_ref[p]
            if start + chunk < count:
                acc_ref[p] = term
            else:
                kept = (own_row < width_ref[a]) & (columns < width_ref[b])
                out_ref[p] = jnp.where(kept, term, 0.0).astype(BF16)


def mat_grad_of(ways, slot_index, slot_width, which, sources, first, grads, own, raw, links, rows):
    slots, samples, width = own.shape
    pairs = slot_index.shape[0] // 2
    chunk = len(ways) + 1
    while chunk * slots * samples * width > (8 << 20) and chunk % 2 == 0:
        chunk //= 2
    size = chunk * slots * samples * (width + rows) * 2 + pairs * rows * width * 6
    return pl.pallas_call(
        functools.partial(mat_grad_kernel, ways, chunk),
        out_shape=jax.ShapeDtypeStruct((pairs, rows, width), BF16),
        in_specs=[SMEM, SMEM, SMEM, SMEM, SMEM, VMEM] + [HBM] * (2 + len(links)),
        out_specs=VMEM,
        scratch_shapes=[
            pltpu.VMEM((slots, chunk * samples, width), BF16),
            pltpu.VMEM((slots, rows, chunk * samples), BF16),
            pltpu.VMEM((pairs, rows, width), F32),
            pltpu.SemaphoreType.DMA((chunk, 2)),
        ],
        compiler_params=limit(size),
        cost_estimate=CHEAP,
    )(slot_index, slot_width, which, sources, first, grads, own, raw, *links)


def line_rounds(n):
    order = []
    for i in range(n):
        order.append([(up, k) for k in range(1, n) for up in (True, False) if (i - k >= 0 if up else i + k < n)])
    return order


def shards(embeddings, field_width, pair_fields, pair_mats, labels):
    owners = lax.axis_size("pair")
    groups = lax.axis_size("dp")
    owner = lax.axis_index("pair")
    group = lax.axis_index("dp")
    fields, samples, width = embeddings.shape
    pairs = pair_mats.shape[0]
    every = owners * fields

    pair_list = pair_fields.T
    field_ids = jnp.arange(fields, dtype=jnp.int32)
    slot_ids = jnp.arange(CAP, dtype=jnp.int32)
    local = pair_list.reshape(2, owners, 1, pairs) - owner * fields
    needed = jnp.any(local == field_ids[None, None, :, None], axis=(0, 3)).astype(jnp.int32)
    rank = jnp.sum(jnp.where(field_ids[:, None] > field_ids[None, :], needed[:, None, :], 0), axis=2)
    chosen = (needed[:, None, :] > 0) & (rank[:, None, :] == slot_ids[None, :, None])
    table = jnp.sum(jnp.where(chosen, field_ids[None, None, :], 0), axis=2).reshape(-1)

    mine = lax.dynamic_slice_in_dim(pair_list, owner * pairs, pairs, 1)
    all_ids = jnp.arange(every, dtype=jnp.int32)
    hit = mine.T.reshape(-1)[:, None] == all_ids[None, :]
    wanted = jnp.any(hit, axis=0).astype(jnp.int32).reshape(owners, fields)
    place = jnp.sum(jnp.where(field_ids[:, None] > field_ids[None, :], wanted[:, None, :], 0), axis=2)
    slot_of = jnp.arange(owners, dtype=jnp.int32)[:, None] * CAP + place
    slot_index = jnp.sum(jnp.where(hit, slot_of.reshape(-1)[None, :], 0), axis=1)
    taken = (wanted[:, None, :] > 0) & (place[:, None, :] == slot_ids[None, :, None])
    slot_width = jnp.sum(jnp.where(taken, field_width.reshape(owners, 1, fields), 0), axis=2).reshape(-1)
    own_width = lax.dynamic_slice_in_dim(field_width, owner * fields, fields, 0)

    def chain(first):
        up, down = [first], [first]
        for k in range(1, groups):
            up.append(lax.ppermute(up[-1], "dp", [(i, i + 1) for i in range(k - 1, groups - 1)]))
            down.append(lax.ppermute(down[-1], "dp", [(i, i - 1) for i in range(1, groups - k + 1)]))
            yield up[-1], down[-1]

    def exchange(rows):
        lines = rows.reshape(owners, -1, width)
        return lax.all_to_all(lines, "pair", split_axis=0, concat_axis=0, tiled=True)

    tie = lax.optimization_barrier
    order = line_rounds(groups)
    ways, which, origin = [], [], []
    for r in range(groups - 1):
        names = sorted({order[i][r] for i in range(groups)})
        ways.append([2 * (k - 1) + (not up) for up, k in names])
        which.append([names.index(order[i][r]) for i in range(groups)])
        origin.append([i - order[i][r][1] if order[i][r][0] else i + order[i][r][1] for i in range(groups)])
    places = jnp.array([list(w) + [i] + list(s) for i, (w, s) in enumerate(zip(zip(*which), zip(*origin)))], jnp.int32)
    places = lax.dynamic_index_in_dim(places, group, 0, keepdims=False)
    which, sources = places[: groups - 1], places[groups - 1 :]

    raw_steps = chain(embeddings[:, :RAW])
    raw = []
    for _ in range(max(1, groups - 2)):
        raw += next(raw_steps)
    picked = pick_rows([[0]], jnp.zeros((1,), jnp.int32), table, [embeddings])
    received = exchange(picked).reshape(owners * CAP, samples, width)
    received, raw = tie((received, raw))

    for step in raw_steps:
        raw += step
    kept_steps = chain(received[:, RAW:])
    sums = forward(slot_index, slot_width, received, pair_mats)
    sums, raw = tie((sums, raw))
    back = exchange(sums)
    far = pick_rows(ways, which, table, raw)
    kept = [*next(kept_steps)]
    far, kept = tie((far, kept))
    far = exchange(far).reshape(owners * CAP, -1, width)
    for step in kept_steps:
        kept += step
    emb_grad, logits, grad = emb_grad_of(table, own_width, back, labels[None, :], fields)
    logits = logits.reshape(samples)
    grads = lax.all_gather(grad, "dp", axis=0)
    rows = width // groups
    mat_grad = mat_grad_of(
        ways, slot_index, slot_width, which, sources, (group * rows).reshape(1), grads, received, far, kept, rows
    )
    return (logits, mat_grad, emb_grad)


def solution(mesh):
    in_specs = (P("pair", "dp", None), P(), P(), P("pair", None, None), P("dp"))
    out_specs = (P("dp"), P("pair", "dp", None), P("pair", "dp", None))
    return jax.shard_map(shards, mesh=mesh, in_specs=in_specs, out_specs=out_specs, check_vma=False)
```

time: 427 us -> 148 us (0.35)
  Pallas kernels: 243 us -> 28.1 us
  waiting for transfers between devices: 84 us -> 52.6 us
  blocking collectives: 45.3 us -> 18.4 us
    pallas_call x6 -> x4, Pallas kernels: 231 us -> 21.3 us  [the longest x1 10.5 us: mat_grad_of(): pl.pallas_call(functools.partial(mat_grad_kernel, ways, chunk), out_shape...]
    all_gather x1, blocking collectives: 45.3 us -> 18.4 us  [shards(): grads = lax.all_gather(grad, 'dp', axis=0)]
    ppermute x6 -> x12, waiting for transfers between devices: 76.7 us -> 52.6 us  [the longest x6 46.1 us: chain(): lax.ppermute(down[-1], 'dp', [(i, i - 1) for i in range(1, groups - k + 1)])]
    ppermute x6 -> x12, starting transfers between devices: 9.78 us -> 20.5 us  [the longest x6 12.8 us: chain(): lax.ppermute(up[-1], 'dp', [(i, i + 1) for i in range(k - 1, groups - 1)])]
    all_to_all x5 -> x3, starting transfers between devices: 20.3 us -> 11.8 us  [exchange(): lax.all_to_all(lines, 'pair', split_axis=0, concat_axis=0, tiled=True)]
    all_to_all x5 -> x3, waiting for transfers between devices: 7.31 us -> 0.01 us  [exchange(): lax.all_to_all(lines, 'pair', split_axis=0, concat_axis=0, tiled=True)]
    pallas_call x1, Pallas kernels: 12.1 us -> 6.82 us  [forward(): pl.pallas_call(functools.partial(forward_kernel, group), grid=(pairs // g...]
    dynamic_slice x6 -> x1, local copies, waits for them, and re-layouts: 5.44 us -> 0.69 us  [shards(): places = lax.dynamic_index_in_dim(places, group, 0, keepdims=False)]
  transfers between devices with their start and end apart: 11 -> 15, of which waited for: 5 -> 6; matrix products, arithmetic and copies ran while one was open for 3% -> 4% of each run, Pallas kernels for 39% -> 12%
where the time goes in v2:
time: 148 us
  waiting for transfers between devices  52.6 us (36%)
  starting transfers between devices  32.3 us (22%)
  Pallas kernels  28.1 us (19%)
  blocking collectives  18.4 us (12%)
  local copies, waits for them, and re-layouts  13.4 us (9%)
  other arithmetic  1.84 us (1%)
    ppermute x6, waiting for transfers between devices, chain(): lax.ppermute(down[-1], 'dp', [(i, i - 1) for i in range(1, groups - k + 1)])  46.1 us
    all_gather x1, blocking collectives, shards(): grads = lax.all_gather(grad, 'dp', axis=0)  18.4 us
    ppermute x6, starting transfers between devices, chain(): lax.ppermute(up[-1], 'dp', [(i, i + 1) for i in range(k - 1, groups - 1)])  12.8 us
    all_to_all x3, starting transfers between devices, exchange(): lax.all_to_all(lines, 'pair', split_axis=0, concat_axis=0, tiled=True)  11.8 us
    pallas_call x1, Pallas kernels, mat_grad_of(): pl.pallas_call(functools.partial(mat_grad_kernel, ways, chunk), out_shape...  10.5 us
    pallas_call x2, Pallas kernels, pick_rows(): pl.pallas_call(functools.partial(pick_rows_kernel, ways), out_shape=jax.S...  8.09 us
    ppermute x6, starting transfers between devices, chain(): lax.ppermute(down[-1], 'dp', [(i, i - 1) for i in range(1, groups - k + 1)])  7.69 us
    unnamed x22, local copies, waits for them, and re-layouts  7.32 us
  transfers between devices with their start and end apart: 15, of which 6 were waited for; matrix products, arithmetic and copies ran while one was open for 4% of the time, Pallas kernels for 12%

profile of v2, /device:TPU:0, one launch (start us, length us, event | category | flops | bytes accessed | tf_op | source)
XLA Modules:
  0.0 147.6 jit_solution(5991013809872972496)
XLA Ops:
  0.6 2.0 %slice.18 = bf16[16,64,256]{2,1,0:T(8,128)(2,1)} slice(bf16[16,128,256]{2,1,0:T(8,128)(2,1)} %refs_0_.1), slice={[0:16], [0:64], [0:256]} | slice | bytes 1048576 | tf_op jit(solution)/shard_map/slice | solution.py:315
  2.6 4.9 %collective-permute-start = (bf16[16,64,256]{2,1,0:T(8,128)(2,1)}, bf16[16,64,256]{2,1,0:T(8,128)(2,1)S(1)}, u32[]{:S(2)}, u32[]{:S(2)}) collective-permute-start(bf16[16,64,256]{2,1,0:T(8,128)(2,1)} %slice.18), channel_id=1, source_target_pairs={{0,8},{8,16},{16,24},{1,9},{9,17},{17,25},{2,10},{10,18},{18,26},{... | collective-permute-start | bytes 1572872 | tf_op jit(solution)/shard_map/ppermute | solution.py:295
  7.6 1.3 collective-permute-start.1
  12.5 4.3 %shard_map.85 = bf16[24,128,256]{2,1,0:T(8,128)(2,1)} custom-call(s32[1]{0:T(128)} %constant.11.clone.1.which_ref, s32[24]{0:T(128)S(1)} %reshape.85.table_ref, bf16[16,128,256]{2,1,0:T(8,128)(2,1)S(1)} %copy-done.2), custom_call_target="tpu_custom_call" | custom-call | bytes 1048576 | tf_op jit(solution)/shard_map/pallas_call | solution.py:51
  16.8 3.7 %all-to-all-start = ((bf16[8,384,256]{2,1,0:T(8,128)(2,1)}), bf16[8,384,256]{2,1,0:T(8,128)(2,1)S(1)}, u32[]{:S(2)}, u32[]{:S(2)}) async-start(bf16[8,384,256]{2,1,0:T(8,128)(2,1)} %bitcast.1), calls=%async_computation | async-start | bytes 3145728 | tf_op jit(solution)/shard_map/all_to_all | solution.py:301
  21.3 1.9 %collective-permute-done.1.refs_1_ = bf16[16,64,256]{2,1,0:T(8,128)(2,1)} collective-permute-done((bf16[16,64,256]{2,1,0:T(8,128)(2,1)}, bf16[16,64,256]{2,1,0:T(8,128)(2,1)}, u32[]{:S(2)}, u32[]{:S(2)}) %collective-permute-start.1) | collective-permute-done | bytes 524320 | tf_op jit(solution)/shard_map/ppermute | solution.py:296
  23.2 1.3 collective-permute-start.3
  24.5 1.5 collective-permute-start.4
  25.9 15.2 %collective-permute-done.3.refs_3_ = bf16[16,64,256]{2,1,0:T(8,128)(2,1)S(1)} collective-permute-done((bf16[16,64,256]{2,1,0:T(8,128)(2,1)}, bf16[16,64,256]{2,1,0:T(8,128)(2,1)S(1)}, u32[]{:S(2)}, u32[]{:S(2)}) %collective-permute-start.3) | collective-permute-done | bytes 524320 | tf_op jit(solution)/shard_map/ppermute | solution.py:296
  41.1 1.3 collective-permute-start.5
  43.0 2.8 %copy-done.1 = bf16[48,256,256]{2,1,0:T(8,128)(2,1)S(1)} copy-done((bf16[48,256,256]{2,1,0:T(8,128)(2,1)S(1)}, bf16[48,256,256]{2,1,0:T(8,128)(2,1)}, u32[]{:S(2)}) %copy-start.1) | copy-done | bytes 6291480
  45.7 6.8 %shard_map.86 = bf16[8,400,256]{2,1,0:T(8,128)(2,1)} custom-call(s32[96]{0:T(128)S(1)} %select_reduce_fusion.2.slot_ref, s32[24]{0:T(128)S(1)} %reshape.86.width_ref, bf16[24,128,256]{2,1,0:T(8,128)(2,1)S(1)} %bitcast.14, bf16[48,256,256]{2,1,0:T(8,128)(2,1)S(1)} %copy-done.1), custom_call_target="tpu_custom_call" | custom-call | bytes 1048576 | tf_op jit(solution)/shard_map/pallas_call | solution.py:115
  52.6 4.1 %collective-permute-done.5.refs_5_ = bf16[16,64,256]{2,1,0:T(8,128)(2,1)} collective-permute-done((bf16[16,64,256]{2,1,0:T(8,128)(2,1)S(1)}, bf16[16,64,256]{2,1,0:T(8,128)(2,1)}, u32[]{:S(2)}, u32[]{:S(2)}) %collective-permute-start.5) | collective-permute-done | bytes 524320 | tf_op jit(solution)/shard_map/ppermute | solution.py:296
  56.7 3.6 %all-to-all-start.1 = ((bf16[8,400,256]{2,1,0:T(8,128)(2,1)}), bf16[8,400,256]{2,1,0:T(8,128)(2,1)S(1)}, u32[]{:S(2)}, u32[]{:S(2)}) async-start(bf16[8,400,256]{2,1,0:T(8,128)(2,1)} %shard_map.86), calls=%async_computation.1 | async-start | bytes 3276800 | tf_op jit(solution)/shard_map/all_to_all | solution.py:301
  61.2 2.4 %collective-permute-start.6 = (bf16[24,64,256]{2,1,0:T(8,128)(2,1)}, bf16[24,64,256]{2,1,0:T(8,128)(2,1)}, u32[]{:S(2)}, u32[]{:S(2)}) collective-permute-start(bf16[24,64,256]{2,1,0:T(8,128)(2,1)} %slice.23), channel_id=1, source_target_pairs={{0,8},{8,16},{16,24},{1,9},{9,17},{17,25},{2,10},{10,18},{18,26},{... | collective-permute-start | bytes 2359304 | tf_op jit(solution)/shard_map/ppermute | solution.py:295
  63.7 1.3 collective-permute-start.7
  65.7 1.0 copy-done.4
  66.7 1.0 copy-done.6
  67.8 1.0 copy-done.8
  68.8 3.8 %shard_map.88 = bf16[24,192,256]{2,1,0:T(8,128)(2,1)S(1)} custom-call(s32[3]{0:T(128)S(1)} %slice_bitcast_fusion.1.which_ref, s32[24]{0:T(128)S(1)} %reshape.85.table_ref, bf16[16,64,256]{2,1,0:T(8,128)(2,1)S(1)} %copy-done.4, bf16[16,64,256]{2,1,0:T(8,128)(2,1)} %collective-permute-done.1.refs_1_, bf16[16,64,256]{2,1,0:T(8,128)(2,1)S(1)} %copy-done.6, ...), custom_call_target="tpu_custom_call" | custom-call | bytes 1048576 | tf_op jit(solution)/shard_map/pallas_call | solution.py:51
  72.6 1.4 copy-done
  74.0 6.5 %collective-permute-done.6.refs_0_ = bf16[24,64,256]{2,1,0:T(8,128)(2,1)} collective-permute-done((bf16[24,64,256]{2,1,0:T(8,128)(2,1)}, bf16[24,64,256]{2,1,0:T(8,128)(2,1)}, u32[]{:S(2)}, u32[]{:S(2)}) %collective-permute-start.6) | collective-permute-done | bytes 786464 | tf_op jit(solution)/shard_map/ppermute | solution.py:295
  80.5 5.0 %collective-permute-done.7.refs_1_ = bf16[24,64,256]{2,1,0:T(8,128)(2,1)} collective-permute-done((bf16[24,64,256]{2,1,0:T(8,128)(2,1)}, bf16[24,64,256]{2,1,0:T(8,128)(2,1)}, u32[]{:S(2)}, u32[]{:S(2)}) %collective-permute-start.7) | collective-permute-done | bytes 786464 | tf_op jit(solution)/shard_map/ppermute | solution.py:296
  85.6 4.5 %all-to-all-start.2 = ((bf16[8,576,256]{2,1,0:T(8,128)(2,1)}), bf16[8,576,256]{2,1,0:T(8,128)(2,1)}, u32[]{:S(2)}, u32[]{:S(2)}) async-start(bf16[8,576,256]{2,1,0:T(8,128)(2,1)} %bitcast.17), calls=%async_computation.2 | async-start | bytes 4718592 | tf_op jit(solution)/shard_map/all_to_all | solution.py:301
  90.1 1.6 %collective-permute-start.8 = (bf16[24,64,256]{2,1,0:T(8,128)(2,1)}, bf16[24,64,256]{2,1,0:T(8,128)(2,1)}, u32[]{:S(2)}, u32[]{:S(2)}) collective-permute-start(bf16[24,64,256]{2,1,0:T(8,128)(2,1)} %collective-permute-done.6.refs_0_), channel_id=1, source_target_pairs={{8,16},{16,24},{9,17},{17,25},{10,18},{18,26},{11,19},{19,27},{12,... | collective-permute-start | bytes 2359304 | tf_op jit(solution)/shard_map/ppermute | solution.py:295
  91.7 1.3 collective-permute-start.9
  93.0 1.7 %collective-permute-start.10 = (bf16[24,64,256]{2,1,0:T(8,128)(2,1)}, bf16[24,64,256]{2,1,0:T(8,128)(2,1)}, u32[]{:S(2)}, u32[]{:S(2)}) collective-permute-start(bf16[24,64,256]{2,1,0:T(8,128)(2,1)} %collective-permute-done.8.refs_2_), channel_id=1, source_target_pairs={{16,24},{17,25},{18,26},{19,27},{20,28},{21,29},{22,30},{23,31}} | collective-permute-start | bytes 2359304 | tf_op jit(solution)/shard_map/ppermute | solution.py:295
  94.6 19.9 %collective-permute-done.9.refs_3_ = bf16[24,64,256]{2,1,0:T(8,128)(2,1)} collective-permute-done((bf16[24,64,256]{2,1,0:T(8,128)(2,1)}, bf16[24,64,256]{2,1,0:T(8,128)(2,1)}, u32[]{:S(2)}, u32[]{:S(2)}) %collective-permute-start.9) | collective-permute-done | bytes 786464 | tf_op jit(solution)/shard_map/ppermute | solution.py:296
  114.5 1.3 collective-permute-start.11
  115.9 2.7 %shard_map.87 = (f32[16,128,256]{2,1,0:T(8,128)}, f32[1,128]{1,0:T(1,128)}, f32[1,128]{1,0:T(1,128)S(1)}) custom-call(s32[24]{0:T(128)S(1)} %reshape.85.table_ref, s32[16]{0:T(128)S(1)} %dynamic_slice.8.width_ref, bf16[8,400,256]{2,1,0:T(8,128)(2,1)S(1)} %all-to-all-done.1.back_ref, s32[1,128]{1,0:T(1,128)S(1)} %bitcast.18), custom_call_target="tpu_custom_call" | custom-call | bytes 1048576 | tf_op jit(solution)/shard_map/pallas_call | solution.py:164
  118.6 18.4 %all-gather.1.grads_ref = f32[4,1,128]{2,1,0:T(1,128)S(1)} all-gather(f32[1,1,128]{2,1,0:T(1,128)S(1)} %bitcast.19), channel_id=2, replica_groups=mesh['dp'=4,'pair'=8] {'dp'}, dimensions={0}, use_global_device_ids=true | all-gather | bytes 2560 | tf_op jit(solution)/shard_map/all_gather | solution.py:337
  137.0 10.5 %shard_map.89 = bf16[48,64,256]{2,1,0:T(8,128)(2,1)} custom-call(s32[96]{0:T(128)S(1)} %select_reduce_fusion.2.slot_ref, s32[24]{0:T(128)S(1)} %reshape.86.width_ref, s32[3]{0:T(128)S(1)} %slice_bitcast_fusion.1.which_ref, s32[4]{0:T(128)S(1)} %slice_bitcast_fusion.source_ref, s32[1]{0:T(128)} %bitcast.7.first_ref, f32[4,1,128]{2,1,0:T(1,128)S(1)} %all-gather.1.grads_ref, ...), custom_call_target="tpu_custom_call" | custom-call | bytes 1048576 | tf_op jit(solution)/shard_map/pallas_call | solution.py:240
  (55 shorter events, 6.7 us)
Async XLA Ops:
  0.6 11.9 %copy-start.2 = (bf16[16,128,256]{2,1,0:T(8,128)(2,1)S(1)}, bf16[16,128,256]{2,1,0:T(8,128)(2,1)}, u32[]{:S(2)}) copy-start(bf16[16,128,256]{2,1,0:T(8,128)(2,1)} %refs_0_.1) | copy-start | bytes 3145732
  2.6 18.0 %collective-permute-start = (bf16[16,64,256]{2,1,0:T(8,128)(2,1)}, bf16[16,64,256]{2,1,0:T(8,128)(2,1)S(1)}, u32[]{:S(2)}, u32[]{:S(2)}) collective-permute-start(bf16[16,64,256]{2,1,0:T(8,128)(2,1)} %slice.18), channel_id=1, source_target_pairs={{0,8},{8,16},{16,24},{1,9},{9,17},{17,25},{2,10},{10,18},{18,26},{... | collective-permute-start | bytes 1572872 | tf_op jit(solution)/shard_map/ppermute | solution.py:295
  7.6 15.6 %collective-permute-start.1 = (bf16[16,64,256]{2,1,0:T(8,128)(2,1)}, bf16[16,64,256]{2,1,0:T(8,128)(2,1)}, u32[]{:S(2)}, u32[]{:S(2)}) collective-permute-start(bf16[16,64,256]{2,1,0:T(8,128)(2,1)} %slice.18), channel_id=1, source_target_pairs={{8,0},{16,8},{24,16},{9,1},{17,9},{25,17},{10,2},{18,10},{26,18},{... | collective-permute-start | bytes 1572872 | tf_op jit(solution)/shard_map/ppermute | solution.py:296
  16.8 26.1 %all-to-all-start = ((bf16[8,384,256]{2,1,0:T(8,128)(2,1)}), bf16[8,384,256]{2,1,0:T(8,128)(2,1)S(1)}, u32[]{:S(2)}, u32[]{:S(2)}) async-start(bf16[8,384,256]{2,1,0:T(8,128)(2,1)} %bitcast.1), calls=%async_computation | async-start | bytes 3145728 | tf_op jit(solution)/shard_map/all_to_all | solution.py:301
  20.6 32.0 %copy-start.3 = (bf16[16,64,256]{2,1,0:T(8,128)(2,1)}, bf16[16,64,256]{2,1,0:T(8,128)(2,1)S(1)}, u32[]{:S(2)}) copy-start(bf16[16,64,256]{2,1,0:T(8,128)(2,1)S(1)} %collective-permute-done.refs_0_) | copy-start | bytes 1572868
  20.6 3.9 %collective-permute-start.2 = (bf16[16,64,256]{2,1,0:T(8,128)(2,1)S(1)}, bf16[16,64,256]{2,1,0:T(8,128)(2,1)S(1)}, u32[]{:S(2)}, u32[]{:S(2)}) collective-permute-start(bf16[16,64,256]{2,1,0:T(8,128)(2,1)S(1)} %collective-permute-done.refs_0_), channel_id=1, source_target_pairs={{8,16},{16,24},{9,17},{17,25},{10,18},{18,26},{11,19},{19,27},{12,... | collective-permute-start | bytes 1572872 | tf_op jit(solution)/shard_map/ppermute | solution.py:295
  23.2 18.0 %collective-permute-start.3 = (bf16[16,64,256]{2,1,0:T(8,128)(2,1)}, bf16[16,64,256]{2,1,0:T(8,128)(2,1)S(1)}, u32[]{:S(2)}, u32[]{:S(2)}) collective-permute-start(bf16[16,64,256]{2,1,0:T(8,128)(2,1)} %collective-permute-done.1.refs_1_), channel_id=1, source_target_pairs={{8,0},{16,8},{9,1},{17,9},{10,2},{18,10},{11,3},{19,11},{12,4},{20... | collective-permute-start | bytes 1572872 | tf_op jit(solution)/shard_map/ppermute | solution.py:296
  24.5 28.1 %copy-start.5 = (bf16[16,64,256]{2,1,0:T(8,128)(2,1)}, bf16[16,64,256]{2,1,0:T(8,128)(2,1)S(1)}, u32[]{:S(2)}) copy-start(bf16[16,64,256]{2,1,0:T(8,128)(2,1)S(1)} %collective-permute-done.2.refs_2_) | copy-start | bytes 1572868
  24.5 28.1 %collective-permute-start.4 = (bf16[16,64,256]{2,1,0:T(8,128)(2,1)S(1)}, bf16[16,64,256]{2,1,0:T(8,128)(2,1)}, u32[]{:S(2)}, u32[]{:S(2)}) collective-permute-start(bf16[16,64,256]{2,1,0:T(8,128)(2,1)S(1)} %collective-permute-done.2.refs_2_), channel_id=1, source_target_pairs={{16,24},{17,25},{18,26},{19,27},{20,28},{21,29},{22,30},{23,31}} | collective-permute-start | bytes 1572872 | tf_op jit(solution)/shard_map/ppermute | solution.py:295
  41.1 11.4 %copy-start.7 = (bf16[16,64,256]{2,1,0:T(8,128)(2,1)}, bf16[16,64,256]{2,1,0:T(8,128)(2,1)S(1)}, u32[]{:S(2)}) copy-start(bf16[16,64,256]{2,1,0:T(8,128)(2,1)S(1)} %collective-permute-done.3.refs_3_) | copy-start | bytes 1572868
  41.1 15.5 %collective-permute-start.5 = (bf16[16,64,256]{2,1,0:T(8,128)(2,1)S(1)}, bf16[16,64,256]{2,1,0:T(8,128)(2,1)}, u32[]{:S(2)}, u32[]{:S(2)}) collective-permute-start(bf16[16,64,256]{2,1,0:T(8,128)(2,1)S(1)} %collective-permute-done.3.refs_3_), channel_id=1, source_target_pairs={{8,0},{9,1},{10,2},{11,3},{12,4},{13,5},{14,6},{15,7}} | collective-permute-start | bytes 1572872 | tf_op jit(solution)/shard_map/ppermute | solution.py:296
  42.9 2.8 %copy-start.1 = (bf16[48,256,256]{2,1,0:T(8,128)(2,1)S(1)}, bf16[48,256,256]{2,1,0:T(8,128)(2,1)}, u32[]{:S(2)}) copy-start(bf16[48,256,256]{2,1,0:T(8,128)(2,1)} %mats_ref.1) | copy-start | bytes 18874372
  56.7 28.9 %all-to-all-start.1 = ((bf16[8,400,256]{2,1,0:T(8,128)(2,1)}), bf16[8,400,256]{2,1,0:T(8,128)(2,1)S(1)}, u32[]{:S(2)}, u32[]{:S(2)}) async-start(bf16[8,400,256]{2,1,0:T(8,128)(2,1)} %shard_map.86), calls=%async_computation.1 | async-start | bytes 3276800 | tf_op jit(solution)/shard_map/all_to_all | solution.py:301
  61.2 19.3 %collective-permute-start.6 = (bf16[24,64,256]{2,1,0:T(8,128)(2,1)}, bf16[24,64,256]{2,1,0:T(8,128)(2,1)}, u32[]{:S(2)}, u32[]{:S(2)}) collective-permute-start(bf16[24,64,256]{2,1,0:T(8,128)(2,1)} %slice.23), channel_id=1, source_target_pairs={{0,8},{8,16},{16,24},{1,9},{9,17},{17,25},{2,10},{10,18},{18,26},{... | collective-permute-start | bytes 2359304 | tf_op jit(solution)/shard_map/ppermute | solution.py:295
  63.7 21.9 %collective-permute-start.7 = (bf16[24,64,256]{2,1,0:T(8,128)(2,1)}, bf16[24,64,256]{2,1,0:T(8,128)(2,1)}, u32[]{:S(2)}, u32[]{:S(2)}) collective-permute-start(bf16[24,64,256]{2,1,0:T(8,128)(2,1)} %slice.23), channel_id=1, source_target_pairs={{8,0},{16,8},{24,16},{9,1},{17,9},{25,17},{10,2},{18,10},{26,18},{... | collective-permute-start | bytes 2359304 | tf_op jit(solution)/shard_map/ppermute | solution.py:296
  65.7 1.0 copy-start.4
  66.7 1.0 copy-start.6
  67.8 1.0 copy-start.8
  72.6 1.4 copy-start
  85.5 30.2 %copy-start.10 = (s32[128]{0:T(128)S(1)}, s32[128]{0:T(128)}, u32[]{:S(2)}) copy-start(s32[128]{0:T(128)} %param.7) | copy-start | bytes 1540
  85.6 30.4 %copy-start.9 = (s32[128]{0:T(128)S(1)}, s32[128]{0:T(128)}, u32[]{:S(2)}) copy-start(s32[128]{0:T(128)} %param.10) | copy-start | bytes 1540
  85.6 51.5 %all-to-all-start.2 = ((bf16[8,576,256]{2,1,0:T(8,128)(2,1)}), bf16[8,576,256]{2,1,0:T(8,128)(2,1)}, u32[]{:S(2)}, u32[]{:S(2)}) async-start(bf16[8,576,256]{2,1,0:T(8,128)(2,1)} %bitcast.17), calls=%async_computation.2 | async-start | bytes 4718592 | tf_op jit(solution)/shard_map/all_to_all | solution.py:301
  90.1 2.9 %collective-permute-start.8 = (bf16[24,64,256]{2,1,0:T(8,128)(2,1)}, bf16[24,64,256]{2,1,0:T(8,128)(2,1)}, u32[]{:S(2)}, u32[]{:S(2)}) collective-permute-start(bf16[24,64,256]{2,1,0:T(8,128)(2,1)} %collective-permute-done.6.refs_0_), channel_id=1, source_target_pairs={{8,16},{16,24},{9,17},{17,25},{10,18},{18,26},{11,19},{19,27},{12,... | collective-permute-start | bytes 2359304 | tf_op jit(solution)/shard_map/ppermute | solution.py:295
  91.7 22.8 %collective-permute-start.9 = (bf16[24,64,256]{2,1,0:T(8,128)(2,1)}, bf16[24,64,256]{2,1,0:T(8,128)(2,1)}, u32[]{:S(2)}, u32[]{:S(2)}) collective-permute-start(bf16[24,64,256]{2,1,0:T(8,128)(2,1)} %collective-permute-done.7.refs_1_), channel_id=1, source_target_pairs={{8,0},{16,8},{9,1},{17,9},{10,2},{18,10},{11,3},{19,11},{12,4},{20... | collective-permute-start | bytes 2359304 | tf_op jit(solution)/shard_map/ppermute | solution.py:296
  93.0 44.1 %collective-permute-start.10 = (bf16[24,64,256]{2,1,0:T(8,128)(2,1)}, bf16[24,64,256]{2,1,0:T(8,128)(2,1)}, u32[]{:S(2)}, u32[]{:S(2)}) collective-permute-start(bf16[24,64,256]{2,1,0:T(8,128)(2,1)} %collective-permute-done.8.refs_2_), channel_id=1, source_target_pairs={{16,24},{17,25},{18,26},{19,27},{20,28},{21,29},{22,30},{23,31}} | collective-permute-start | bytes 2359304 | tf_op jit(solution)/shard_map/ppermute | solution.py:295
  114.5 22.5 %collective-permute-start.11 = (bf16[24,64,256]{2,1,0:T(8,128)(2,1)}, bf16[24,64,256]{2,1,0:T(8,128)(2,1)}, u32[]{:S(2)}, u32[]{:S(2)}) collective-permute-start(bf16[24,64,256]{2,1,0:T(8,128)(2,1)} %collective-permute-done.9.refs_3_), channel_id=1, source_target_pairs={{8,0},{9,1},{10,2},{11,3},{12,4},{13,5},{14,6},{15,7}} | collective-permute-start | bytes 2359304 | tf_op jit(solution)/shard_map/ppermute | solution.py:296

commit v3 on v2

--- a/solution.py
+++ b/solution.py
@@ -10,53 +10,121 @@
 
 CAP = 3
 NOTE = 16
-RAW = 64
+RAW = 48
 VMEM = pl.BlockSpec(memory_space=pltpu.VMEM)
 SMEM = pl.BlockSpec(memory_space=pltpu.SMEM)
 HBM = pl.BlockSpec(memory_space=pl.ANY)
 F32 = jnp.float32
 BF16 = jnp.bfloat16
-CHEAP = pl.CostEstimate(flops=0, bytes_accessed=1 << 20, transcendentals=0)
+CHEAP = pl.CostEstimate(flops=0, bytes_accessed=0, transcendentals=0)
 
 
 def limit(size):
     return pltpu.CompilerParams(vmem_limit_bytes=size + (4 << 20))
 
 
-def pick_rows_kernel(ways, which_ref, table_ref, *refs):
-    *sources, out_ref, sems = refs
-    slots = out_ref.shape[0]
+def own_rows_kernel(owner_ref, pairs_ref, rows_ref, out_ref, near_ref, table_ref, scalar_ref, sems, table_sem):
+    fields = rows_ref.shape[0]
+    owners = out_ref.shape[0]
+    lines, width = out_ref.shape[1] // CAP, out_ref.shape[2]
+    total = pairs_ref.shape[1]
+    near = pltpu.make_async_copy(rows_ref.at[:, pl.ds(0, near_ref.shape[1]), :], near_ref, sems.at[owners * CAP])
+    near.start()
+    local = pairs_ref[...] - owner_ref[0] * fields
+    field = lax.broadcasted_iota(jnp.int32, (fields, total), 0)
+    hit = ((local[0:1] == field) | (local[1:2] == field)).astype(BF16)
+    low = lax.broadcasted_iota(jnp.int32, (total, 128), 1) * (total // owners)
+    at = lax.broadcasted_iota(jnp.int32, (total, 128), 0)
+    segment = ((at >= low) & (at < low + total // owners)).astype(BF16)
+    needed = jnp.dot(hit, segment, preferred_element_type=F32) > 0
+    before = lax.broadcasted_iota(jnp.int32, (fields, fields), 0) > lax.broadcasted_iota(jnp.int32, (fields, fields), 1)
+    rank = jnp.dot(before.astype(BF16), needed.astype(BF16), preferred_element_type=F32)
+    ids = lax.broadcasted_iota(jnp.int32, (fields, 128), 0).astype(F32)
+    rows = lax.broadcasted_iota(jnp.int32, (8, 128), 0)
+    table = jnp.zeros((8, 128), F32)
+    for c in range(CAP):
+        chosen = jnp.sum(jnp.where(needed & (rank == c), ids, 0.0), axis=0, keepdims=True)
+        table = jnp.where(rows == c, chosen, table)
+    table_ref[...] = table.astype(jnp.int32)
+    copy = pltpu.make_async_copy(table_ref, scalar_ref, table_sem)
+    copy.start()
+    copy.wait()
+
+    def move(d, c, f):
+        place = out_ref.at[d, pl.ds(c * lines, lines), :]
+        return pltpu.make_async_copy(rows_ref.at[f], place, sems.at[d * CAP + c])
+
+    @pl.loop(0, owners)
+    def _(d):
+        for c in range(CAP):
+            move(d, c, scalar_ref[c, d]).start()
+
+    @pl.loop(0, owners)
+    def _(d):
+        for c in range(CAP):
+            move(d, c, 0).wait()
+
+    near.wait()
+
+
+def own_rows(owner, pair_list, embeddings, owners):
+    fields, samples, width = embeddings.shape
+    out = (owners, CAP * samples, width)
+    near = (fields, RAW, width)
+    return pl.pallas_call(
+        own_rows_kernel,
+        out_shape=(
+            jax.ShapeDtypeStruct(out, BF16),
+            jax.ShapeDtypeStruct(near, BF16),
+            jax.ShapeDtypeStruct((8, 128), jnp.int32),
+        ),
+        in_specs=[SMEM, VMEM, HBM],
+        out_specs=(VMEM, VMEM, VMEM),
+        scratch_shapes=[
+            pltpu.SMEM((8, 128), jnp.int32),
+            pltpu.SemaphoreType.DMA((owners * CAP + 1,)),
+            pltpu.SemaphoreType.DMA,
+        ],
+        compiler_params=limit(56 << 20),
+        cost_estimate=CHEAP,
+    )(owner, pair_list, embeddings)
+
+
+def far_rows_kernel(ways, count, owner_ref, which_ref, table_ref, *refs):
+    sources, outs, sems = refs[:count], refs[count:-1], refs[-1]
     lines = sources[0].shape[1]
+
+    def move(r, source, k, c, f):
+        place = outs[k].at[c, pl.ds(r * lines, lines), :]
+        return pltpu.make_async_copy(source.at[f], place, sems.at[r, k * CAP + c])
+
     for r, choices in enumerate(ways):
         for at, source in enumerate(choices):
 
             @pl.when(which_ref[r] == at)
             def _(r=r, source=source):
-                @pl.loop(0, slots)
-                def _(j):
-                    place = out_ref.at[j, pl.ds(r * lines, lines), :]
-                    pltpu.make_async_copy(sources[source].at[table_ref[j]], place, sems.at[r, j]).start()
+                for k in range(len(outs)):
+                    for c in range(CAP):
+                        move(r, sources[source], k, c, table_ref[c, owner_ref[0] ^ k]).start()
 
     for r in range(len(ways)):
-
-        @pl.loop(0, slots)
-        def _(j, r=r):
-            place = out_ref.at[j, pl.ds(r * lines, lines), :]
-            pltpu.make_async_copy(sources[0].at[0], place, sems.at[r, j]).wait()
-
-
-def pick_rows(ways, which, table, sources):
+        for k in range(len(outs)):
+            for c in range(CAP):
+                move(r, sources[0], k, c, 0).wait()
+
+
+def far_rows(ways, owner, which, table, sources, owners):
     _, lines, width = sources[0].shape
-    shape = (table.shape[0], len(ways) * lines, width)
+    shape = (CAP, len(ways) * lines, width)
     return pl.pallas_call(
-        functools.partial(pick_rows_kernel, ways),
-        out_shape=jax.ShapeDtypeStruct(shape, BF16),
-        in_specs=[SMEM, SMEM] + [HBM] * len(sources),
-        out_specs=VMEM,
-        scratch_shapes=[pltpu.SemaphoreType.DMA((len(ways), shape[0]))],
-        compiler_params=limit(math.prod(shape) * 2),
+        functools.partial(far_rows_kernel, ways, len(sources)),
+        out_shape=[jax.ShapeDtypeStruct(shape, BF16)] * owners,
+        in_specs=[SMEM, SMEM, SMEM] + [HBM] * len(sources),
+        out_specs=[VMEM] * owners,
+        scratch_shapes=[pltpu.SemaphoreType.DMA((len(ways), owners * CAP))],
+        compiler_params=limit(owners * math.prod(shape) * 2),
         cost_estimate=CHEAP,
-    )(which, table, *sources)
+    )(owner, which, table, *sources)
 
 
 def forward_kernel(group, slot_ref, width_ref, rows_ref, mats_ref, sums_ref, x_ref, u_ref, acc_ref):
@@ -140,7 +208,7 @@
     @pl.loop(0, owners)
     def _(o):
         for c in range(CAP):
-            f = table_ref[o * CAP + c]
+            f = table_ref[c, o]
             out_ref[f] += back_ref[o, c * samples : (c + 1) * samples, :].astype(F32)
 
     note = back_ref[0, lines : lines + NOTE, 0:samples].astype(F32)
@@ -175,8 +243,9 @@
     )(table, own_width, back, labels)
 
 
-def mat_grad_kernel(ways, chunk, slot_ref, width_ref, which_ref, source_ref, first_ref, grads_ref, own_ref, raw_ref, *refs):
-    *links, out_ref, x_ref, t_ref, acc_ref, sems = refs
+def mat_grad_kernel(ways, chunk, owners, slot_ref, width_ref, which_ref, source_ref, first_ref, owner_ref, grads_ref, own_ref, *refs):
+    raws = refs[:owners]
+    *links, out_ref, x_ref, t_ref, acc_ref, sems = refs[owners:]
     count = len(ways) + 1
     width = x_ref.shape[2]
     slots, samples, _ = own_ref.shape
@@ -198,9 +267,11 @@
                 waits[-1].start()
                 continue
             r = start + k - 1
-            raw = raw_ref.at[:, pl.ds(r * raw_lines, raw_lines), :]
-            waits.append(pltpu.make_async_copy(raw, place(k, 0, raw_lines), sems.at[k, 0]))
-            waits[-1].start()
+            for d in range(owners):
+                raw = raws[d].at[:, pl.ds(r * raw_lines, raw_lines), :]
+                spot = x_ref.at[pl.ds((owner_ref[0] ^ d) * CAP, CAP), pl.ds(k * samples, raw_lines), :]
+                waits.append(pltpu.make_async_copy(raw, spot, sems.at[k, 2 + d]))
+                waits[-1].start()
             for at, link in enumerate(ways[r]):
 
                 @pl.when(which_ref[r] == at)
@@ -230,7 +301,7 @@
                 out_ref[p] = jnp.where(kept, term, 0.0).astype(BF16)
 
 
-def mat_grad_of(ways, slot_index, slot_width, which, sources, first, grads, own, raw, links, rows):
+def mat_grad_of(ways, slot_index, slot_width, which, sources, first, owner, grads, own, raw, links, rows):
     slots, samples, width = own.shape
     pairs = slot_index.shape[0] // 2
     chunk = len(ways) + 1
@@ -238,19 +309,19 @@
         chunk //= 2
     size = chunk * slots * samples * (width + rows) * 2 + pairs * rows * width * 6
     return pl.pallas_call(
-        functools.partial(mat_grad_kernel, ways, chunk),
+        functools.partial(mat_grad_kernel, ways, chunk, len(raw)),
         out_shape=jax.ShapeDtypeStruct((pairs, rows, width), BF16),
-        in_specs=[SMEM, SMEM, SMEM, SMEM, SMEM, VMEM] + [HBM] * (2 + len(links)),
+        in_specs=[SMEM] * 6 + [VMEM] + [HBM] * (1 + len(raw) + len(links)),
         out_specs=VMEM,
         scratch_shapes=[
             pltpu.VMEM((slots, chunk * samples, width), BF16),
             pltpu.VMEM((slots, rows, chunk * samples), BF16),
             pltpu.VMEM((pairs, rows, width), F32),
-            pltpu.SemaphoreType.DMA((chunk, 2)),
+            pltpu.SemaphoreType.DMA((chunk, 2 + len(raw))),
         ],
         compiler_params=limit(size),
         cost_estimate=CHEAP,
-    )(slot_index, slot_width, which, sources, first, grads, own, raw, *links)
+    )(slot_index, slot_width, which, sources, first, owner, grads, own, *raw, *links)
 
 
 def line_rounds(n):
@@ -272,11 +343,7 @@
     pair_list = pair_fields.T
     field_ids = jnp.arange(fields, dtype=jnp.int32)
     slot_ids = jnp.arange(CAP, dtype=jnp.int32)
-    local = pair_list.reshape(2, owners, 1, pairs) - owner * fields
-    needed = jnp.any(local == field_ids[None, None, :, None], axis=(0, 3)).astype(jnp.int32)
-    rank = jnp.sum(jnp.where(field_ids[:, None] > field_ids[None, :], needed[:, None, :], 0), axis=2)
-    chosen = (needed[:, None, :] > 0) & (rank[:, None, :] == slot_ids[None, :, None])
-    table = jnp.sum(jnp.where(chosen, field_ids[None, None, :], 0), axis=2).reshape(-1)
+    picked, near, table = own_rows(owner.reshape(1), pair_list, embeddings, owners)
 
     mine = lax.dynamic_slice_in_dim(pair_list, owner * pairs, pairs, 1)
     all_ids = jnp.arange(every, dtype=jnp.int32)
@@ -289,12 +356,22 @@
     slot_width = jnp.sum(jnp.where(taken, field_width.reshape(owners, 1, fields), 0), axis=2).reshape(-1)
     own_width = lax.dynamic_slice_in_dim(field_width, owner * fields, fields, 0)
 
-    def chain(first):
-        up, down = [first], [first]
-        for k in range(1, groups):
-            up.append(lax.ppermute(up[-1], "dp", [(i, i + 1) for i in range(k - 1, groups - 1)]))
-            down.append(lax.ppermute(down[-1], "dp", [(i, i - 1) for i in range(1, groups - k + 1)]))
-            yield up[-1], down[-1]
+    def chain(own):
+        up = lax.ppermute(own, "dp", [(i, i + 1) for i in range(groups - 1)])
+        down = lax.ppermute(own, "dp", [(i + 1, i) for i in range(groups - 1)])
+        yield [up, down]
+        found = [up, down]
+        for k in range(2, groups):
+            if k == 2:
+                found.append(lax.ppermute(up, "dp", [(i, i + 1) for i in range(1, groups - 1)]))
+                found.append(lax.ppermute(down, "dp", [(i, i - 1) for i in range(1, groups - 1)]))
+            elif 2 * k >= groups:
+                ends = [(i, i + k) for i in range(groups - k)]
+                found += [lax.ppermute(own, "dp", ends + [(j, i) for i, j in ends])] * 2
+            else:
+                found.append(lax.ppermute(own, "dp", [(i, i + k) for i in range(groups - k)]))
+                found.append(lax.ppermute(own, "dp", [(i + k, i) for i in range(groups - k)]))
+        yield found
 
     def exchange(rows):
         lines = rows.reshape(owners, -1, width)
@@ -312,32 +389,26 @@
     places = lax.dynamic_index_in_dim(places, group, 0, keepdims=False)
     which, sources = places[: groups - 1], places[groups - 1 :]
 
-    raw_steps = chain(embeddings[:, :RAW])
-    raw = []
-    for _ in range(max(1, groups - 2)):
-        raw += next(raw_steps)
-    picked = pick_rows([[0]], jnp.zeros((1,), jnp.int32), table, [embeddings])
+    raw_steps = chain(near)
+    close = next(raw_steps)
     received = exchange(picked).reshape(owners * CAP, samples, width)
-    received, raw = tie((received, raw))
-
-    for step in raw_steps:
-        raw += step
+    received, close[:] = tie((received, close))
+    raw = next(raw_steps)
     kept_steps = chain(received[:, RAW:])
     sums = forward(slot_index, slot_width, received, pair_mats)
     sums, raw = tie((sums, raw))
     back = exchange(sums)
-    far = pick_rows(ways, which, table, raw)
-    kept = [*next(kept_steps)]
-    far, kept = tie((far, kept))
-    far = exchange(far).reshape(owners * CAP, -1, width)
-    for step in kept_steps:
-        kept += step
+    near_kept = next(kept_steps)
+    raw, near_kept[:] = tie((raw, near_kept))
+    far = far_rows(ways, owner.reshape(1), which, table, raw, owners)
+    far = [lax.ppermute(x, "pair", [(i, i ^ k) for i in range(owners)]) if k else x for k, x in enumerate(far)]
+    kept = next(kept_steps)
     emb_grad, logits, grad = emb_grad_of(table, own_width, back, labels[None, :], fields)
     logits = logits.reshape(samples)
-    grads = lax.all_gather(grad, "dp", axis=0)
+    grads = lax.all_to_all(jnp.broadcast_to(grad, (groups, 1, samples)), "dp", split_axis=0, concat_axis=0, tiled=True)
     rows = width // groups
     mat_grad = mat_grad_of(
-        ways, slot_index, slot_width, which, sources, (group * rows).reshape(1), grads, received, far, kept, rows
+        ways, slot_index, slot_width, which, sources, (group * rows).reshape(1), owner.reshape(1), grads, received, far, kept, rows
     )
     return (logits, mat_grad, emb_grad)
 

time: 148 us -> 132 us (0.89)
  waiting for transfers between devices: 52.6 us -> 22.2 us
  starting transfers between devices: 32.3 us -> 59.8 us
  blocking collectives: 18.4 us -> 0 us
  Pallas kernels: 28.1 us -> 30.3 us
  local copies, waits for them, and re-layouts: 13.4 us -> 15.5 us
    ppermute x12 -> x17, waiting for transfers between devices: 52.6 us -> 20 us  [the longest x7 9.97 us: shards(): lax.ppermute(x, 'pair', [(i, i ^ k) for i in range(owners)])]
    ppermute x12 -> x17, starting transfers between devices: 20.5 us -> 43.5 us  [the longest x2 15.1 us: chain(): up = lax.ppermute(own, 'dp', [(i, i + 1) for i in range(groups - 1)])]
    all_gather x1 -> x0, blocking collectives: 18.4 us -> none  [shards(): grads = lax.all_gather(grad, 'dp', axis=0)]
    all_to_all x0 -> x1, starting transfers between devices: none -> 6.96 us  [shards(): lax.all_to_all(jnp.broadcast_to(grad, (groups, 1, samples)), 'dp', split_...]
    unnamed x22 -> x42, local copies, waits for them, and re-layouts: 7.32 us -> 11.7 us
    all_to_all x3 -> x2, starting transfers between devices: 11.8 us -> 9.27 us  [exchange(): lax.all_to_all(lines, 'pair', split_axis=0, concat_axis=0, tiled=True)]
    all_to_all x3 -> x2, waiting for transfers between devices: 0.01 us -> 2.21 us  [exchange(): lax.all_to_all(lines, 'pair', split_axis=0, concat_axis=0, tiled=True)]
    slice x1 -> x0, local copies, waits for them, and re-layouts: 1.97 us -> none  [shards(): raw_steps = chain(embeddings[:, :RAW])]
  transfers between devices with their start and end apart: 15 -> 20, of which waited for: 6 -> 6; matrix products, arithmetic and copies ran while one was open for 4% -> 4% of each run, Pallas kernels for 12% -> 12%
where the time goes in v3:
time: 132 us; the launch traced here: 131 us
  starting transfers between devices  59.8 us (45%)
  Pallas kernels  30.3 us (23%)
  waiting for transfers between devices  22.2 us (17%)
  local copies, waits for them, and re-layouts  15.5 us (12%)
  other arithmetic  1.9 us (1%)
    ppermute x2, starting transfers between devices, chain(): up = lax.ppermute(own, 'dp', [(i, i + 1) for i in range(groups - 1)])  15.1 us
    ppermute x2, starting transfers between devices, chain(): found += [lax.ppermute(own, 'dp', ends + [(j, i) for i, j in ends])] * 2  12 us
    unnamed x42, local copies, waits for them, and re-layouts  11.7 us
    pallas_call x1, Pallas kernels, mat_grad_of(): pl.pallas_call(functools.partial(mat_grad_kernel, ways, chunk, len(raw)),...  10.8 us
    ppermute x7, waiting for transfers between devices, shards(): lax.ppermute(x, 'pair', [(i, i ^ k) for i in range(owners)])  9.97 us
    all_to_all x2, starting transfers between devices, exchange(): lax.all_to_all(lines, 'pair', split_axis=0, concat_axis=0, tiled=True)  9.27 us
    ppermute x7, starting transfers between devices, shards(): lax.ppermute(x, 'pair', [(i, i ^ k) for i in range(owners)])  9 us
    pallas_call x1, Pallas kernels, forward(): pl.pallas_call(functools.partial(forward_kernel, group), grid=(pairs // g...  7.1 us
  transfers between devices with their start and end apart: 20, of which 6 were waited for; matrix products, arithmetic and copies ran while one was open for 4% of the time, Pallas kernels for 12%

profile of v3, /device:TPU:0, one launch (start us, length us, event | category | flops | bytes accessed | tf_op | source)
XLA Modules:
  0.0 130.6 jit_solution(740353673732989446)
XLA Ops:
  0.6 4.4 %shard_map.85 = (bf16[8,384,256]{2,1,0:T(8,128)(2,1)}, bf16[16,48,256]{2,1,0:T(8,128)(2,1)}, s32[8,128]{1,0:T(8,128)}) custom-call(s32[1]{0:T(128)} %bitcast.owner_ref, s32[2,384]{1,0:T(2,128)} %bitcast.16, bf16[16,128,256]{2,1,0:T(8,128)(2,1)} %rows_ref.1), custom_call_target="tpu_custom_call" | custom-call | tf_op jit(solution)/shard_map/pallas_call | solution.py:74
  5.1 5.4 %all-to-all-start = ((bf16[8,384,256]{2,1,0:T(8,128)(2,1)}), bf16[8,384,256]{2,1,0:T(8,128)(2,1)S(1)}, u32[]{:S(2)}, u32[]{:S(2)}) async-start(bf16[8,384,256]{2,1,0:T(8,128)(2,1)} %get-tuple-element.32), calls=%async_computation | async-start | bytes 3145728 | tf_op jit(solution)/shard_map/all_to_all | solution.py:378
  10.5 3.5 %collective-permute-start = (bf16[16,48,256]{2,1,0:T(8,128)(2,1)}, bf16[16,48,256]{2,1,0:T(8,128)(2,1)S(1)}, u32[]{:S(2)}, u32[]{:S(2)}) collective-permute-start(bf16[16,48,256]{2,1,0:T(8,128)(2,1)} %get-tuple-element.33), channel_id=1, source_target_pairs={{0,8},{8,16},{16,24},{1,9},{9,17},{17,25},{2,10},{10,18},{18,26},{... | collective-permute-start | bytes 1179656 | tf_op jit(solution)/shard_map/ppermute | solution.py:360
  14.0 1.3 collective-permute-start.1
  15.3 6.6 %collective-permute-start.4 = (bf16[16,48,256]{2,1,0:T(8,128)(2,1)}, bf16[16,48,256]{2,1,0:T(8,128)(2,1)S(1)}, u32[]{:S(2)}, u32[]{:S(2)}) collective-permute-start(bf16[16,48,256]{2,1,0:T(8,128)(2,1)} %get-tuple-element.33), channel_id=1, source_target_pairs={{0,24},{24,0},{1,25},{25,1},{2,26},{26,2},{3,27},{27,3},{4,28},{28... | collective-permute-start | bytes 1179656 | tf_op jit(solution)/shard_map/ppermute | solution.py:370
  24.4 3.0 %collective-permute-done.1.refs_1_ = bf16[16,48,256]{2,1,0:T(8,128)(2,1)S(1)} collective-permute-done((bf16[16,48,256]{2,1,0:T(8,128)(2,1)}, bf16[16,48,256]{2,1,0:T(8,128)(2,1)S(1)}, u32[]{:S(2)}, u32[]{:S(2)}) %collective-permute-start.1) | collective-permute-done | bytes 393248 | tf_op jit(solution)/shard_map/ppermute | solution.py:361
  27.3 1.3 collective-permute-start.3
  29.3 2.2 %all-to-all-done = bf16[8,384,256]{2,1,0:T(8,128)(2,1)S(1)} async-done(((bf16[8,384,256]{2,1,0:T(8,128)(2,1)}), bf16[8,384,256]{2,1,0:T(8,128)(2,1)S(1)}, u32[]{:S(2)}, u32[]{:S(2)}) %all-to-all-start) | async-done | bytes 1572896 | tf_op jit(solution)/shard_map/all_to_all | solution.py:378
  31.5 1.0 slice.19
  32.5 11.6 %collective-permute-start.5 = (bf16[24,80,256]{2,1,0:T(8,128)(2,1)}, bf16[24,80,256]{2,1,0:T(8,128)(2,1)}, u32[]{:S(2)}, u32[]{:S(2)}) collective-permute-start(bf16[24,80,256]{2,1,0:T(8,128)(2,1)} %slice.19), channel_id=1, source_target_pairs={{0,8},{8,16},{16,24},{1,9},{9,17},{17,25},{2,10},{10,18},{18,26},{... | collective-permute-start | bytes 2949128 | tf_op jit(solution)/shard_map/ppermute | solution.py:360
  44.1 1.3 collective-permute-start.6
  46.4 2.8 %copy-done = bf16[48,256,256]{2,1,0:T(8,128)(2,1)S(1)} copy-done((bf16[48,256,256]{2,1,0:T(8,128)(2,1)S(1)}, bf16[48,256,256]{2,1,0:T(8,128)(2,1)}, u32[]{:S(2)}) %copy-start) | copy-done | bytes 6291480
  49.2 7.1 %shard_map.86 = bf16[8,400,256]{2,1,0:T(8,128)(2,1)} custom-call(s32[96]{0:T(128)S(1)} %select_reduce_fusion.1.slot_ref, s32[24]{0:T(128)S(1)} %reshape.62.width_ref, bf16[24,128,256]{2,1,0:T(8,128)(2,1)S(1)} %bitcast.12, bf16[48,256,256]{2,1,0:T(8,128)(2,1)S(1)} %copy-done), custom_call_target="tpu_custom_call" | custom-call | tf_op jit(solution)/shard_map/pallas_call | solution.py:183
  58.6 3.8 %all-to-all-start.1 = ((bf16[8,400,256]{2,1,0:T(8,128)(2,1)}), bf16[8,400,256]{2,1,0:T(8,128)(2,1)S(1)}, u32[]{:S(2)}, u32[]{:S(2)}) async-start(bf16[8,400,256]{2,1,0:T(8,128)(2,1)} %shard_map.86), calls=%async_computation.1 | async-start | bytes 3276800 | tf_op jit(solution)/shard_map/all_to_all | solution.py:378
  62.5 5.4 %collective-permute-start.16 = (bf16[24,80,256]{2,1,0:T(8,128)(2,1)}, bf16[24,80,256]{2,1,0:T(8,128)(2,1)}, u32[]{:S(2)}, u32[]{:S(2)}) collective-permute-start(bf16[24,80,256]{2,1,0:T(8,128)(2,1)} %slice.19), channel_id=1, source_target_pairs={{0,24},{24,0},{1,25},{25,1},{2,26},{26,2},{3,27},{27,3},{4,28},{28... | collective-permute-start | bytes 2949128 | tf_op jit(solution)/shard_map/ppermute | solution.py:370
  67.9 1.6 %collective-permute-start.14 = (bf16[24,80,256]{2,1,0:T(8,128)(2,1)}, bf16[24,80,256]{2,1,0:T(8,128)(2,1)}, u32[]{:S(2)}, u32[]{:S(2)}) collective-permute-start(bf16[24,80,256]{2,1,0:T(8,128)(2,1)} %collective-permute-done.5.refs_8_), channel_id=1, source_target_pairs={{8,16},{16,24},{9,17},{17,25},{10,18},{18,26},{11,19},{19,27},{12,... | collective-permute-start | bytes 2949128 | tf_op jit(solution)/shard_map/ppermute | solution.py:366
  69.6 1.3 collective-permute-start.15
  71.6 1.0 copy-done.2
  72.6 1.0 copy-done.4
  73.6 1.0 copy-done.6
  74.6 1.0 copy-done.8
  75.6 1.0 copy-done.10
  76.6 5.2 %shard_map.88 = (bf16[3,144,256]{2,1,0:T(8,128)(2,1)S(1)}, bf16[3,144,256]{2,1,0:T(8,128)(2,1)S(1)}, bf16[3,144,256]{2,1,0:T(8,128)(2,1)S(1)}, bf16[3,144,256]{2...) custom-call(s32[1]{0:T(128)} %bitcast.owner_ref, ...), custom_call_target="tpu_custom_call" | custom-call | tf_op jit(solution)/shard_map/pallas_call | solution.py:119
  81.8 2.2 %collective-permute-start.10 = (bf16[3,144,256]{2,1,0:T(8,128)(2,1)S(1)}, bf16[3,144,256]{2,1,0:T(8,128)(2,1)S(1)}, u32[]{:S(2)}, u32[]{:S(2)}) collective-permute-start(bf16[3,144,256]{2,1,0:T(8,128)(2,1)S(1)} %get-tuple-element.54), channel_id=1, source_target_pairs={{0,4},{1,5},{2,6},{3,7},{4,0},{5,1},{6,2},{7,3},{8,12},{9,13},{10,... | collective-permute-start | bytes 663560 | tf_op jit(solution)/shard_map/ppermute | solution.py:404
  84.0 6.9 %collective-permute-done.16.refs_12_.refs_13_ = bf16[24,80,256]{2,1,0:T(8,128)(2,1)} collective-permute-done((bf16[24,80,256]{2,1,0:T(8,128)(2,1)}, bf16[24,80,256]{2,1,0:T(8,128)(2,1)}, u32[]{:S(2)}, u32[]{:S(2)}) %collective-permute-start.16) | collective-permute-done | bytes 983072 | tf_op jit(solution)/shard_map/ppermute | solution.py:370
  90.9 2.6 %collective-permute-start.12 = (bf16[3,144,256]{2,1,0:T(8,128)(2,1)}, bf16[3,144,256]{2,1,0:T(8,128)(2,1)}, u32[]{:S(2)}, u32[]{:S(2)}) collective-permute-start(bf16[3,144,256]{2,1,0:T(8,128)(2,1)} %get-tuple-element.56), channel_id=1, source_target_pairs={{0,6},{1,7},{2,4},{3,5},{4,2},{5,3},{6,0},{7,1},{8,14},{9,15},{10,... | collective-permute-start | bytes 663560 | tf_op jit(solution)/shard_map/ppermute | solution.py:404
  94.3 2.7 %shard_map.87 = (f32[16,128,256]{2,1,0:T(8,128)}, f32[1,128]{1,0:T(1,128)}, f32[1,128]{1,0:T(1,128)S(1)}) custom-call(s32[8,128]{1,0:T(8,128)S(1)} %copy-done.13, s32[16]{0:T(128)S(1)} %dynamic_slice.8.width_ref, bf16[8,400,256]{2,1,0:T(8,128)(2,1)S(1)} %all-to-all-done.1.back_ref, s32[1,128]{1,0:T(1,128)S(1)} %bitcast.14), custom_call_target="tpu_custom_call" | custom-call | tf_op jit(solution)/shard_map/pallas_call | solution.py:232
  97.6 7.0 %all-to-all-start.2 = ((f32[4,1,128]{2,1,0:T(1,128)}), f32[4,1,128]{2,1,0:T(1,128)S(1)}, u32[]{:S(2)}, u32[]{:S(2)}) async-start(f32[4,1,128]{2,1,0:T(1,128)} %broadcast_in_dim.63), calls=%async_computation.2 | async-start | bytes 4096 | tf_op jit(solution)/shard_map/all_to_all | solution.py:408
  104.6 2.8 %collective-permute-start.7 = (bf16[3,144,256]{2,1,0:T(8,128)(2,1)}, bf16[3,144,256]{2,1,0:T(8,128)(2,1)S(1)}, u32[]{:S(2)}, u32[]{:S(2)}) collective-permute-start(bf16[3,144,256]{2,1,0:T(8,128)(2,1)} %copy-done.17), channel_id=1, source_target_pairs={{0,1},{1,0},{2,3},{3,2},{4,5},{5,4},{6,7},{7,6},{8,9},{9,8},{10,11... | collective-permute-start | bytes 663560 | tf_op jit(solution)/shard_map/ppermute | solution.py:404
  108.9 7.0 %collective-permute-done.8.refs_2_ = bf16[3,144,256]{2,1,0:T(8,128)(2,1)S(1)} collective-permute-done((bf16[3,144,256]{2,1,0:T(8,128)(2,1)}, bf16[3,144,256]{2,1,0:T(8,128)(2,1)S(1)}, u32[]{:S(2)}, u32[]{:S(2)}) %collective-permute-start.8) | collective-permute-done | bytes 221216 | tf_op jit(solution)/shard_map/ppermute | solution.py:404
  115.9 3.0 %collective-permute-done.9.refs_3_ = bf16[3,144,256]{2,1,0:T(8,128)(2,1)S(1)} collective-permute-done((bf16[3,144,256]{2,1,0:T(8,128)(2,1)}, bf16[3,144,256]{2,1,0:T(8,128)(2,1)S(1)}, u32[]{:S(2)}, u32[]{:S(2)}) %collective-permute-start.9) | collective-permute-done | bytes 221216 | tf_op jit(solution)/shard_map/ppermute | solution.py:404
  119.8 10.8 %shard_map.89 = bf16[48,64,256]{2,1,0:T(8,128)(2,1)} custom-call(s32[96]{0:T(128)S(1)} %select_reduce_fusion.1.slot_ref, s32[24]{0:T(128)S(1)} %reshape.62.width_ref, s32[3]{0:T(128)S(1)} %slice_bitcast_fusion.1.which_ref, s32[4]{0:T(128)S(1)} %slice_bitcast_fusion.source_ref, s32[1]{0:T(128)} %bitcast.7.first_ref, s32[1]{0:T(128)} %bitcast.owner_ref, ...), custom_call_target="tpu_custom_call" | custom-call | tf_op jit(solution)/shard_map/pallas_call | solution.py:311
  (78 shorter events, 11.0 us)
Async XLA Ops:
  5.1 18.2 %copy-start.18 = (s32[128]{0:T(128)S(1)}, s32[128]{0:T(128)}, u32[]{:S(2)}) copy-start(s32[128]{0:T(128)} %param.7) | copy-start | bytes 1540
  5.1 26.5 %all-to-all-start = ((bf16[8,384,256]{2,1,0:T(8,128)(2,1)}), bf16[8,384,256]{2,1,0:T(8,128)(2,1)S(1)}, u32[]{:S(2)}, u32[]{:S(2)}) async-start(bf16[8,384,256]{2,1,0:T(8,128)(2,1)} %get-tuple-element.32), calls=%async_computation | async-start | bytes 3145728 | tf_op jit(solution)/shard_map/all_to_all | solution.py:378
  10.5 13.2 %collective-permute-start = (bf16[16,48,256]{2,1,0:T(8,128)(2,1)}, bf16[16,48,256]{2,1,0:T(8,128)(2,1)S(1)}, u32[]{:S(2)}, u32[]{:S(2)}) collective-permute-start(bf16[16,48,256]{2,1,0:T(8,128)(2,1)} %get-tuple-element.33), channel_id=1, source_target_pairs={{0,8},{8,16},{16,24},{1,9},{9,17},{17,25},{2,10},{10,18},{18,26},{... | collective-permute-start | bytes 1179656 | tf_op jit(solution)/shard_map/ppermute | solution.py:360
  14.0 13.3 %collective-permute-start.1 = (bf16[16,48,256]{2,1,0:T(8,128)(2,1)}, bf16[16,48,256]{2,1,0:T(8,128)(2,1)S(1)}, u32[]{:S(2)}, u32[]{:S(2)}) collective-permute-start(bf16[16,48,256]{2,1,0:T(8,128)(2,1)} %get-tuple-element.33), channel_id=1, source_target_pairs={{8,0},{16,8},{24,16},{9,1},{17,9},{25,17},{10,2},{18,10},{26,18},{... | collective-permute-start | bytes 1179656 | tf_op jit(solution)/shard_map/ppermute | solution.py:361
  15.3 41.0 %collective-permute-start.4 = (bf16[16,48,256]{2,1,0:T(8,128)(2,1)}, bf16[16,48,256]{2,1,0:T(8,128)(2,1)S(1)}, u32[]{:S(2)}, u32[]{:S(2)}) collective-permute-start(bf16[16,48,256]{2,1,0:T(8,128)(2,1)} %get-tuple-element.33), channel_id=1, source_target_pairs={{0,24},{24,0},{1,25},{25,1},{2,26},{26,2},{3,27},{27,3},{4,28},{28... | collective-permute-start | bytes 1179656 | tf_op jit(solution)/shard_map/ppermute | solution.py:370
  23.7 32.6 %copy-start.3 = (bf16[16,48,256]{2,1,0:T(8,128)(2,1)}, bf16[16,48,256]{2,1,0:T(8,128)(2,1)S(1)}, u32[]{:S(2)}) copy-start(bf16[16,48,256]{2,1,0:T(8,128)(2,1)S(1)} %collective-permute-done.refs_0_) | copy-start | bytes 1179652
  23.7 33.4 %collective-permute-start.2 = (bf16[16,48,256]{2,1,0:T(8,128)(2,1)S(1)}, bf16[16,48,256]{2,1,0:T(8,128)(2,1)S(1)}, u32[]{:S(2)}, u32[]{:S(2)}) collective-permute-start(bf16[16,48,256]{2,1,0:T(8,128)(2,1)S(1)} %collective-permute-done.refs_0_), channel_id=1, source_target_pairs={{8,16},{16,24},{9,17},{17,25},{10,18},{18,26},{11,19},{19,27},{12,... | collective-permute-start | bytes 1179656 | tf_op jit(solution)/shard_map/ppermute | solution.py:366
  27.3 29.0 %copy-start.5 = (bf16[16,48,256]{2,1,0:T(8,128)(2,1)}, bf16[16,48,256]{2,1,0:T(8,128)(2,1)S(1)}, u32[]{:S(2)}) copy-start(bf16[16,48,256]{2,1,0:T(8,128)(2,1)S(1)} %collective-permute-done.1.refs_1_) | copy-start | bytes 1179652
  27.3 30.5 %collective-permute-start.3 = (bf16[16,48,256]{2,1,0:T(8,128)(2,1)S(1)}, bf16[16,48,256]{2,1,0:T(8,128)(2,1)S(1)}, u32[]{:S(2)}, u32[]{:S(2)}) collective-permute-start(bf16[16,48,256]{2,1,0:T(8,128)(2,1)S(1)} %collective-permute-done.1.refs_1_), channel_id=1, source_target_pairs={{8,0},{16,8},{9,1},{17,9},{10,2},{18,10},{11,3},{19,11},{12,4},{20... | collective-permute-start | bytes 1179656 | tf_op jit(solution)/shard_map/ppermute | solution.py:367
  31.5 13.9 %copy-start.20 = (s32[8]{0:T(128)S(1)}, s32[8]{0:T(128)}, u32[]{:S(2)}) copy-start(s32[8]{0:T(128)} %iota_multiply_fusion) | copy-start | bytes 100
  32.5 35.4 %collective-permute-start.5 = (bf16[24,80,256]{2,1,0:T(8,128)(2,1)}, bf16[24,80,256]{2,1,0:T(8,128)(2,1)}, u32[]{:S(2)}, u32[]{:S(2)}) collective-permute-start(bf16[24,80,256]{2,1,0:T(8,128)(2,1)} %slice.19), channel_id=1, source_target_pairs={{0,8},{8,16},{16,24},{1,9},{9,17},{17,25},{2,10},{10,18},{18,26},{... | collective-permute-start | bytes 2949128 | tf_op jit(solution)/shard_map/ppermute | solution.py:360
  44.1 25.4 %collective-permute-start.6 = (bf16[24,80,256]{2,1,0:T(8,128)(2,1)}, bf16[24,80,256]{2,1,0:T(8,128)(2,1)}, u32[]{:S(2)}, u32[]{:S(2)}) collective-permute-start(bf16[24,80,256]{2,1,0:T(8,128)(2,1)} %slice.19), channel_id=1, source_target_pairs={{8,0},{16,8},{24,16},{9,1},{17,9},{25,17},{10,2},{18,10},{26,18},{... | collective-permute-start | bytes 2949128 | tf_op jit(solution)/shard_map/ppermute | solution.py:361
  46.4 2.8 %copy-start = (bf16[48,256,256]{2,1,0:T(8,128)(2,1)S(1)}, bf16[48,256,256]{2,1,0:T(8,128)(2,1)}, u32[]{:S(2)}) copy-start(bf16[48,256,256]{2,1,0:T(8,128)(2,1)} %mats_ref.1) | copy-start | bytes 18874372
  56.3 15.2 %copy-start.13 = (s32[8,128]{1,0:T(8,128)S(1)}, s32[8,128]{1,0:T(8,128)}, u32[]{:S(2)}) copy-start(s32[8,128]{1,0:T(8,128)} %get-tuple-element.31.table_ref) | copy-start | bytes 12292
  58.6 35.7 %all-to-all-start.1 = ((bf16[8,400,256]{2,1,0:T(8,128)(2,1)}), bf16[8,400,256]{2,1,0:T(8,128)(2,1)S(1)}, u32[]{:S(2)}, u32[]{:S(2)}) async-start(bf16[8,400,256]{2,1,0:T(8,128)(2,1)} %shard_map.86), calls=%async_computation.1 | async-start | bytes 3276800 | tf_op jit(solution)/shard_map/all_to_all | solution.py:378
  62.5 31.8 %copy-start.14 = (s32[128]{0:T(128)S(1)}, s32[128]{0:T(128)}, u32[]{:S(2)}) copy-start(s32[128]{0:T(128)} %param.10) | copy-start | bytes 1540
  62.5 28.4 %collective-permute-start.16 = (bf16[24,80,256]{2,1,0:T(8,128)(2,1)}, bf16[24,80,256]{2,1,0:T(8,128)(2,1)}, u32[]{:S(2)}, u32[]{:S(2)}) collective-permute-start(bf16[24,80,256]{2,1,0:T(8,128)(2,1)} %slice.19), channel_id=1, source_target_pairs={{0,24},{24,0},{1,25},{25,1},{2,26},{26,2},{3,27},{27,3},{4,28},{28... | collective-permute-start | bytes 2949128 | tf_op jit(solution)/shard_map/ppermute | solution.py:370
  67.9 50.9 %collective-permute-start.14 = (bf16[24,80,256]{2,1,0:T(8,128)(2,1)}, bf16[24,80,256]{2,1,0:T(8,128)(2,1)}, u32[]{:S(2)}, u32[]{:S(2)}) collective-permute-start(bf16[24,80,256]{2,1,0:T(8,128)(2,1)} %collective-permute-done.5.refs_8_), channel_id=1, source_target_pairs={{8,16},{16,24},{9,17},{17,25},{10,18},{18,26},{11,19},{19,27},{12,... | collective-permute-start | bytes 2949128 | tf_op jit(solution)/shard_map/ppermute | solution.py:366
  69.6 49.3 %collective-permute-start.15 = (bf16[24,80,256]{2,1,0:T(8,128)(2,1)}, bf16[24,80,256]{2,1,0:T(8,128)(2,1)}, u32[]{:S(2)}, u32[]{:S(2)}) collective-permute-start(bf16[24,80,256]{2,1,0:T(8,128)(2,1)} %collective-permute-done.6.refs_9_), channel_id=1, source_target_pairs={{8,0},{16,8},{9,1},{17,9},{10,2},{18,10},{11,3},{19,11},{12,4},{20... | collective-permute-start | bytes 2949128 | tf_op jit(solution)/shard_map/ppermute | solution.py:367
  71.6 1.0 copy-start.2
  74.6 1.0 copy-start.8
  81.8 11.7 %copy-start.15 = (bf16[3,144,256]{2,1,0:T(8,128)(2,1)}, bf16[3,144,256]{2,1,0:T(8,128)(2,1)S(1)}, u32[]{:S(2)}) copy-start(bf16[3,144,256]{2,1,0:T(8,128)(2,1)S(1)} %get-tuple-element.53) | copy-start | bytes 663556
  81.8 12.4 %copy-start.16 = (bf16[3,144,256]{2,1,0:T(8,128)(2,1)}, bf16[3,144,256]{2,1,0:T(8,128)(2,1)S(1)}, u32[]{:S(2)}) copy-start(bf16[3,144,256]{2,1,0:T(8,128)(2,1)S(1)} %get-tuple-element.52) | copy-start | bytes 663556
  81.8 12.4 %copy-start.17 = (bf16[3,144,256]{2,1,0:T(8,128)(2,1)}, bf16[3,144,256]{2,1,0:T(8,128)(2,1)S(1)}, u32[]{:S(2)}) copy-start(bf16[3,144,256]{2,1,0:T(8,128)(2,1)S(1)} %get-tuple-element.51) | copy-start | bytes 663556
  81.8 11.7 %collective-permute-start.10 = (bf16[3,144,256]{2,1,0:T(8,128)(2,1)S(1)}, bf16[3,144,256]{2,1,0:T(8,128)(2,1)S(1)}, u32[]{:S(2)}, u32[]{:S(2)}) collective-permute-start(bf16[3,144,256]{2,1,0:T(8,128)(2,1)S(1)} %get-tuple-element.54), channel_id=1, source_target_pairs={{0,4},{1,5},{2,6},{3,7},{4,0},{5,1},{6,2},{7,3},{8,12},{9,13},{10,... | collective-permute-start | bytes 663560 | tf_op jit(solution)/shard_map/ppermute | solution.py:404
  84.0 20.5 %collective-permute-start.11 = (bf16[3,144,256]{2,1,0:T(8,128)(2,1)}, bf16[3,144,256]{2,1,0:T(8,128)(2,1)}, u32[]{:S(2)}, u32[]{:S(2)}) collective-permute-start(bf16[3,144,256]{2,1,0:T(8,128)(2,1)} %get-tuple-element.55), channel_id=1, source_target_pairs={{0,5},{1,4},{2,7},{3,6},{4,1},{5,0},{6,3},{7,2},{8,13},{9,12},{10,... | collective-permute-start | bytes 663560 | tf_op jit(solution)/shard_map/ppermute | solution.py:404
  90.9 16.4 %collective-permute-start.12 = (bf16[3,144,256]{2,1,0:T(8,128)(2,1)}, bf16[3,144,256]{2,1,0:T(8,128)(2,1)}, u32[]{:S(2)}, u32[]{:S(2)}) collective-permute-start(bf16[3,144,256]{2,1,0:T(8,128)(2,1)} %get-tuple-element.56), channel_id=1, source_target_pairs={{0,6},{1,7},{2,4},{3,5},{4,2},{5,3},{6,0},{7,1},{8,14},{9,15},{10,... | collective-permute-start | bytes 663560 | tf_op jit(solution)/shard_map/ppermute | solution.py:404
  94.2 13.7 %collective-permute-start.13 = (bf16[3,144,256]{2,1,0:T(8,128)(2,1)}, bf16[3,144,256]{2,1,0:T(8,128)(2,1)}, u32[]{:S(2)}, u32[]{:S(2)}) collective-permute-start(bf16[3,144,256]{2,1,0:T(8,128)(2,1)} %get-tuple-element.57), channel_id=1, source_target_pairs={{0,7},{1,6},{2,5},{3,4},{4,3},{5,2},{6,1},{7,0},{8,15},{9,14},{10,... | collective-permute-start | bytes 663560 | tf_op jit(solution)/shard_map/ppermute | solution.py:404
  97.6 21.2 %all-to-all-start.2 = ((f32[4,1,128]{2,1,0:T(1,128)}), f32[4,1,128]{2,1,0:T(1,128)S(1)}, u32[]{:S(2)}, u32[]{:S(2)}) async-start(f32[4,1,128]{2,1,0:T(1,128)} %broadcast_in_dim.63), calls=%async_computation.2 | async-start | bytes 4096 | tf_op jit(solution)/shard_map/all_to_all | solution.py:408
  104.6 4.3 %collective-permute-start.7 = (bf16[3,144,256]{2,1,0:T(8,128)(2,1)}, bf16[3,144,256]{2,1,0:T(8,128)(2,1)S(1)}, u32[]{:S(2)}, u32[]{:S(2)}) collective-permute-start(bf16[3,144,256]{2,1,0:T(8,128)(2,1)} %copy-done.17), channel_id=1, source_target_pairs={{0,1},{1,0},{2,3},{3,2},{4,5},{5,4},{6,7},{7,6},{8,9},{9,8},{10,11... | collective-permute-start | bytes 663560 | tf_op jit(solution)/shard_map/ppermute | solution.py:404
  107.4 8.5 %collective-permute-start.8 = (bf16[3,144,256]{2,1,0:T(8,128)(2,1)}, bf16[3,144,256]{2,1,0:T(8,128)(2,1)S(1)}, u32[]{:S(2)}, u32[]{:S(2)}) collective-permute-start(bf16[3,144,256]{2,1,0:T(8,128)(2,1)} %copy-done.16), channel_id=1, source_target_pairs={{0,2},{1,3},{2,0},{3,1},{4,6},{5,7},{6,4},{7,5},{8,10},{9,11},{10,... | collective-permute-start | bytes 663560 | tf_op jit(solution)/shard_map/ppermute | solution.py:404
  107.9 10.9 %collective-permute-start.9 = (bf16[3,144,256]{2,1,0:T(8,128)(2,1)}, bf16[3,144,256]{2,1,0:T(8,128)(2,1)S(1)}, u32[]{:S(2)}, u32[]{:S(2)}) collective-permute-start(bf16[3,144,256]{2,1,0:T(8,128)(2,1)} %copy-done.15), channel_id=1, source_target_pairs={{0,3},{1,2},{2,1},{3,0},{4,7},{5,6},{6,5},{7,4},{8,11},{9,10},{10,... | collective-permute-start | bytes 663560 | tf_op jit(solution)/shard_map/ppermute | solution.py:404
  (9 other events, 7.6 us)

commit v4 on v3

--- a/solution.py
+++ b/solution.py
@@ -122,76 +122,80 @@
         in_specs=[SMEM, SMEM, SMEM] + [HBM] * len(sources),
         out_specs=[VMEM] * owners,
         scratch_shapes=[pltpu.SemaphoreType.DMA((len(ways), owners * CAP))],
-        compiler_params=limit(owners * math.prod(shape) * 2),
+        compiler_params=limit(56 << 20),
         cost_estimate=CHEAP,
     )(owner, which, table, *sources)
 
 
-def forward_kernel(group, slot_ref, width_ref, rows_ref, mats_ref, sums_ref, x_ref, u_ref, acc_ref):
-    step = pl.program_id(0)
+def forward_kernel(group, slot_ref, width_ref, rows_ref, mats_ref, sums_ref, x_ref, u_ref, acc_ref, mats, sems):
     slots, samples, width = x_ref.shape
-
-    @pl.when(step == 0)
-    def _():
-        columns = lax.broadcasted_iota(jnp.int32, (samples, width), 1)
-
-        @pl.loop(0, slots)
-        def _(j):
-            x_ref[j] = jnp.where(columns < width_ref[j], rows_ref[j], jnp.zeros_like(rows_ref[j]))
-            u_ref[j] = jnp.zeros((samples, width), F32)
-
-        acc_ref[...] = jnp.zeros_like(acc_ref)
-
-    acc = jnp.zeros((samples, width), F32)
-    for k in range(group):
-        p = step * group + k
-        a, b = slot_ref[2 * p], slot_ref[2 * p + 1]
-        left, right, mat = x_ref[a], x_ref[b], mats_ref[k]
-        projected = jnp.dot(left, mat, preferred_element_type=F32)
-        back = lax.dot_general(right, mat, (((1,), (1,)), ((), ())), preferred_element_type=F32)
-        acc += projected * right.astype(F32)
-        u_ref[b] += projected
-        u_ref[a] += back
-    acc_ref[...] += acc
-
-    @pl.when(step == pl.num_programs(0) - 1)
-    def _():
-        total = acc_ref[:, 0:128]
-        for at in range(128, width, 128):
-            total = total + acc_ref[:, at : at + 128]
-        part = jnp.sum(total.T, axis=0, keepdims=True)
-        note = jnp.zeros((NOTE, width), F32)
-        for row in range(3):
-            piece = part.astype(BF16).astype(F32)
-            part = part - piece
-            at = lax.broadcasted_iota(jnp.int32, (NOTE, width), 0) == row
-            note = jnp.where(at, jnp.concatenate([piece] * (width // samples), axis=1), note)
-        lines = CAP * samples
-
-        @pl.loop(0, slots // CAP)
-        def _(o):
-            for c in range(CAP):
-                sums_ref[o, c * samples : (c + 1) * samples, :] = u_ref[o * CAP + c].astype(BF16)
-            sums_ref[o, lines : lines + NOTE, :] = note.astype(BF16)
+    steps = mats.shape[0] // group
+
+    def load(i):
+        part = pl.ds(i * group, group)
+        return pltpu.make_async_copy(mats_ref.at[part], mats.at[part], sems.at[i])
+
+    for i in range(steps):
+        load(i).start()
+    columns = lax.broadcasted_iota(jnp.int32, (samples, width), 1)
+
+    @pl.loop(0, slots, unroll=4)
+    def _(j):
+        x_ref[j] = jnp.where(columns < width_ref[j], rows_ref[j], jnp.zeros_like(rows_ref[j]))
+        u_ref[j] = jnp.zeros((samples, width), F32)
+
+    acc_ref[...] = jnp.zeros_like(acc_ref)
+
+    @pl.loop(0, steps)
+    def _(i):
+        load(i).wait()
+        acc = jnp.zeros((samples, width), F32)
+        for k in range(group):
+            p = i * group + k
+            a, b = slot_ref[2 * p], slot_ref[2 * p + 1]
+            left, right, mat = x_ref[a], x_ref[b], mats[p]
+            projected = jnp.dot(left, mat, preferred_element_type=F32)
+            back = lax.dot_general(right, mat, (((1,), (1,)), ((), ())), preferred_element_type=F32)
+            acc += projected * right.astype(F32)
+            u_ref[b] += projected
+            u_ref[a] += back
+        acc_ref[...] += acc
+
+    total = acc_ref[:, 0:128]
+    for at in range(128, width, 128):
+        total = total + acc_ref[:, at : at + 128]
+    part = jnp.sum(total.T, axis=0, keepdims=True)
+    note = jnp.zeros((NOTE, width), F32)
+    for row in range(3):
+        piece = part.astype(BF16).astype(F32)
+        part = part - piece
+        at = lax.broadcasted_iota(jnp.int32, (NOTE, width), 0) == row
+        note = jnp.where(at, jnp.concatenate([piece] * (width // samples), axis=1), note)
+    lines = CAP * samples
+
+    @pl.loop(0, slots // CAP)
+    def _(o):
+        for c in range(CAP):
+            sums_ref[o, c * samples : (c + 1) * samples, :] = u_ref[o * CAP + c].astype(BF16)
+        sums_ref[o, lines : lines + NOTE, :] = note.astype(BF16)
 
 
 def forward(slot_index, slot_width, rows, mats, group=8):
     slots, samples, width = rows.shape
-    pairs = mats.shape[0]
-    whole = lambda *shape: pl.BlockSpec(shape, lambda i: (0,) * len(shape))
     sums = (slots // CAP, CAP * samples + NOTE, width)
     return pl.pallas_call(
         functools.partial(forward_kernel, group),
-        grid=(pairs // group,),
         out_shape=jax.ShapeDtypeStruct(sums, BF16),
-        in_specs=[SMEM, SMEM, whole(*rows.shape), pl.BlockSpec((group, width, width), lambda i: (i, 0, 0))],
-        out_specs=whole(*sums),
+        in_specs=[SMEM, SMEM, VMEM, HBM],
+        out_specs=VMEM,
         scratch_shapes=[
             pltpu.VMEM(rows.shape, BF16),
             pltpu.VMEM(rows.shape, F32),
             pltpu.VMEM((samples, width), F32),
+            pltpu.VMEM(mats.shape, BF16),
+            pltpu.SemaphoreType.DMA((mats.shape[0] // group,)),
         ],
-        compiler_params=limit(14 * math.prod(rows.shape) + 4 * group * width * width),
+        compiler_params=limit(52 << 20),
         cost_estimate=CHEAP,
     )(slot_index, slot_width, rows, mats)
 
@@ -245,7 +249,8 @@
 
 def mat_grad_kernel(ways, chunk, owners, slot_ref, width_ref, which_ref, source_ref, first_ref, owner_ref, grads_ref, own_ref, *refs):
     raws = refs[:owners]
-    *links, out_ref, x_ref, t_ref, acc_ref, sems = refs[owners:]
+    *links, out_ref, x_ref, t_ref, acc_ref, done_ref, sems, done_sems = refs[owners:]
+    group = done_ref.shape[0] // done_sems.shape[0]
     count = len(ways) + 1
     width = x_ref.shape[2]
     slots, samples, _ = own_ref.shape
@@ -259,46 +264,66 @@
     def place(k, low, size):
         return x_ref.at[:, pl.ds(k * samples + low, size), :]
 
+    def store(i):
+        part = pl.ds(i * group, group)
+        return pltpu.make_async_copy(done_ref.at[part], out_ref.at[part], done_sems.at[i])
+
     for start in range(0, count, chunk):
-        waits = []
+        waits = [[] for _ in range(chunk)]
         for k in range(chunk):
             if start + k == 0:
-                waits.append(pltpu.make_async_copy(own_ref, place(k, 0, samples), sems.at[k, 0]))
-                waits[-1].start()
+                waits[k].append(pltpu.make_async_copy(own_ref, place(k, 0, samples), sems.at[k, 0]))
+                waits[k][-1].start()
                 continue
             r = start + k - 1
             for d in range(owners):
                 raw = raws[d].at[:, pl.ds(r * raw_lines, raw_lines), :]
                 spot = x_ref.at[pl.ds((owner_ref[0] ^ d) * CAP, CAP), pl.ds(k * samples, raw_lines), :]
-                waits.append(pltpu.make_async_copy(raw, spot, sems.at[k, 2 + d]))
-                waits[-1].start()
+                waits[k].append(pltpu.make_async_copy(raw, spot, sems.at[k, 2 + d]))
+                waits[k][-1].start()
             for at, link in enumerate(ways[r]):
 
                 @pl.when(which_ref[r] == at)
                 def _(k=k, link=link):
                     pltpu.make_async_copy(links[link], place(k, raw_lines, kept_lines), sems.at[k, 1]).start()
 
-            waits.append(pltpu.make_async_copy(links[0], place(k, raw_lines, kept_lines), sems.at[k, 1]))
-        for copy in waits:
-            copy.wait()
-        grad = jnp.concatenate([grads_ref[source_ref[start + k]] for k in range(chunk)], axis=1)
-
-        @pl.loop(0, slots, unroll=4)
-        def _(j, grad=grad):
-            turned = lax.dot_general(pick, x_ref[j], (((1,), (1,)), ((), ())), preferred_element_type=F32)
-            t_ref[j] = (turned * grad).astype(BF16)
-
-        @pl.loop(0, pairs, unroll=4)
-        def _(p, start=start):
+            waits[k].append(pltpu.make_async_copy(links[0], place(k, raw_lines, kept_lines), sems.at[k, 1]))
+        for k in range(chunk):
+            for copy in waits[k]:
+                copy.wait()
+            grad = grads_ref[source_ref[start + k]]
+
+            @pl.loop(0, slots, unroll=12)
+            def _(j, k=k, grad=grad):
+                x = x_ref[j, k * samples : (k + 1) * samples, :]
+                turned = lax.dot_general(pick, x, (((1,), (1,)), ((), ())), preferred_element_type=F32)
+                t_ref[j, :, k * samples : (k + 1) * samples] = (turned * grad).astype(BF16)
+
+        def term_of(p):
             a, b = slot_ref[2 * p], slot_ref[2 * p + 1]
             term = jnp.dot(t_ref[a], x_ref[b], preferred_element_type=F32)
-            if start > 0:
-                term += acc_ref[p]
-            if start + chunk < count:
-                acc_ref[p] = term
-            else:
+            return term if start == 0 else term + acc_ref[p]
+
+        if start + chunk < count:
+
+            @pl.loop(0, pairs, unroll=8)
+            def _(p, term_of=term_of):
+                acc_ref[p] = term_of(p)
+
+            continue
+
+        @pl.loop(0, pairs // group)
+        def _(i, term_of=term_of):
+            for k in range(group):
+                p = i * group + k
+                a, b = slot_ref[2 * p], slot_ref[2 * p + 1]
                 kept = (own_row < width_ref[a]) & (columns < width_ref[b])
-                out_ref[p] = jnp.where(kept, term, 0.0).astype(BF16)
+                done_ref[p] = jnp.where(kept, term_of(p), 0.0).astype(BF16)
+            store(i).start()
+
+        @pl.loop(0, pairs // group)
+        def _(i):
+            store(i).wait()
 
 
 def mat_grad_of(ways, slot_index, slot_width, which, sources, first, owner, grads, own, raw, links, rows):
@@ -312,14 +337,16 @@
         functools.partial(mat_grad_kernel, ways, chunk, len(raw)),
         out_shape=jax.ShapeDtypeStruct((pairs, rows, width), BF16),
         in_specs=[SMEM] * 6 + [VMEM] + [HBM] * (1 + len(raw) + len(links)),
-        out_specs=VMEM,
+        out_specs=HBM,
         scratch_shapes=[
             pltpu.VMEM((slots, chunk * samples, width), BF16),
             pltpu.VMEM((slots, rows, chunk * samples), BF16),
             pltpu.VMEM((pairs, rows, width), F32),
+            pltpu.VMEM((pairs, rows, width), BF16),
             pltpu.SemaphoreType.DMA((chunk, 2 + len(raw))),
+            pltpu.SemaphoreType.DMA((pairs // 8,)),
         ],
-        compiler_params=limit(size),
+        compiler_params=limit(56 << 20),
         cost_estimate=CHEAP,
     )(slot_index, slot_width, which, sources, first, owner, grads, own, *raw, *links)
 

time: 132 us -> 123 us (0.932)
  local copies, waits for them, and re-layouts: 15.5 us -> 6.97 us
  waiting for transfers between devices: 22.2 us -> 26.3 us
  starting transfers between devices: 59.8 us -> 56.9 us
    unnamed x42 -> x34, local copies, waits for them, and re-layouts: 11.7 us -> 1.46 us
    ppermute x2, waiting for transfers between devices: 6.91 us -> 12.3 us  [chain(): found += [lax.ppermute(own, 'dp', ends + [(j, i) for i, j in ends])] * 2]
    all_to_all x1, starting transfers between devices: 6.96 us -> 4.85 us  [shards(): lax.all_to_all(jnp.broadcast_to(grad, (groups, 1, samples)), 'dp', split_...]
    pallas_call x1, Pallas kernels: 7.1 us -> 8.69 us  [forward(): pl.pallas_call(functools.partial(forward_kernel, group), out_shape=jax.Sh...]
    pallas_call x1, Pallas kernels: 10.8 us -> 9.26 us  [mat_grad_of(): pl.pallas_call(functools.partial(mat_grad_kernel, ways, chunk, len(raw)),...]
  transfers between devices with their start and end apart: 20 -> 20, of which waited for: 6 -> 6; matrix products, arithmetic and copies ran while one was open for 4% -> 6% of each run, Pallas kernels for 12% -> 13%
where the time goes in v4:
time: 123 us; the launch traced here: 122 us
  starting transfers between devices  56.9 us (46%)
  Pallas kernels  29.4 us (24%)
  waiting for transfers between devices  26.3 us (21%)
  local copies, waits for them, and re-layouts  6.97 us (6%)
  other arithmetic  1.29 us (1%)
    ppermute x2, starting transfers between devices, chain(): up = lax.ppermute(own, 'dp', [(i, i + 1) for i in range(groups - 1)])  15.2 us
    ppermute x2, starting transfers between devices, chain(): found += [lax.ppermute(own, 'dp', ends + [(j, i) for i, j in ends])] * 2  12.8 us
    ppermute x2, waiting for transfers between devices, chain(): found += [lax.ppermute(own, 'dp', ends + [(j, i) for i, j in ends])] * 2  12.3 us
    pallas_call x1, Pallas kernels, mat_grad_of(): pl.pallas_call(functools.partial(mat_grad_kernel, ways, chunk, len(raw)),...  9.26 us
    all_to_all x2, starting transfers between devices, exchange(): lax.all_to_all(lines, 'pair', split_axis=0, concat_axis=0, tiled=True)  8.98 us
    ppermute x7, waiting for transfers between devices, shards(): lax.ppermute(x, 'pair', [(i, i ^ k) for i in range(owners)])  8.7 us
    pallas_call x1, Pallas kernels, forward(): pl.pallas_call(functools.partial(forward_kernel, group), out_shape=jax.Sh...  8.69 us
    ppermute x7, starting transfers between devices, shards(): lax.ppermute(x, 'pair', [(i, i ^ k) for i in range(owners)])  7.76 us
  transfers between devices with their start and end apart: 20, of which 6 were waited for; matrix products, arithmetic and copies ran while one was open for 6% of the time, Pallas kernels for 13%

profile of v4, /device:TPU:0, one launch (start us, length us, event | category | flops | bytes accessed | tf_op | source)
XLA Modules:
  0.0 121.9 jit_solution(10839202512346127626)
XLA Ops:
  0.6 4.5 %shard_map.85 = (bf16[8,384,256]{2,1,0:T(8,128)(2,1)}, bf16[16,48,256]{2,1,0:T(8,128)(2,1)}, s32[8,128]{1,0:T(8,128)}) custom-call(s32[1]{0:T(128)} %bitcast.owner_ref, s32[2,384]{1,0:T(2,128)} %bitcast.16, bf16[16,128,256]{2,1,0:T(8,128)(2,1)} %rows_ref.1), custom_call_target="tpu_custom_call" | custom-call | tf_op jit(solution)/shard_map/pallas_call | solution.py:74
  5.2 5.1 %all-to-all-start = ((bf16[8,384,256]{2,1,0:T(8,128)(2,1)}), bf16[8,384,256]{2,1,0:T(8,128)(2,1)S(1)}, u32[]{:S(2)}, u32[]{:S(2)}) async-start(bf16[8,384,256]{2,1,0:T(8,128)(2,1)} %get-tuple-element.32), calls=%async_computation | async-start | bytes 3145728 | tf_op jit(solution)/shard_map/all_to_all | solution.py:405
  10.3 3.5 %collective-permute-start = (bf16[16,48,256]{2,1,0:T(8,128)(2,1)}, bf16[16,48,256]{2,1,0:T(8,128)(2,1)S(1)}, u32[]{:S(2)}, u32[]{:S(2)}) collective-permute-start(bf16[16,48,256]{2,1,0:T(8,128)(2,1)} %get-tuple-element.33), channel_id=1, source_target_pairs={{0,8},{8,16},{16,24},{1,9},{9,17},{17,25},{2,10},{10,18},{18,26},{... | collective-permute-start | bytes 1179656 | tf_op jit(solution)/shard_map/ppermute | solution.py:387
  13.8 1.3 %collective-permute-start.1 = (bf16[16,48,256]{2,1,0:T(8,128)(2,1)}, bf16[16,48,256]{2,1,0:T(8,128)(2,1)S(1)}, u32[]{:S(2)}, u32[]{:S(2)}) collective-permute-start(bf16[16,48,256]{2,1,0:T(8,128)(2,1)} %get-tuple-element.33), channel_id=1, source_target_pairs={{8,0},{16,8},{24,16},{9,1},{17,9},{25,17},{10,2},{18,10},{26,18},{... | collective-permute-start | bytes 1179656 | tf_op jit(solution)/shard_map/ppermute | solution.py:388
  15.1 6.6 %collective-permute-start.4 = (bf16[16,48,256]{2,1,0:T(8,128)(2,1)}, bf16[16,48,256]{2,1,0:T(8,128)(2,1)S(1)}, u32[]{:S(2)}, u32[]{:S(2)}) collective-permute-start(bf16[16,48,256]{2,1,0:T(8,128)(2,1)} %get-tuple-element.33), channel_id=1, source_target_pairs={{0,24},{24,0},{1,25},{25,1},{2,26},{26,2},{3,27},{27,3},{4,28},{28... | collective-permute-start | bytes 1179656 | tf_op jit(solution)/shard_map/ppermute | solution.py:397
  21.7 0.8 constant_dynamic-slice_fusion.1
  23.5 0.7 collective-permute-start.2
  24.2 3.0 %collective-permute-done.1.refs_1_ = bf16[16,48,256]{2,1,0:T(8,128)(2,1)S(1)} collective-permute-done((bf16[16,48,256]{2,1,0:T(8,128)(2,1)}, bf16[16,48,256]{2,1,0:T(8,128)(2,1)S(1)}, u32[]{:S(2)}, u32[]{:S(2)}) %collective-permute-start.1) | collective-permute-done | bytes 393248 | tf_op jit(solution)/shard_map/ppermute | solution.py:388
  27.2 1.3 %collective-permute-start.3 = (bf16[16,48,256]{2,1,0:T(8,128)(2,1)S(1)}, bf16[16,48,256]{2,1,0:T(8,128)(2,1)}, u32[]{:S(2)}, u32[]{:S(2)}) collective-permute-start(bf16[16,48,256]{2,1,0:T(8,128)(2,1)S(1)} %collective-permute-done.1.refs_1_), channel_id=1, source_target_pairs={{8,0},{16,8},{9,1},{17,9},{10,2},{18,10},{11,3},{19,11},{12,4},{20... | collective-permute-start | bytes 1179656 | tf_op jit(solution)/shard_map/ppermute | solution.py:394
  29.2 2.1 %all-to-all-done = bf16[8,384,256]{2,1,0:T(8,128)(2,1)S(1)} async-done(((bf16[8,384,256]{2,1,0:T(8,128)(2,1)}), bf16[8,384,256]{2,1,0:T(8,128)(2,1)S(1)}, u32[]{:S(2)}, u32[]{:S(2)}) %all-to-all-start) | async-done | bytes 1572896 | tf_op jit(solution)/shard_map/all_to_all | solution.py:405
  31.4 1.1 slice.19
  32.4 11.7 %collective-permute-start.5 = (bf16[24,80,256]{2,1,0:T(8,128)(2,1)}, bf16[24,80,256]{2,1,0:T(8,128)(2,1)}, u32[]{:S(2)}, u32[]{:S(2)}) collective-permute-start(bf16[24,80,256]{2,1,0:T(8,128)(2,1)} %slice.19), channel_id=1, source_target_pairs={{0,8},{8,16},{16,24},{1,9},{9,17},{17,25},{2,10},{10,18},{18,26},{... | collective-permute-start | bytes 2949128 | tf_op jit(solution)/shard_map/ppermute | solution.py:387
  44.1 1.3 %collective-permute-start.6 = (bf16[24,80,256]{2,1,0:T(8,128)(2,1)}, bf16[24,80,256]{2,1,0:T(8,128)(2,1)}, u32[]{:S(2)}, u32[]{:S(2)}) collective-permute-start(bf16[24,80,256]{2,1,0:T(8,128)(2,1)} %slice.19), channel_id=1, source_target_pairs={{8,0},{16,8},{24,16},{9,1},{17,9},{25,17},{10,2},{18,10},{26,18},{... | collective-permute-start | bytes 2949128 | tf_op jit(solution)/shard_map/ppermute | solution.py:388
  45.6 0.7 select_reduce_fusion.1.slot_ref
  46.3 8.7 %shard_map.86 = bf16[8,400,256]{2,1,0:T(8,128)(2,1)} custom-call(s32[96]{0:T(128)} %select_reduce_fusion.1.slot_ref, s32[24]{0:T(128)} %reshape.62.width_ref, bf16[24,128,256]{2,1,0:T(8,128)(2,1)} %bitcast.14, bf16[48,256,256]{2,1,0:T(8,128)(2,1)} %mats_ref.1), custom_call_target="tpu_custom_call" | custom-call | tf_op jit(solution)/shard_map/pallas_call | solution.py:186
  55.1 0.8 copy-done.7
  55.8 3.8 %all-to-all-start.1 = ((bf16[8,400,256]{2,1,0:T(8,128)(2,1)}), bf16[8,400,256]{2,1,0:T(8,128)(2,1)S(1)}, u32[]{:S(2)}, u32[]{:S(2)}) async-start(bf16[8,400,256]{2,1,0:T(8,128)(2,1)} %shard_map.86), calls=%async_computation.1 | async-start | bytes 3276800 | tf_op jit(solution)/shard_map/all_to_all | solution.py:405
  59.7 6.2 %collective-permute-start.16 = (bf16[24,80,256]{2,1,0:T(8,128)(2,1)}, bf16[24,80,256]{2,1,0:T(8,128)(2,1)S(1)}, u32[]{:S(2)}, u32[]{:S(2)}) collective-permute-start(bf16[24,80,256]{2,1,0:T(8,128)(2,1)} %slice.19), channel_id=1, source_target_pairs={{0,24},{24,0},{1,25},{25,1},{2,26},{26,2},{3,27},{27,3},{4,28},{28... | collective-permute-start | bytes 2949128 | tf_op jit(solution)/shard_map/ppermute | solution.py:397
  65.9 1.6 %collective-permute-start.14 = (bf16[24,80,256]{2,1,0:T(8,128)(2,1)}, bf16[24,80,256]{2,1,0:T(8,128)(2,1)}, u32[]{:S(2)}, u32[]{:S(2)}) collective-permute-start(bf16[24,80,256]{2,1,0:T(8,128)(2,1)} %collective-permute-done.5.refs_8_), channel_id=1, source_target_pairs={{8,16},{16,24},{9,17},{17,25},{10,18},{18,26},{11,19},{19,27},{12,... | collective-permute-start | bytes 2949128 | tf_op jit(solution)/shard_map/ppermute | solution.py:393
  67.5 1.3 %collective-permute-start.15 = (bf16[24,80,256]{2,1,0:T(8,128)(2,1)}, bf16[24,80,256]{2,1,0:T(8,128)(2,1)}, u32[]{:S(2)}, u32[]{:S(2)}) collective-permute-start(bf16[24,80,256]{2,1,0:T(8,128)(2,1)} %collective-permute-done.6.refs_9_), channel_id=1, source_target_pairs={{8,0},{16,8},{9,1},{17,9},{10,2},{18,10},{11,3},{19,11},{12,4},{20... | collective-permute-start | bytes 2949128 | tf_op jit(solution)/shard_map/ppermute | solution.py:394
  68.8 0.7 constant_dynamic-slice_fusion
  70.0 4.2 %shard_map.88 = (bf16[3,144,256]{2,1,0:T(8,128)(2,1)}, bf16[3,144,256]{2,1,0:T(8,128)(2,1)}, bf16[3,144,256]{2,1,0:T(8,128)(2,1)}, bf16[3,144,256]{2,1,0:T(8,128...) custom-call(s32[1]{0:T(128)} %bitcast.owner_ref, ...), custom_call_target="tpu_custom_call" | custom-call | tf_op jit(solution)/shard_map/pallas_call | solution.py:119
  74.3 2.2 %collective-permute-start.10 = (bf16[3,144,256]{2,1,0:T(8,128)(2,1)}, bf16[3,144,256]{2,1,0:T(8,128)(2,1)S(1)}, u32[]{:S(2)}, u32[]{:S(2)}) collective-permute-start(bf16[3,144,256]{2,1,0:T(8,128)(2,1)} %get-tuple-element.54), channel_id=1, source_target_pairs={{0,4},{1,5},{2,6},{3,7},{4,0},{5,1},{6,2},{7,3},{8,12},{9,13},{10,... | collective-permute-start | bytes 663560 | tf_op jit(solution)/shard_map/ppermute | solution.py:431
  76.5 12.3 %collective-permute-done.16.refs_12_.refs_13_ = bf16[24,80,256]{2,1,0:T(8,128)(2,1)S(1)} collective-permute-done((bf16[24,80,256]{2,1,0:T(8,128)(2,1)}, bf16[24,80,256]{2,1,0:T(8,128)(2,1)S(1)}, u32[]{:S(2)}, u32[]{:S(2)}) %collective-permute-start.16) | collective-permute-done | bytes 983072 | tf_op jit(solution)/shard_map/ppermute | solution.py:397
  88.8 2.6 %collective-permute-start.12 = (bf16[3,144,256]{2,1,0:T(8,128)(2,1)}, bf16[3,144,256]{2,1,0:T(8,128)(2,1)S(1)}, u32[]{:S(2)}, u32[]{:S(2)}) collective-permute-start(bf16[3,144,256]{2,1,0:T(8,128)(2,1)} %get-tuple-element.56), channel_id=1, source_target_pairs={{0,6},{1,7},{2,4},{3,5},{4,2},{5,3},{6,0},{7,1},{8,14},{9,15},{10,... | collective-permute-start | bytes 663560 | tf_op jit(solution)/shard_map/ppermute | solution.py:431
  91.5 2.7 %shard_map.87 = (f32[16,128,256]{2,1,0:T(8,128)}, f32[1,128]{1,0:T(1,128)}, f32[1,128]{1,0:T(1,128)S(1)}) custom-call(s32[8,128]{1,0:T(8,128)S(1)} %copy-done, s32[16]{0:T(128)S(1)} %dynamic_slice.8.width_ref, bf16[8,400,256]{2,1,0:T(8,128)(2,1)S(1)} %all-to-all-done.1.back_ref, s32[1,128]{1,0:T(1,128)S(1)} %bitcast.11), custom_call_target="tpu_custom_call" | custom-call | tf_op jit(solution)/shard_map/pallas_call | solution.py:236
  94.8 4.8 %all-to-all-start.2 = ((f32[4,1,128]{2,1,0:T(1,128)}), f32[4,1,128]{2,1,0:T(1,128)S(1)}, u32[]{:S(2)}, u32[]{:S(2)}) async-start(f32[4,1,128]{2,1,0:T(1,128)} %broadcast_in_dim.63), calls=%async_computation.2 | async-start | bytes 4096 | tf_op jit(solution)/shard_map/all_to_all | solution.py:435
  99.9 1.7 %collective-permute-start.8 = (bf16[3,144,256]{2,1,0:T(8,128)(2,1)}, bf16[3,144,256]{2,1,0:T(8,128)(2,1)S(1)}, u32[]{:S(2)}, u32[]{:S(2)}) collective-permute-start(bf16[3,144,256]{2,1,0:T(8,128)(2,1)} %get-tuple-element.52), channel_id=1, source_target_pairs={{0,2},{1,3},{2,0},{3,1},{4,6},{5,7},{6,4},{7,5},{8,10},{9,11},{10,... | collective-permute-start | bytes 663560 | tf_op jit(solution)/shard_map/ppermute | solution.py:431
  101.6 1.0 collective-permute-start.9
  103.2 5.1 %collective-permute-done.8.refs_2_ = bf16[3,144,256]{2,1,0:T(8,128)(2,1)S(1)} collective-permute-done((bf16[3,144,256]{2,1,0:T(8,128)(2,1)}, bf16[3,144,256]{2,1,0:T(8,128)(2,1)S(1)}, u32[]{:S(2)}, u32[]{:S(2)}) %collective-permute-start.8) | collective-permute-done | bytes 221216 | tf_op jit(solution)/shard_map/ppermute | solution.py:431
  108.3 3.6 %collective-permute-done.9.refs_3_ = bf16[3,144,256]{2,1,0:T(8,128)(2,1)S(1)} collective-permute-done((bf16[3,144,256]{2,1,0:T(8,128)(2,1)}, bf16[3,144,256]{2,1,0:T(8,128)(2,1)S(1)}, u32[]{:S(2)}, u32[]{:S(2)}) %collective-permute-start.9) | collective-permute-done | bytes 221216 | tf_op jit(solution)/shard_map/ppermute | solution.py:431
  112.6 9.3 %shard_map.89 = bf16[48,64,256]{2,1,0:T(8,128)(2,1)} custom-call(s32[96]{0:T(128)} %select_reduce_fusion.1.slot_ref, s32[24]{0:T(128)} %reshape.62.width_ref, s32[3]{0:T(128)} %slice_bitcast_fusion.1.which_ref, s32[4]{0:T(128)} %slice_bitcast_fusion.source_ref, s32[1]{0:T(128)} %bitcast.7.first_ref, s32[1]{0:T(128)} %bitcast.owner_ref, ...), custom_call_target="tpu_custom_call" | custom-call | tf_op jit(solution)/shard_map/pallas_call | solution.py:336
  (70 shorter events, 4.7 us)
Async XLA Ops:
  5.2 17.9 %copy-start.16 = (s32[128]{0:T(128)S(1)}, s32[128]{0:T(128)}, u32[]{:S(2)}) copy-start(s32[128]{0:T(128)} %param.7) | copy-start | bytes 1540
  5.2 26.2 %all-to-all-start = ((bf16[8,384,256]{2,1,0:T(8,128)(2,1)}), bf16[8,384,256]{2,1,0:T(8,128)(2,1)S(1)}, u32[]{:S(2)}, u32[]{:S(2)}) async-start(bf16[8,384,256]{2,1,0:T(8,128)(2,1)} %get-tuple-element.32), calls=%async_computation | async-start | bytes 3145728 | tf_op jit(solution)/shard_map/all_to_all | solution.py:405
  10.3 13.2 %collective-permute-start = (bf16[16,48,256]{2,1,0:T(8,128)(2,1)}, bf16[16,48,256]{2,1,0:T(8,128)(2,1)S(1)}, u32[]{:S(2)}, u32[]{:S(2)}) collective-permute-start(bf16[16,48,256]{2,1,0:T(8,128)(2,1)} %get-tuple-element.33), channel_id=1, source_target_pairs={{0,8},{8,16},{16,24},{1,9},{9,17},{17,25},{2,10},{10,18},{18,26},{... | collective-permute-start | bytes 1179656 | tf_op jit(solution)/shard_map/ppermute | solution.py:387
  13.8 13.3 %collective-permute-start.1 = (bf16[16,48,256]{2,1,0:T(8,128)(2,1)}, bf16[16,48,256]{2,1,0:T(8,128)(2,1)S(1)}, u32[]{:S(2)}, u32[]{:S(2)}) collective-permute-start(bf16[16,48,256]{2,1,0:T(8,128)(2,1)} %get-tuple-element.33), channel_id=1, source_target_pairs={{8,0},{16,8},{24,16},{9,1},{17,9},{25,17},{10,2},{18,10},{26,18},{... | collective-permute-start | bytes 1179656 | tf_op jit(solution)/shard_map/ppermute | solution.py:388
  15.1 39.9 %collective-permute-start.4 = (bf16[16,48,256]{2,1,0:T(8,128)(2,1)}, bf16[16,48,256]{2,1,0:T(8,128)(2,1)S(1)}, u32[]{:S(2)}, u32[]{:S(2)}) collective-permute-start(bf16[16,48,256]{2,1,0:T(8,128)(2,1)} %get-tuple-element.33), channel_id=1, source_target_pairs={{0,24},{24,0},{1,25},{25,1},{2,26},{26,2},{3,27},{27,3},{4,28},{28... | collective-permute-start | bytes 1179656 | tf_op jit(solution)/shard_map/ppermute | solution.py:397
  23.5 31.5 %copy-start.5 = (bf16[16,48,256]{2,1,0:T(8,128)(2,1)}, bf16[16,48,256]{2,1,0:T(8,128)(2,1)S(1)}, u32[]{:S(2)}) copy-start(bf16[16,48,256]{2,1,0:T(8,128)(2,1)S(1)} %collective-permute-done.refs_0_) | copy-start | bytes 1179652
  23.5 31.5 %collective-permute-start.2 = (bf16[16,48,256]{2,1,0:T(8,128)(2,1)S(1)}, bf16[16,48,256]{2,1,0:T(8,128)(2,1)S(1)}, u32[]{:S(2)}, u32[]{:S(2)}) collective-permute-start(bf16[16,48,256]{2,1,0:T(8,128)(2,1)S(1)} %collective-permute-done.refs_0_), channel_id=1, source_target_pairs={{8,16},{16,24},{9,17},{17,25},{10,18},{18,26},{11,19},{19,27},{12,... | collective-permute-start | bytes 1179656 | tf_op jit(solution)/shard_map/ppermute | solution.py:393
  27.2 27.8 %copy-start.6 = (bf16[16,48,256]{2,1,0:T(8,128)(2,1)}, bf16[16,48,256]{2,1,0:T(8,128)(2,1)S(1)}, u32[]{:S(2)}) copy-start(bf16[16,48,256]{2,1,0:T(8,128)(2,1)S(1)} %collective-permute-done.1.refs_1_) | copy-start | bytes 1179652
  27.2 27.9 %collective-permute-start.3 = (bf16[16,48,256]{2,1,0:T(8,128)(2,1)S(1)}, bf16[16,48,256]{2,1,0:T(8,128)(2,1)}, u32[]{:S(2)}, u32[]{:S(2)}) collective-permute-start(bf16[16,48,256]{2,1,0:T(8,128)(2,1)S(1)} %collective-permute-done.1.refs_1_), channel_id=1, source_target_pairs={{8,0},{16,8},{9,1},{17,9},{10,2},{18,10},{11,3},{19,11},{12,4},{20... | collective-permute-start | bytes 1179656 | tf_op jit(solution)/shard_map/ppermute | solution.py:394
  31.4 14.9 %copy-start.2 = (bf16[8,384,256]{2,1,0:T(8,128)(2,1)}, bf16[8,384,256]{2,1,0:T(8,128)(2,1)S(1)}, u32[]{:S(2)}) copy-start(bf16[8,384,256]{2,1,0:T(8,128)(2,1)S(1)} %all-to-all-done) | copy-start | bytes 4718596
  32.4 33.5 %collective-permute-start.5 = (bf16[24,80,256]{2,1,0:T(8,128)(2,1)}, bf16[24,80,256]{2,1,0:T(8,128)(2,1)}, u32[]{:S(2)}, u32[]{:S(2)}) collective-permute-start(bf16[24,80,256]{2,1,0:T(8,128)(2,1)} %slice.19), channel_id=1, source_target_pairs={{0,8},{8,16},{16,24},{1,9},{9,17},{17,25},{2,10},{10,18},{18,26},{... | collective-permute-start | bytes 2949128 | tf_op jit(solution)/shard_map/ppermute | solution.py:387
  44.1 23.4 %collective-permute-start.6 = (bf16[24,80,256]{2,1,0:T(8,128)(2,1)}, bf16[24,80,256]{2,1,0:T(8,128)(2,1)}, u32[]{:S(2)}, u32[]{:S(2)}) collective-permute-start(bf16[24,80,256]{2,1,0:T(8,128)(2,1)} %slice.19), channel_id=1, source_target_pairs={{8,0},{16,8},{24,16},{9,1},{17,9},{25,17},{10,2},{18,10},{26,18},{... | collective-permute-start | bytes 2949128 | tf_op jit(solution)/shard_map/ppermute | solution.py:388
  55.0 10.9 %copy-start.4 = (bf16[16,48,256]{2,1,0:T(8,128)(2,1)}, bf16[16,48,256]{2,1,0:T(8,128)(2,1)S(1)}, u32[]{:S(2)}) copy-start(bf16[16,48,256]{2,1,0:T(8,128)(2,1)S(1)} %collective-permute-done.4.refs_4_.refs_5_) | copy-start | bytes 1179652
  55.8 35.6 %all-to-all-start.1 = ((bf16[8,400,256]{2,1,0:T(8,128)(2,1)}), bf16[8,400,256]{2,1,0:T(8,128)(2,1)S(1)}, u32[]{:S(2)}, u32[]{:S(2)}) async-start(bf16[8,400,256]{2,1,0:T(8,128)(2,1)} %shard_map.86), calls=%async_computation.1 | async-start | bytes 3276800 | tf_op jit(solution)/shard_map/all_to_all | solution.py:405
  59.7 31.8 %copy-start = (s32[8,128]{1,0:T(8,128)S(1)}, s32[8,128]{1,0:T(8,128)}, u32[]{:S(2)}) copy-start(s32[8,128]{1,0:T(8,128)} %get-tuple-element.31.table_ref) | copy-start | bytes 12292
  59.7 31.8 %copy-start.1 = (s32[128]{0:T(128)S(1)}, s32[128]{0:T(128)}, u32[]{:S(2)}) copy-start(s32[128]{0:T(128)} %param.10) | copy-start | bytes 1540
  59.7 29.1 %collective-permute-start.16 = (bf16[24,80,256]{2,1,0:T(8,128)(2,1)}, bf16[24,80,256]{2,1,0:T(8,128)(2,1)S(1)}, u32[]{:S(2)}, u32[]{:S(2)}) collective-permute-start(bf16[24,80,256]{2,1,0:T(8,128)(2,1)} %slice.19), channel_id=1, source_target_pairs={{0,24},{24,0},{1,25},{25,1},{2,26},{26,2},{3,27},{27,3},{4,28},{28... | collective-permute-start | bytes 2949128 | tf_op jit(solution)/shard_map/ppermute | solution.py:397
  65.9 46.0 %collective-permute-start.14 = (bf16[24,80,256]{2,1,0:T(8,128)(2,1)}, bf16[24,80,256]{2,1,0:T(8,128)(2,1)}, u32[]{:S(2)}, u32[]{:S(2)}) collective-permute-start(bf16[24,80,256]{2,1,0:T(8,128)(2,1)} %collective-permute-done.5.refs_8_), channel_id=1, source_target_pairs={{8,16},{16,24},{9,17},{17,25},{10,18},{18,26},{11,19},{19,27},{12,... | collective-permute-start | bytes 2949128 | tf_op jit(solution)/shard_map/ppermute | solution.py:393
  67.5 44.3 %collective-permute-start.15 = (bf16[24,80,256]{2,1,0:T(8,128)(2,1)}, bf16[24,80,256]{2,1,0:T(8,128)(2,1)}, u32[]{:S(2)}, u32[]{:S(2)}) collective-permute-start(bf16[24,80,256]{2,1,0:T(8,128)(2,1)} %collective-permute-done.6.refs_9_), channel_id=1, source_target_pairs={{8,0},{16,8},{9,1},{17,9},{10,2},{18,10},{11,3},{19,11},{12,4},{20... | collective-permute-start | bytes 2949128 | tf_op jit(solution)/shard_map/ppermute | solution.py:394
  74.3 17.1 %collective-permute-start.10 = (bf16[3,144,256]{2,1,0:T(8,128)(2,1)}, bf16[3,144,256]{2,1,0:T(8,128)(2,1)S(1)}, u32[]{:S(2)}, u32[]{:S(2)}) collective-permute-start(bf16[3,144,256]{2,1,0:T(8,128)(2,1)} %get-tuple-element.54), channel_id=1, source_target_pairs={{0,4},{1,5},{2,6},{3,7},{4,0},{5,1},{6,2},{7,3},{8,12},{9,13},{10,... | collective-permute-start | bytes 663560 | tf_op jit(solution)/shard_map/ppermute | solution.py:431
  76.5 23.1 %collective-permute-start.11 = (bf16[3,144,256]{2,1,0:T(8,128)(2,1)}, bf16[3,144,256]{2,1,0:T(8,128)(2,1)S(1)}, u32[]{:S(2)}, u32[]{:S(2)}) collective-permute-start(bf16[3,144,256]{2,1,0:T(8,128)(2,1)} %get-tuple-element.55), channel_id=1, source_target_pairs={{0,5},{1,4},{2,7},{3,6},{4,1},{5,0},{6,3},{7,2},{8,13},{9,12},{10,... | collective-permute-start | bytes 663560 | tf_op jit(solution)/shard_map/ppermute | solution.py:431
  88.8 23.1 %copy-start.3 = (bf16[24,80,256]{2,1,0:T(8,128)(2,1)}, bf16[24,80,256]{2,1,0:T(8,128)(2,1)S(1)}, u32[]{:S(2)}) copy-start(bf16[24,80,256]{2,1,0:T(8,128)(2,1)S(1)} %collective-permute-done.16.refs_12_.refs_13_) | copy-start | bytes 2949124
  88.8 11.1 %collective-permute-start.12 = (bf16[3,144,256]{2,1,0:T(8,128)(2,1)}, bf16[3,144,256]{2,1,0:T(8,128)(2,1)S(1)}, u32[]{:S(2)}, u32[]{:S(2)}) collective-permute-start(bf16[3,144,256]{2,1,0:T(8,128)(2,1)} %get-tuple-element.56), channel_id=1, source_target_pairs={{0,6},{1,7},{2,4},{3,5},{4,2},{5,3},{6,0},{7,1},{8,14},{9,15},{10,... | collective-permute-start | bytes 663560 | tf_op jit(solution)/shard_map/ppermute | solution.py:431
  91.4 20.6 %copy-start.8 = (bf16[3,144,256]{2,1,0:T(8,128)(2,1)}, bf16[3,144,256]{2,1,0:T(8,128)(2,1)S(1)}, u32[]{:S(2)}) copy-start(bf16[3,144,256]{2,1,0:T(8,128)(2,1)S(1)} %collective-permute-done.10.refs_4_) | copy-start | bytes 663556
  91.4 10.2 %collective-permute-start.13 = (bf16[3,144,256]{2,1,0:T(8,128)(2,1)}, bf16[3,144,256]{2,1,0:T(8,128)(2,1)S(1)}, u32[]{:S(2)}, u32[]{:S(2)}) collective-permute-start(bf16[3,144,256]{2,1,0:T(8,128)(2,1)} %get-tuple-element.57), channel_id=1, source_target_pairs={{0,7},{1,6},{2,5},{3,4},{4,3},{5,2},{6,1},{7,0},{8,15},{9,14},{10,... | collective-permute-start | bytes 663560 | tf_op jit(solution)/shard_map/ppermute | solution.py:431
  94.8 17.1 %all-to-all-start.2 = ((f32[4,1,128]{2,1,0:T(1,128)}), f32[4,1,128]{2,1,0:T(1,128)S(1)}, u32[]{:S(2)}, u32[]{:S(2)}) async-start(f32[4,1,128]{2,1,0:T(1,128)} %broadcast_in_dim.63), calls=%async_computation.2 | async-start | bytes 4096 | tf_op jit(solution)/shard_map/all_to_all | solution.py:435
  99.6 12.3 %copy-start.9 = (bf16[3,144,256]{2,1,0:T(8,128)(2,1)}, bf16[3,144,256]{2,1,0:T(8,128)(2,1)S(1)}, u32[]{:S(2)}) copy-start(bf16[3,144,256]{2,1,0:T(8,128)(2,1)S(1)} %collective-permute-done.11.refs_5_) | copy-start | bytes 663556
  99.6 3.6 %collective-permute-start.7 = (bf16[3,144,256]{2,1,0:T(8,128)(2,1)}, bf16[3,144,256]{2,1,0:T(8,128)(2,1)S(1)}, u32[]{:S(2)}, u32[]{:S(2)}) collective-permute-start(bf16[3,144,256]{2,1,0:T(8,128)(2,1)} %get-tuple-element.51), channel_id=1, source_target_pairs={{0,1},{1,0},{2,3},{3,2},{4,5},{5,4},{6,7},{7,6},{8,9},{9,8},{10,11... | collective-permute-start | bytes 663560 | tf_op jit(solution)/shard_map/ppermute | solution.py:431
  99.9 12.1 %copy-start.10 = (bf16[3,144,256]{2,1,0:T(8,128)(2,1)}, bf16[3,144,256]{2,1,0:T(8,128)(2,1)S(1)}, u32[]{:S(2)}) copy-start(bf16[3,144,256]{2,1,0:T(8,128)(2,1)S(1)} %collective-permute-done.12.refs_6_) | copy-start | bytes 663556
  99.9 8.5 %collective-permute-start.8 = (bf16[3,144,256]{2,1,0:T(8,128)(2,1)}, bf16[3,144,256]{2,1,0:T(8,128)(2,1)S(1)}, u32[]{:S(2)}, u32[]{:S(2)}) collective-permute-start(bf16[3,144,256]{2,1,0:T(8,128)(2,1)} %get-tuple-element.52), channel_id=1, source_target_pairs={{0,2},{1,3},{2,0},{3,1},{4,6},{5,7},{6,4},{7,5},{8,10},{9,11},{10,... | collective-permute-start | bytes 663560 | tf_op jit(solution)/shard_map/ppermute | solution.py:431
  101.6 10.4 %copy-start.11 = (bf16[3,144,256]{2,1,0:T(8,128)(2,1)}, bf16[3,144,256]{2,1,0:T(8,128)(2,1)S(1)}, u32[]{:S(2)}) copy-start(bf16[3,144,256]{2,1,0:T(8,128)(2,1)S(1)} %collective-permute-done.13.refs_7_) | copy-start | bytes 663556
  101.6 10.3 %collective-permute-start.9 = (bf16[3,144,256]{2,1,0:T(8,128)(2,1)}, bf16[3,144,256]{2,1,0:T(8,128)(2,1)S(1)}, u32[]{:S(2)}, u32[]{:S(2)}) collective-permute-start(bf16[3,144,256]{2,1,0:T(8,128)(2,1)} %get-tuple-element.53), channel_id=1, source_target_pairs={{0,3},{1,2},{2,1},{3,0},{4,7},{5,6},{6,5},{7,4},{8,11},{9,10},{10,... | collective-permute-start | bytes 663560 | tf_op jit(solution)/shard_map/ppermute | solution.py:431
  (5 other events, 14.7 us)

commit v5 on v4

--- a/solution.py
+++ b/solution.py
@@ -10,7 +10,7 @@
 
 CAP = 3
 NOTE = 16
-RAW = 48
+RAW = 64
 VMEM = pl.BlockSpec(memory_space=pltpu.VMEM)
 SMEM = pl.BlockSpec(memory_space=pltpu.SMEM)
 HBM = pl.BlockSpec(memory_space=pl.ANY)
@@ -23,13 +23,11 @@
     return pltpu.CompilerParams(vmem_limit_bytes=size + (4 << 20))
 
 
-def own_rows_kernel(owner_ref, pairs_ref, rows_ref, out_ref, near_ref, table_ref, scalar_ref, sems, table_sem):
+def own_rows_kernel(owner_ref, pairs_ref, rows_ref, out_ref, table_ref, scalar_ref, sems, table_sem):
     fields = rows_ref.shape[0]
     owners = out_ref.shape[0]
     lines, width = out_ref.shape[1] // CAP, out_ref.shape[2]
     total = pairs_ref.shape[1]
-    near = pltpu.make_async_copy(rows_ref.at[:, pl.ds(0, near_ref.shape[1]), :], near_ref, sems.at[owners * CAP])
-    near.start()
     local = pairs_ref[...] - owner_ref[0] * fields
     field = lax.broadcasted_iota(jnp.int32, (fields, total), 0)
     hit = ((local[0:1] == field) | (local[1:2] == field)).astype(BF16)
@@ -64,25 +62,21 @@
         for c in range(CAP):
             move(d, c, 0).wait()
 
-    near.wait()
-
 
 def own_rows(owner, pair_list, embeddings, owners):
     fields, samples, width = embeddings.shape
     out = (owners, CAP * samples, width)
-    near = (fields, RAW, width)
     return pl.pallas_call(
         own_rows_kernel,
         out_shape=(
             jax.ShapeDtypeStruct(out, BF16),
-            jax.ShapeDtypeStruct(near, BF16),
             jax.ShapeDtypeStruct((8, 128), jnp.int32),
         ),
         in_specs=[SMEM, VMEM, HBM],
-        out_specs=(VMEM, VMEM, VMEM),
+        out_specs=(VMEM, VMEM),
         scratch_shapes=[
             pltpu.SMEM((8, 128), jnp.int32),
-            pltpu.SemaphoreType.DMA((owners * CAP + 1,)),
+            pltpu.SemaphoreType.DMA((owners * CAP,)),
             pltpu.SemaphoreType.DMA,
         ],
         compiler_params=limit(56 << 20),
@@ -101,7 +95,7 @@
     for r, choices in enumerate(ways):
         for at, source in enumerate(choices):
 
-            @pl.when(which_ref[r] == at)
+            @pl.when((len(choices) == 1) | (which_ref[0] == at))
             def _(r=r, source=source):
                 for k in range(len(outs)):
                     for c in range(CAP):
@@ -200,10 +194,32 @@
     )(slot_index, slot_width, rows, mats)
 
 
-def emb_grad_kernel(table_ref, width_ref, back_ref, labels_ref, out_ref, logit_ref, grad_ref):
+def factor_kernel(back_ref, labels_ref, logit_ref, grad_ref):
+    samples = logit_ref.shape[1]
+    lines = back_ref.shape[1] - NOTE
+    note = jnp.sum(back_ref[:, lines : lines + NOTE, 0:samples].astype(F32), axis=0)
+    logit = note[0:1] + note[1:2] + note[2:3]
+    logit_ref[...] = logit
+    grad = jax.nn.sigmoid(logit) - labels_ref[...].astype(F32)
+    for g in range(grad_ref.shape[0]):
+        grad_ref[g] = grad
+
+
+def factor_of(back, labels, groups):
+    samples = labels.shape[1]
+    return pl.pallas_call(
+        factor_kernel,
+        out_shape=(jax.ShapeDtypeStruct((1, samples), F32), jax.ShapeDtypeStruct((groups, 1, samples), F32)),
+        in_specs=[VMEM, VMEM],
+        out_specs=(VMEM, VMEM),
+        compiler_params=limit(math.prod(back.shape) * 2),
+        cost_estimate=CHEAP,
+    )(back, labels)
+
+
+def emb_grad_kernel(table_ref, width_ref, back_ref, grad_ref, out_ref):
     fields, samples, width = out_ref.shape
     owners = back_ref.shape[0]
-    lines = CAP * samples
 
     @pl.loop(0, fields)
     def _(f):
@@ -215,14 +231,7 @@
             f = table_ref[c, o]
             out_ref[f] += back_ref[o, c * samples : (c + 1) * samples, :].astype(F32)
 
-    note = back_ref[0, lines : lines + NOTE, 0:samples].astype(F32)
-    for o in range(1, owners):
-        note += back_ref[o, lines : lines + NOTE, 0:samples].astype(F32)
-    logit = note[0:1] + note[1:2] + note[2:3]
-    grad = jax.nn.sigmoid(logit) - labels_ref[...].astype(F32)
-    logit_ref[...] = logit
-    grad_ref[...] = grad
-    factor = jnp.broadcast_to(grad, (128, samples)).T
+    factor = jnp.broadcast_to(grad_ref[0], (128, samples)).T
     factor = jnp.concatenate([factor] * (width // 128), axis=1)
     columns = lax.broadcasted_iota(jnp.int32, (samples, width), 1)
 
@@ -231,20 +240,16 @@
         out_ref[f] = jnp.where(columns < width_ref[f], out_ref[f] * factor, 0.0)
 
 
-def emb_grad_of(table, own_width, back, labels, fields):
-    samples, width = labels.shape[1], back.shape[2]
+def emb_grad_of(table, own_width, back, grad, fields):
+    samples, width = grad.shape[2], back.shape[2]
     return pl.pallas_call(
         emb_grad_kernel,
-        out_shape=(
-            jax.ShapeDtypeStruct((fields, samples, width), F32),
-            jax.ShapeDtypeStruct((1, samples), F32),
-            jax.ShapeDtypeStruct((1, samples), F32),
-        ),
+        out_shape=jax.ShapeDtypeStruct((fields, samples, width), F32),
         in_specs=[SMEM, SMEM, VMEM, VMEM],
-        out_specs=(VMEM, VMEM, VMEM),
+        out_specs=VMEM,
         compiler_params=limit(math.prod(back.shape) * 2 + fields * samples * width * 4),
         cost_estimate=CHEAP,
-    )(table, own_width, back, labels)
+    )(table, own_width, back, grad)
 
 
 def mat_grad_kernel(ways, chunk, owners, slot_ref, width_ref, which_ref, source_ref, first_ref, owner_ref, grads_ref, own_ref, *refs):
@@ -283,7 +288,7 @@
                 waits[k][-1].start()
             for at, link in enumerate(ways[r]):
 
-                @pl.when(which_ref[r] == at)
+                @pl.when((len(ways[r]) == 1) | (which_ref[0] == at))
                 def _(k=k, link=link):
                     pltpu.make_async_copy(links[link], place(k, raw_lines, kept_lines), sems.at[k, 1]).start()
 
@@ -351,13 +356,6 @@
     )(slot_index, slot_width, which, sources, first, owner, grads, own, *raw, *links)
 
 
-def line_rounds(n):
-    order = []
-    for i in range(n):
-        order.append([(up, k) for k in range(1, n) for up in (True, False) if (i - k >= 0 if up else i + k < n)])
-    return order
-
-
 def shards(embeddings, field_width, pair_fields, pair_mats, labels):
     owners = lax.axis_size("pair")
     groups = lax.axis_size("dp")
@@ -370,7 +368,7 @@
     pair_list = pair_fields.T
     field_ids = jnp.arange(fields, dtype=jnp.int32)
     slot_ids = jnp.arange(CAP, dtype=jnp.int32)
-    picked, near, table = own_rows(owner.reshape(1), pair_list, embeddings, owners)
+    picked, table = own_rows(owner.reshape(1), pair_list, embeddings, owners)
 
     mine = lax.dynamic_slice_in_dim(pair_list, owner * pairs, pairs, 1)
     all_ids = jnp.arange(every, dtype=jnp.int32)
@@ -383,40 +381,30 @@
     slot_width = jnp.sum(jnp.where(taken, field_width.reshape(owners, 1, fields), 0), axis=2).reshape(-1)
     own_width = lax.dynamic_slice_in_dim(field_width, owner * fields, fields, 0)
 
+    def swap(rows, k, members=range(groups)):
+        return lax.ppermute(rows, "dp", [(i, i ^ k) for i in members])
+
     def chain(own):
-        up = lax.ppermute(own, "dp", [(i, i + 1) for i in range(groups - 1)])
-        down = lax.ppermute(own, "dp", [(i + 1, i) for i in range(groups - 1)])
-        yield [up, down]
-        found = [up, down]
-        for k in range(2, groups):
-            if k == 2:
-                found.append(lax.ppermute(up, "dp", [(i, i + 1) for i in range(1, groups - 1)]))
-                found.append(lax.ppermute(down, "dp", [(i, i - 1) for i in range(1, groups - 1)]))
-            elif 2 * k >= groups:
-                ends = [(i, i + k) for i in range(groups - k)]
-                found += [lax.ppermute(own, "dp", ends + [(j, i) for i, j in ends])] * 2
-            else:
-                found.append(lax.ppermute(own, "dp", [(i, i + k) for i in range(groups - k)]))
-                found.append(lax.ppermute(own, "dp", [(i + k, i) for i in range(groups - k)]))
-        yield found
+        if groups != 4:
+            found = [swap(own, k) for k in range(1, groups)]
+            yield found
+            yield found
+            return
+        beside, across = swap(own, 1), swap(own, 3)
+        yield [beside, across]
+        yield [beside, across, swap(beside, 3, (1, 2)), swap(across, 1, (1, 2))]
 
     def exchange(rows):
         lines = rows.reshape(owners, -1, width)
         return lax.all_to_all(lines, "pair", split_axis=0, concat_axis=0, tiled=True)
 
     tie = lax.optimization_barrier
-    order = line_rounds(groups)
-    ways, which, origin = [], [], []
-    for r in range(groups - 1):
-        names = sorted({order[i][r] for i in range(groups)})
-        ways.append([2 * (k - 1) + (not up) for up, k in names])
-        which.append([names.index(order[i][r]) for i in range(groups)])
-        origin.append([i - order[i][r][1] if order[i][r][0] else i + order[i][r][1] for i in range(groups)])
-    places = jnp.array([list(w) + [i] + list(s) for i, (w, s) in enumerate(zip(zip(*which), zip(*origin)))], jnp.int32)
-    places = lax.dynamic_index_in_dim(places, group, 0, keepdims=False)
-    which, sources = places[: groups - 1], places[groups - 1 :]
-
-    raw_steps = chain(near)
+    ways = [[0], [1], [2, 3]] if groups == 4 else [[k] for k in range(groups - 1)]
+    steps = (1, 3, 2) if groups == 4 else range(1, groups)
+    which = ((group == 0) | (group == 3)).astype(jnp.int32).reshape(1)
+    sources = jnp.stack([group] + [group ^ k for k in steps]).astype(jnp.int32)
+
+    raw_steps = chain(embeddings[:, :RAW])
     close = next(raw_steps)
     received = exchange(picked).reshape(owners * CAP, samples, width)
     received, close[:] = tie((received, close))
@@ -426,13 +414,20 @@
     sums, raw = tie((sums, raw))
     back = exchange(sums)
     near_kept = next(kept_steps)
-    raw, near_kept[:] = tie((raw, near_kept))
     far = far_rows(ways, owner.reshape(1), which, table, raw, owners)
-    far = [lax.ppermute(x, "pair", [(i, i ^ k) for i in range(owners)]) if k else x for k, x in enumerate(far)]
+    first = [k for k in range(2, owners, 2)]
+    moved = {k: lax.ppermute(far[k], "pair", [(i, i ^ k) for i in range(owners)]) for k in first}
+    rest = [k for k in range(owners - 1, 0, -1) if k not in first]
+    if owners == 8:
+        moved, far = tie((moved, far))
+    moved |= {k: lax.ppermute(far[k], "pair", [(i, i ^ k) for i in range(owners)]) for k in rest}
+    far = [moved.get(k, far[k]) for k in range(owners)]
     kept = next(kept_steps)
-    emb_grad, logits, grad = emb_grad_of(table, own_width, back, labels[None, :], fields)
+    back, near_kept[:] = tie((back, near_kept))
+    logits, grad = factor_of(back, labels[None, :], groups)
     logits = logits.reshape(samples)
-    grads = lax.all_to_all(jnp.broadcast_to(grad, (groups, 1, samples)), "dp", split_axis=0, concat_axis=0, tiled=True)
+    grads = lax.all_to_all(grad, "dp", split_axis=0, concat_axis=0, tiled=True)
+    emb_grad = emb_grad_of(table, own_width, back, grad, fields)
     rows = width // groups
     mat_grad = mat_grad_of(
         ways, slot_index, slot_width, which, sources, (group * rows).reshape(1), owner.reshape(1), grads, received, far, kept, rows

time: 123 us -> 123 us (level)
  waiting for transfers between devices: 26.3 us -> 51.4 us
  starting transfers between devices: 56.9 us -> 34.2 us
  local copies, waits for them, and re-layouts: 6.97 us -> 3.66 us
    ppermute x17 -> x15, waiting for transfers between devices: 24.1 us -> 51.4 us  [the longest x8 39.1 us: swap(): return lax.ppermute(rows, 'dp', [(i, i ^ k) for i in members])]
    ppermute x17 -> x15, starting transfers between devices: 43.1 us -> 21.7 us  [the longest x8 16 us: swap(): return lax.ppermute(rows, 'dp', [(i, i ^ k) for i in members])]
    all_to_all x2, waiting for transfers between devices: 2.13 us -> 0.01 us  [exchange(): lax.all_to_all(lines, 'pair', split_axis=0, concat_axis=0, tiled=True)]
    all_to_all x1, starting transfers between devices: 4.85 us -> 3.22 us  [shards(): grads = lax.all_to_all(grad, 'dp', split_axis=0, concat_axis=0, tiled=True)]
    pallas_call x1 -> x2, Pallas kernels: 2.72 us -> 3.38 us  [the longest x1 2.78 us: emb_grad_of(): pl.pallas_call(emb_grad_kernel, out_shape=jax.ShapeDtypeStruct((fields, s...]
  transfers between devices with their start and end apart: 20 -> 18, of which waited for: 6 -> 6; matrix products, arithmetic and copies ran while one was open for 6% -> 4% of each run, Pallas kernels for 13% -> 13%
where the time goes in v5:
time: 123 us; the launch traced here: 122 us
  waiting for transfers between devices  51.4 us (42%)
  starting transfers between devices  34.2 us (28%)
  Pallas kernels  30.2 us (25%)
  local copies, waits for them, and re-layouts  3.66 us (3%)
  other arithmetic  1.92 us (2%)
    ppermute x8, waiting for transfers between devices, swap(): return lax.ppermute(rows, 'dp', [(i, i ^ k) for i in members])  39.1 us
    ppermute x8, starting transfers between devices, swap(): return lax.ppermute(rows, 'dp', [(i, i ^ k) for i in members])  16 us
    ppermute x7, waiting for transfers between devices, shards(): lax.ppermute(far[k], 'pair', [(i, i ^ k) for i in range(owners)])  12.3 us
    pallas_call x1, Pallas kernels, mat_grad_of(): pl.pallas_call(functools.partial(mat_grad_kernel, ways, chunk, len(raw)),...  9.39 us
    all_to_all x2, starting transfers between devices, exchange(): lax.all_to_all(lines, 'pair', split_axis=0, concat_axis=0, tiled=True)  9.26 us
    pallas_call x1, Pallas kernels, forward(): pl.pallas_call(functools.partial(forward_kernel, group), out_shape=jax.Sh...  8.52 us
    ppermute x7, starting transfers between devices, shards(): lax.ppermute(far[k], 'pair', [(i, i ^ k) for i in range(owners)])  5.69 us
    pallas_call x1, Pallas kernels, far_rows(): pl.pallas_call(functools.partial(far_rows_kernel, ways, len(sources)), ou...  4.52 us
  transfers between devices with their start and end apart: 18, of which 6 were waited for; matrix products, arithmetic and copies ran while one was open for 4% of the time, Pallas kernels for 13%

profile of v5, /device:TPU:0, one launch (start us, length us, event | category | flops | bytes accessed | tf_op | source)
XLA Modules:
  0.0 122.2 jit_solution(10359115005353519933)
XLA Ops:
  0.6 4.3 %shard_map.76 = (bf16[8,384,256]{2,1,0:T(8,128)(2,1)}, s32[8,128]{1,0:T(8,128)}) custom-call(s32[1]{0:T(128)} %bitcast.owner_ref, s32[2,384]{1,0:T(2,128)} %bitcast.15, bf16[16,128,256]{2,1,0:T(8,128)(2,1)} %rows_ref.1), custom_call_target="tpu_custom_call" | custom-call | tf_op jit(solution)/shard_map/pallas_call | solution.py:69
  5.0 5.4 %all-to-all-start = ((bf16[8,384,256]{2,1,0:T(8,128)(2,1)}), bf16[8,384,256]{2,1,0:T(8,128)(2,1)S(1)}, u32[]{:S(2)}, u32[]{:S(2)}) async-start(bf16[8,384,256]{2,1,0:T(8,128)(2,1)} %get-tuple-element.30), calls=%async_computation | async-start | bytes 3145728 | tf_op jit(solution)/shard_map/all_to_all | solution.py:399
  10.5 1.6 %collective-permute-start = (bf16[16,64,256]{2,1,0:T(8,128)(2,1)S(1)}, bf16[16,64,256]{2,1,0:T(8,128)(2,1)}, u32[]{:S(2)}, u32[]{:S(2)}) collective-permute-start(bf16[16,64,256]{2,1,0:T(8,128)(2,1)S(1)} %slice.6), channel_id=1, source_target_pairs={{0,8},{8,0},{16,24},{24,16},{1,9},{9,1},{17,25},{25,17},{2,10},{10... | collective-permute-start | bytes 1572872 | tf_op jit(solution)/shard_map/ppermute | solution.py:385
  12.1 2.5 %collective-permute-start.1 = (bf16[16,64,256]{2,1,0:T(8,128)(2,1)S(1)}, bf16[16,64,256]{2,1,0:T(8,128)(2,1)}, u32[]{:S(2)}, u32[]{:S(2)}) collective-permute-start(bf16[16,64,256]{2,1,0:T(8,128)(2,1)S(1)} %slice.6), channel_id=1, source_target_pairs={{0,24},{8,16},{16,8},{24,0},{1,25},{9,17},{17,9},{25,1},{2,26},{10... | collective-permute-start | bytes 1572872 | tf_op jit(solution)/shard_map/ppermute | solution.py:385
  14.6 0.8 constant_dynamic-slice_fusion
  16.0 9.0 %collective-permute-done.refs_0_ = bf16[16,64,256]{2,1,0:T(8,128)(2,1)} collective-permute-done((bf16[16,64,256]{2,1,0:T(8,128)(2,1)S(1)}, bf16[16,64,256]{2,1,0:T(8,128)(2,1)}, u32[]{:S(2)}, u32[]{:S(2)}) %collective-permute-start) | collective-permute-done | bytes 524320 | tf_op jit(solution)/shard_map/ppermute | solution.py:385
  25.0 1.5 %collective-permute-start.2 = (bf16[16,64,256]{2,1,0:T(8,128)(2,1)}, bf16[16,64,256]{2,1,0:T(8,128)(2,1)}, u32[]{:S(2)}, u32[]{:S(2)}) collective-permute-start(bf16[16,64,256]{2,1,0:T(8,128)(2,1)} %collective-permute-done.refs_0_), channel_id=1, source_target_pairs={{8,16},{16,8},{9,17},{17,9},{10,18},{18,10},{11,19},{19,11},{12,20... | collective-permute-start | bytes 1572872 | tf_op jit(solution)/shard_map/ppermute | solution.py:385
  26.4 11.9 %collective-permute-done.1.refs_1_ = bf16[16,64,256]{2,1,0:T(8,128)(2,1)} collective-permute-done((bf16[16,64,256]{2,1,0:T(8,128)(2,1)S(1)}, bf16[16,64,256]{2,1,0:T(8,128)(2,1)}, u32[]{:S(2)}, u32[]{:S(2)}) %collective-permute-start.1) | collective-permute-done | bytes 524320 | tf_op jit(solution)/shard_map/ppermute | solution.py:385
  38.3 1.3 %collective-permute-start.3 = (bf16[16,64,256]{2,1,0:T(8,128)(2,1)}, bf16[16,64,256]{2,1,0:T(8,128)(2,1)}, u32[]{:S(2)}, u32[]{:S(2)}) collective-permute-start(bf16[16,64,256]{2,1,0:T(8,128)(2,1)} %collective-permute-done.1.refs_1_), channel_id=1, source_target_pairs={{8,0},{16,24},{9,1},{17,25},{10,2},{18,26},{11,3},{19,27},{12,4},{... | collective-permute-start | bytes 1572872 | tf_op jit(solution)/shard_map/ppermute | solution.py:385
  39.9 0.8 select_reduce_fusion.1.slot_ref
  40.7 1.0 slice.7
  41.6 3.4 %collective-permute-start.4 = (bf16[24,64,256]{2,1,0:T(8,128)(2,1)}, bf16[24,64,256]{2,1,0:T(8,128)(2,1)S(1)}, u32[]{:S(2)}, u32[]{:S(2)}) collective-permute-start(bf16[24,64,256]{2,1,0:T(8,128)(2,1)} %slice.7), channel_id=1, source_target_pairs={{0,8},{8,0},{16,24},{24,16},{1,9},{9,1},{17,25},{25,17},{2,10},{10... | collective-permute-start | bytes 2359304 | tf_op jit(solution)/shard_map/ppermute | solution.py:385
  45.1 2.9 %collective-permute-start.5 = (bf16[24,64,256]{2,1,0:T(8,128)(2,1)}, bf16[24,64,256]{2,1,0:T(8,128)(2,1)S(1)}, u32[]{:S(2)}, u32[]{:S(2)}) collective-permute-start(bf16[24,64,256]{2,1,0:T(8,128)(2,1)} %slice.7), channel_id=1, source_target_pairs={{0,24},{8,16},{16,8},{24,0},{1,25},{9,17},{17,9},{25,1},{2,26},{10... | collective-permute-start | bytes 2359304 | tf_op jit(solution)/shard_map/ppermute | solution.py:385
  48.2 0.7 reshape.63.width_ref
  48.9 8.5 %shard_map.77 = bf16[8,400,256]{2,1,0:T(8,128)(2,1)} custom-call(s32[96]{0:T(128)} %select_reduce_fusion.1.slot_ref, s32[24]{0:T(128)} %reshape.63.width_ref, bf16[24,128,256]{2,1,0:T(8,128)(2,1)} %bitcast.13, bf16[48,256,256]{2,1,0:T(8,128)(2,1)} %mats_ref.1), custom_call_target="tpu_custom_call" | custom-call | tf_op jit(solution)/shard_map/pallas_call | solution.py:180
  57.4 3.9 %all-to-all-start.1 = ((bf16[8,400,256]{2,1,0:T(8,128)(2,1)}), bf16[8,400,256]{2,1,0:T(8,128)(2,1)S(1)}, u32[]{:S(2)}, u32[]{:S(2)}) async-start(bf16[8,400,256]{2,1,0:T(8,128)(2,1)} %shard_map.77), calls=%async_computation.1 | async-start | bytes 3276800 | tf_op jit(solution)/shard_map/all_to_all | solution.py:399
  61.3 4.5 %shard_map.79 = (bf16[3,192,256]{2,1,0:T(8,128)(2,1)}, bf16[3,192,256]{2,1,0:T(8,128)(2,1)}, bf16[3,192,256]{2,1,0:T(8,128)(2,1)}, bf16[3,192,256]{2,1,0:T(8,128...) custom-call(s32[1]{0:T(128)} %bitcast.owner_ref, ...), custom_call_target="tpu_custom_call" | custom-call | tf_op jit(solution)/shard_map/pallas_call | solution.py:113
  65.8 2.1 %collective-permute-start.6 = (bf16[3,192,256]{2,1,0:T(8,128)(2,1)}, bf16[3,192,256]{2,1,0:T(8,128)(2,1)S(1)}, u32[]{:S(2)}, u32[]{:S(2)}) collective-permute-start(bf16[3,192,256]{2,1,0:T(8,128)(2,1)} %get-tuple-element.41), channel_id=1, source_target_pairs={{0,2},{1,3},{2,0},{3,1},{4,6},{5,7},{6,4},{7,5},{8,10},{9,11},{10,... | collective-permute-start | bytes 884744 | tf_op jit(solution)/shard_map/ppermute | solution.py:419
  67.9 1.5 %collective-permute-start.7 = (bf16[3,192,256]{2,1,0:T(8,128)(2,1)}, bf16[3,192,256]{2,1,0:T(8,128)(2,1)}, u32[]{:S(2)}, u32[]{:S(2)}) collective-permute-start(bf16[3,192,256]{2,1,0:T(8,128)(2,1)} %get-tuple-element.42), channel_id=1, source_target_pairs={{0,4},{1,5},{2,6},{3,7},{4,0},{5,1},{6,2},{7,3},{8,12},{9,13},{10,... | collective-permute-start | bytes 884744 | tf_op jit(solution)/shard_map/ppermute | solution.py:419
  69.4 18.2 %collective-permute-done.4.refs_8_ = bf16[24,64,256]{2,1,0:T(8,128)(2,1)S(1)} collective-permute-done((bf16[24,64,256]{2,1,0:T(8,128)(2,1)}, bf16[24,64,256]{2,1,0:T(8,128)(2,1)S(1)}, u32[]{:S(2)}, u32[]{:S(2)}) %collective-permute-start.4) | collective-permute-done | bytes 786464 | tf_op jit(solution)/shard_map/ppermute | solution.py:385
  87.6 1.5 %collective-permute-start.13 = (bf16[24,64,256]{2,1,0:T(8,128)(2,1)S(1)}, bf16[24,64,256]{2,1,0:T(8,128)(2,1)}, u32[]{:S(2)}, u32[]{:S(2)}) collective-permute-start(bf16[24,64,256]{2,1,0:T(8,128)(2,1)S(1)} %collective-permute-done.4.refs_8_), channel_id=1, source_target_pairs={{8,16},{16,8},{9,17},{17,9},{10,18},{18,10},{11,19},{19,11},{12,20... | collective-permute-start | bytes 2359304 | tf_op jit(solution)/shard_map/ppermute | solution.py:385
  89.2 1.3 %collective-permute-start.14 = (bf16[24,64,256]{2,1,0:T(8,128)(2,1)S(1)}, bf16[24,64,256]{2,1,0:T(8,128)(2,1)}, u32[]{:S(2)}, u32[]{:S(2)}) collective-permute-start(bf16[24,64,256]{2,1,0:T(8,128)(2,1)S(1)} %collective-permute-done.5.refs_9_), channel_id=1, source_target_pairs={{8,0},{16,24},{9,1},{17,25},{10,2},{18,26},{11,3},{19,27},{12,4},{... | collective-permute-start | bytes 2359304 | tf_op jit(solution)/shard_map/ppermute | solution.py:385
  90.5 5.3 %collective-permute-done.8.refs_6_ = bf16[3,192,256]{2,1,0:T(8,128)(2,1)} collective-permute-done((bf16[3,192,256]{2,1,0:T(8,128)(2,1)}, bf16[3,192,256]{2,1,0:T(8,128)(2,1)}, u32[]{:S(2)}, u32[]{:S(2)}) %collective-permute-start.8) | collective-permute-done | bytes 294944 | tf_op jit(solution)/shard_map/ppermute | solution.py:419
  95.8 0.7 collective-permute-start.10
  96.5 1.2 %collective-permute-done.9.refs_1_ = bf16[3,192,256]{2,1,0:T(8,128)(2,1)} collective-permute-done((bf16[3,192,256]{2,1,0:T(8,128)(2,1)}, bf16[3,192,256]{2,1,0:T(8,128)(2,1)}, u32[]{:S(2)}, u32[]{:S(2)}) %collective-permute-start.9) | collective-permute-done | bytes 294944 | tf_op jit(solution)/shard_map/ppermute | solution.py:423
  97.7 1.4 %collective-permute-start.12 = (bf16[3,192,256]{2,1,0:T(8,128)(2,1)}, bf16[3,192,256]{2,1,0:T(8,128)(2,1)}, u32[]{:S(2)}, u32[]{:S(2)}) collective-permute-start(bf16[3,192,256]{2,1,0:T(8,128)(2,1)} %get-tuple-element.56), channel_id=1, source_target_pairs={{0,7},{1,6},{2,5},{3,4},{4,3},{5,2},{6,1},{7,0},{8,15},{9,14},{10,... | collective-permute-start | bytes 884744 | tf_op jit(solution)/shard_map/ppermute | solution.py:423
  99.1 0.6 shard_map.78
  99.7 3.2 %all-to-all-start.2 = ((f32[4,1,128]{2,1,0:T(1,128)}), f32[4,1,128]{2,1,0:T(1,128)S(1)}, u32[]{:S(2)}, u32[]{:S(2)}) async-start(f32[4,1,128]{2,1,0:T(1,128)} %get-tuple-element.35.grad_ref), calls=%async_computation.2 | async-start | bytes 4096 | tf_op jit(solution)/shard_map/all_to_all | solution.py:429
  103.0 0.6 pad_add_fusion.source_ref
  103.6 2.8 %shard_map.81 = f32[16,128,256]{2,1,0:T(8,128)} custom-call(s32[8,128]{1,0:T(8,128)S(1)} %copy-done, s32[16]{0:T(128)S(1)} %dynamic_slice.4.width_ref, bf16[8,400,256]{2,1,0:T(8,128)(2,1)S(1)} %all-to-all-done.1.back_ref, f32[4,1,128]{2,1,0:T(1,128)} %get-tuple-element.35.grad_ref), custom_call_target="tpu_custom_call" | custom-call | tf_op jit(solution)/shard_map/pallas_call | solution.py:245
  106.4 5.8 %collective-permute-done.11.refs_5_ = bf16[3,192,256]{2,1,0:T(8,128)(2,1)} collective-permute-done((bf16[3,192,256]{2,1,0:T(8,128)(2,1)}, bf16[3,192,256]{2,1,0:T(8,128)(2,1)}, u32[]{:S(2)}, u32[]{:S(2)}) %collective-permute-start.11) | collective-permute-done | bytes 294944 | tf_op jit(solution)/shard_map/ppermute | solution.py:423
  112.8 9.4 %shard_map.80 = bf16[48,64,256]{2,1,0:T(8,128)(2,1)} custom-call(s32[96]{0:T(128)} %select_reduce_fusion.1.slot_ref, s32[24]{0:T(128)} %reshape.63.width_ref, s32[1]{0:T(128)} %bitcast.5.which_ref, s32[4]{0:T(128)} %pad_add_fusion.source_ref, s32[1]{0:T(128)} %bitcast.10.first_ref, s32[1]{0:T(128)} %bitcast.owner_ref, f32[4,1,128]{2,1,0:T(1,128)} %copy-done.7, ...), custom_call_target="tpu_custom_call" | custom-call | tf_op jit(solution)/shard_map/pallas_call | solution.py:341
  (49 shorter events, 1.9 us)
Async XLA Ops:
  5.0 5.4 %copy-start.3 = (bf16[16,128,256]{2,1,0:T(8,128)(2,1)S(1)}, bf16[16,128,256]{2,1,0:T(8,128)(2,1)}, u32[]{:S(2)}) copy-start(bf16[16,128,256]{2,1,0:T(8,128)(2,1)} %rows_ref.1) | copy-start | bytes 3145732
  5.0 34.8 %copy-start.8 = (s32[128]{0:T(128)S(1)}, s32[128]{0:T(128)}, u32[]{:S(2)}) copy-start(s32[128]{0:T(128)} %param.6) | copy-start | bytes 1540
  5.0 35.6 %all-to-all-start = ((bf16[8,384,256]{2,1,0:T(8,128)(2,1)}), bf16[8,384,256]{2,1,0:T(8,128)(2,1)S(1)}, u32[]{:S(2)}, u32[]{:S(2)}) async-start(bf16[8,384,256]{2,1,0:T(8,128)(2,1)} %get-tuple-element.30), calls=%async_computation | async-start | bytes 3145728 | tf_op jit(solution)/shard_map/all_to_all | solution.py:399
  10.5 14.5 %collective-permute-start = (bf16[16,64,256]{2,1,0:T(8,128)(2,1)S(1)}, bf16[16,64,256]{2,1,0:T(8,128)(2,1)}, u32[]{:S(2)}, u32[]{:S(2)}) collective-permute-start(bf16[16,64,256]{2,1,0:T(8,128)(2,1)S(1)} %slice.6), channel_id=1, source_target_pairs={{0,8},{8,0},{16,24},{24,16},{1,9},{9,1},{17,25},{25,17},{2,10},{10... | collective-permute-start | bytes 1572872 | tf_op jit(solution)/shard_map/ppermute | solution.py:385
  12.1 26.2 %collective-permute-start.1 = (bf16[16,64,256]{2,1,0:T(8,128)(2,1)S(1)}, bf16[16,64,256]{2,1,0:T(8,128)(2,1)}, u32[]{:S(2)}, u32[]{:S(2)}) collective-permute-start(bf16[16,64,256]{2,1,0:T(8,128)(2,1)S(1)} %slice.6), channel_id=1, source_target_pairs={{0,24},{8,16},{16,8},{24,0},{1,25},{9,17},{17,9},{25,1},{2,26},{10... | collective-permute-start | bytes 1572872 | tf_op jit(solution)/shard_map/ppermute | solution.py:385
  25.0 32.4 %collective-permute-start.2 = (bf16[16,64,256]{2,1,0:T(8,128)(2,1)}, bf16[16,64,256]{2,1,0:T(8,128)(2,1)}, u32[]{:S(2)}, u32[]{:S(2)}) collective-permute-start(bf16[16,64,256]{2,1,0:T(8,128)(2,1)} %collective-permute-done.refs_0_), channel_id=1, source_target_pairs={{8,16},{16,8},{9,17},{17,9},{10,18},{18,10},{11,19},{19,11},{12,20... | collective-permute-start | bytes 1572872 | tf_op jit(solution)/shard_map/ppermute | solution.py:385
  38.3 19.1 %collective-permute-start.3 = (bf16[16,64,256]{2,1,0:T(8,128)(2,1)}, bf16[16,64,256]{2,1,0:T(8,128)(2,1)}, u32[]{:S(2)}, u32[]{:S(2)}) collective-permute-start(bf16[16,64,256]{2,1,0:T(8,128)(2,1)} %collective-permute-done.1.refs_1_), channel_id=1, source_target_pairs={{8,0},{16,24},{9,1},{17,25},{10,2},{18,26},{11,3},{19,27},{12,4},{... | collective-permute-start | bytes 1572872 | tf_op jit(solution)/shard_map/ppermute | solution.py:385
  40.6 8.2 %copy-start.2 = (bf16[8,384,256]{2,1,0:T(8,128)(2,1)}, bf16[8,384,256]{2,1,0:T(8,128)(2,1)S(1)}, u32[]{:S(2)}) copy-start(bf16[8,384,256]{2,1,0:T(8,128)(2,1)S(1)} %all-to-all-done) | copy-start | bytes 4718596
  41.6 46.0 %collective-permute-start.4 = (bf16[24,64,256]{2,1,0:T(8,128)(2,1)}, bf16[24,64,256]{2,1,0:T(8,128)(2,1)S(1)}, u32[]{:S(2)}, u32[]{:S(2)}) collective-permute-start(bf16[24,64,256]{2,1,0:T(8,128)(2,1)} %slice.7), channel_id=1, source_target_pairs={{0,8},{8,0},{16,24},{24,16},{1,9},{9,1},{17,25},{25,17},{2,10},{10... | collective-permute-start | bytes 2359304 | tf_op jit(solution)/shard_map/ppermute | solution.py:385
  45.1 44.1 %collective-permute-start.5 = (bf16[24,64,256]{2,1,0:T(8,128)(2,1)}, bf16[24,64,256]{2,1,0:T(8,128)(2,1)S(1)}, u32[]{:S(2)}, u32[]{:S(2)}) collective-permute-start(bf16[24,64,256]{2,1,0:T(8,128)(2,1)} %slice.7), channel_id=1, source_target_pairs={{0,24},{8,16},{16,8},{24,0},{1,25},{9,17},{17,9},{25,1},{2,26},{10... | collective-permute-start | bytes 2359304 | tf_op jit(solution)/shard_map/ppermute | solution.py:385
  57.4 41.7 %all-to-all-start.1 = ((bf16[8,400,256]{2,1,0:T(8,128)(2,1)}), bf16[8,400,256]{2,1,0:T(8,128)(2,1)S(1)}, u32[]{:S(2)}, u32[]{:S(2)}) async-start(bf16[8,400,256]{2,1,0:T(8,128)(2,1)} %shard_map.77), calls=%async_computation.1 | async-start | bytes 3276800 | tf_op jit(solution)/shard_map/all_to_all | solution.py:399
  61.3 37.9 %copy-start.1 = (s32[128]{0:T(128)S(1)}, s32[128]{0:T(128)}, u32[]{:S(2)}) copy-start(s32[128]{0:T(128)} %param.9) | copy-start | bytes 1540
  61.3 42.3 %copy-start = (s32[8,128]{1,0:T(8,128)S(1)}, s32[8,128]{1,0:T(8,128)}, u32[]{:S(2)}) copy-start(s32[8,128]{1,0:T(8,128)} %get-tuple-element.36.table_ref) | copy-start | bytes 12292
  65.8 24.6 %collective-permute-start.6 = (bf16[3,192,256]{2,1,0:T(8,128)(2,1)}, bf16[3,192,256]{2,1,0:T(8,128)(2,1)S(1)}, u32[]{:S(2)}, u32[]{:S(2)}) collective-permute-start(bf16[3,192,256]{2,1,0:T(8,128)(2,1)} %get-tuple-element.41), channel_id=1, source_target_pairs={{0,2},{1,3},{2,0},{3,1},{4,6},{5,7},{6,4},{7,5},{8,10},{9,11},{10,... | collective-permute-start | bytes 884744 | tf_op jit(solution)/shard_map/ppermute | solution.py:419
  67.9 22.6 %collective-permute-start.7 = (bf16[3,192,256]{2,1,0:T(8,128)(2,1)}, bf16[3,192,256]{2,1,0:T(8,128)(2,1)}, u32[]{:S(2)}, u32[]{:S(2)}) collective-permute-start(bf16[3,192,256]{2,1,0:T(8,128)(2,1)} %get-tuple-element.42), channel_id=1, source_target_pairs={{0,4},{1,5},{2,6},{3,7},{4,0},{5,1},{6,2},{7,3},{8,12},{9,13},{10,... | collective-permute-start | bytes 884744 | tf_op jit(solution)/shard_map/ppermute | solution.py:419
  69.4 26.4 %collective-permute-start.8 = (bf16[3,192,256]{2,1,0:T(8,128)(2,1)}, bf16[3,192,256]{2,1,0:T(8,128)(2,1)}, u32[]{:S(2)}, u32[]{:S(2)}) collective-permute-start(bf16[3,192,256]{2,1,0:T(8,128)(2,1)} %get-tuple-element.43), channel_id=1, source_target_pairs={{0,6},{1,7},{2,4},{3,5},{4,2},{5,3},{6,0},{7,1},{8,14},{9,15},{10,... | collective-permute-start | bytes 884744 | tf_op jit(solution)/shard_map/ppermute | solution.py:419
  87.6 18.8 %copy-start.4 = (bf16[24,64,256]{2,1,0:T(8,128)(2,1)}, bf16[24,64,256]{2,1,0:T(8,128)(2,1)S(1)}, u32[]{:S(2)}) copy-start(bf16[24,64,256]{2,1,0:T(8,128)(2,1)S(1)} %collective-permute-done.4.refs_8_) | copy-start | bytes 2359300
  87.6 24.6 %collective-permute-start.13 = (bf16[24,64,256]{2,1,0:T(8,128)(2,1)S(1)}, bf16[24,64,256]{2,1,0:T(8,128)(2,1)}, u32[]{:S(2)}, u32[]{:S(2)}) collective-permute-start(bf16[24,64,256]{2,1,0:T(8,128)(2,1)S(1)} %collective-permute-done.4.refs_8_), channel_id=1, source_target_pairs={{8,16},{16,8},{9,17},{17,9},{10,18},{18,10},{11,19},{19,11},{12,20... | collective-permute-start | bytes 2359304 | tf_op jit(solution)/shard_map/ppermute | solution.py:385
  89.2 17.2 %copy-start.5 = (bf16[24,64,256]{2,1,0:T(8,128)(2,1)}, bf16[24,64,256]{2,1,0:T(8,128)(2,1)S(1)}, u32[]{:S(2)}) copy-start(bf16[24,64,256]{2,1,0:T(8,128)(2,1)S(1)} %collective-permute-done.5.refs_9_) | copy-start | bytes 2359300
  89.2 23.1 %collective-permute-start.14 = (bf16[24,64,256]{2,1,0:T(8,128)(2,1)S(1)}, bf16[24,64,256]{2,1,0:T(8,128)(2,1)}, u32[]{:S(2)}, u32[]{:S(2)}) collective-permute-start(bf16[24,64,256]{2,1,0:T(8,128)(2,1)S(1)} %collective-permute-done.5.refs_9_), channel_id=1, source_target_pairs={{8,0},{16,24},{9,1},{17,25},{10,2},{18,26},{11,3},{19,27},{12,4},{... | collective-permute-start | bytes 2359304 | tf_op jit(solution)/shard_map/ppermute | solution.py:385
  90.5 16.0 %copy-start.6 = (bf16[3,192,256]{2,1,0:T(8,128)(2,1)}, bf16[3,192,256]{2,1,0:T(8,128)(2,1)S(1)}, u32[]{:S(2)}) copy-start(bf16[3,192,256]{2,1,0:T(8,128)(2,1)S(1)} %collective-permute-done.6.refs_2_) | copy-start | bytes 884740
  95.8 1.9 %collective-permute-start.9 = (bf16[3,192,256]{2,1,0:T(8,128)(2,1)}, bf16[3,192,256]{2,1,0:T(8,128)(2,1)}, u32[]{:S(2)}, u32[]{:S(2)}) collective-permute-start(bf16[3,192,256]{2,1,0:T(8,128)(2,1)} %get-tuple-element.50), channel_id=1, source_target_pairs={{0,1},{1,0},{2,3},{3,2},{4,5},{5,4},{6,7},{7,6},{8,9},{9,8},{10,11... | collective-permute-start | bytes 884744 | tf_op jit(solution)/shard_map/ppermute | solution.py:423
  95.8 10.6 %collective-permute-start.10 = (bf16[3,192,256]{2,1,0:T(8,128)(2,1)}, bf16[3,192,256]{2,1,0:T(8,128)(2,1)}, u32[]{:S(2)}, u32[]{:S(2)}) collective-permute-start(bf16[3,192,256]{2,1,0:T(8,128)(2,1)} %get-tuple-element.52), channel_id=1, source_target_pairs={{0,3},{1,2},{2,1},{3,0},{4,7},{5,6},{6,5},{7,4},{8,11},{9,10},{10,... | collective-permute-start | bytes 884744 | tf_op jit(solution)/shard_map/ppermute | solution.py:423
  96.5 15.8 %collective-permute-start.11 = (bf16[3,192,256]{2,1,0:T(8,128)(2,1)}, bf16[3,192,256]{2,1,0:T(8,128)(2,1)}, u32[]{:S(2)}, u32[]{:S(2)}) collective-permute-start(bf16[3,192,256]{2,1,0:T(8,128)(2,1)} %get-tuple-element.54), channel_id=1, source_target_pairs={{0,5},{1,4},{2,7},{3,6},{4,1},{5,0},{6,3},{7,2},{8,13},{9,12},{10,... | collective-permute-start | bytes 884744 | tf_op jit(solution)/shard_map/ppermute | solution.py:423
  97.7 14.5 %collective-permute-start.12 = (bf16[3,192,256]{2,1,0:T(8,128)(2,1)}, bf16[3,192,256]{2,1,0:T(8,128)(2,1)}, u32[]{:S(2)}, u32[]{:S(2)}) collective-permute-start(bf16[3,192,256]{2,1,0:T(8,128)(2,1)} %get-tuple-element.56), channel_id=1, source_target_pairs={{0,7},{1,6},{2,5},{3,4},{4,3},{5,2},{6,1},{7,0},{8,15},{9,14},{10,... | collective-permute-start | bytes 884744 | tf_op jit(solution)/shard_map/ppermute | solution.py:423
  99.7 12.5 %all-to-all-start.2 = ((f32[4,1,128]{2,1,0:T(1,128)}), f32[4,1,128]{2,1,0:T(1,128)S(1)}, u32[]{:S(2)}, u32[]{:S(2)}) async-start(f32[4,1,128]{2,1,0:T(1,128)} %get-tuple-element.35.grad_ref), calls=%async_computation.2 | async-start | bytes 4096 | tf_op jit(solution)/shard_map/all_to_all | solution.py:429
  112.2 0.6 copy-start.7

commit v6 on v5

--- a/solution.py
+++ b/solution.py
@@ -23,11 +23,13 @@
     return pltpu.CompilerParams(vmem_limit_bytes=size + (4 << 20))
 
 
-def own_rows_kernel(owner_ref, pairs_ref, rows_ref, out_ref, table_ref, scalar_ref, sems, table_sem):
+def own_rows_kernel(owner_ref, pairs_ref, rows_ref, out_ref, table_ref, held_ref, scalar_ref, sems, table_sem, load_sem):
     fields = rows_ref.shape[0]
     owners = out_ref.shape[0]
     lines, width = out_ref.shape[1] // CAP, out_ref.shape[2]
     total = pairs_ref.shape[1]
+    load = pltpu.make_async_copy(rows_ref, held_ref, load_sem)
+    load.start()
     local = pairs_ref[...] - owner_ref[0] * fields
     field = lax.broadcasted_iota(jnp.int32, (fields, total), 0)
     hit = ((local[0:1] == field) | (local[1:2] == field)).astype(BF16)
@@ -47,10 +49,11 @@
     copy = pltpu.make_async_copy(table_ref, scalar_ref, table_sem)
     copy.start()
     copy.wait()
+    load.wait()
 
     def move(d, c, f):
         place = out_ref.at[d, pl.ds(c * lines, lines), :]
-        return pltpu.make_async_copy(rows_ref.at[f], place, sems.at[d * CAP + c])
+        return pltpu.make_async_copy(held_ref.at[f], place, sems.at[d * CAP + c])
 
     @pl.loop(0, owners)
     def _(d):
@@ -73,11 +76,13 @@
             jax.ShapeDtypeStruct((8, 128), jnp.int32),
         ),
         in_specs=[SMEM, VMEM, HBM],
-        out_specs=(VMEM, VMEM),
+        out_specs=(HBM, VMEM),
         scratch_shapes=[
+            pltpu.VMEM(embeddings.shape, BF16),
             pltpu.SMEM((8, 128), jnp.int32),
             pltpu.SemaphoreType.DMA((owners * CAP,)),
             pltpu.SemaphoreType.DMA,
+            pltpu.SemaphoreType.DMA,
         ],
         compiler_params=limit(56 << 20),
         cost_estimate=CHEAP,
@@ -85,26 +90,33 @@
 
 
 def far_rows_kernel(ways, count, owner_ref, which_ref, table_ref, *refs):
-    sources, outs, sems = refs[:count], refs[count:-1], refs[-1]
+    sources, outs, (held_ref, sems, load_sems) = refs[:count], refs[count:-3], refs[-3:]
     lines = sources[0].shape[1]
 
-    def move(r, source, k, c, f):
+    def move(r, k, c, f):
         place = outs[k].at[c, pl.ds(r * lines, lines), :]
-        return pltpu.make_async_copy(source.at[f], place, sems.at[r, k * CAP + c])
+        return pltpu.make_async_copy(held_ref.at[r, f], place, sems.at[r, k * CAP + c])
+
+    def load(r, source):
+        return pltpu.make_async_copy(source, held_ref.at[r], load_sems.at[r])
 
     for r, choices in enumerate(ways):
         for at, source in enumerate(choices):
 
             @pl.when((len(choices) == 1) | (which_ref[0] == at))
             def _(r=r, source=source):
-                for k in range(len(outs)):
-                    for c in range(CAP):
-                        move(r, sources[source], k, c, table_ref[c, owner_ref[0] ^ k]).start()
+                load(r, sources[source]).start()
+
+    for r in range(len(ways)):
+        load(r, sources[0]).wait()
+        for k in range(len(outs)):
+            for c in range(CAP):
+                move(r, k, c, table_ref[c, owner_ref[0] ^ k]).start()
 
     for r in range(len(ways)):
         for k in range(len(outs)):
             for c in range(CAP):
-                move(r, sources[0], k, c, 0).wait()
+                move(r, k, c, 0).wait()
 
 
 def far_rows(ways, owner, which, table, sources, owners):
@@ -114,8 +126,12 @@
         functools.partial(far_rows_kernel, ways, len(sources)),
         out_shape=[jax.ShapeDtypeStruct(shape, BF16)] * owners,
         in_specs=[SMEM, SMEM, SMEM] + [HBM] * len(sources),
-        out_specs=[VMEM] * owners,
-        scratch_shapes=[pltpu.SemaphoreType.DMA((len(ways), owners * CAP))],
+        out_specs=[HBM] * owners,
+        scratch_shapes=[
+            pltpu.VMEM((len(ways), *sources[0].shape), BF16),
+            pltpu.SemaphoreType.DMA((len(ways), owners * CAP)),
+            pltpu.SemaphoreType.DMA((len(ways),)),
+        ],
         compiler_params=limit(56 << 20),
         cost_estimate=CHEAP,
     )(owner, which, table, *sources)

time: 123 us -> 122 us (level)
  no operation moved by 1% of the time
where the time goes in v6:
time: 122 us
  waiting for transfers between devices  52 us (43%)
  starting transfers between devices  34.2 us (28%)
  Pallas kernels  29 us (24%)
  local copies, waits for them, and re-layouts  3.66 us (3%)
  other arithmetic  1.92 us (2%)
    ppermute x8, waiting for transfers between devices, swap(): return lax.ppermute(rows, 'dp', [(i, i ^ k) for i in members])  39.7 us
    ppermute x8, starting transfers between devices, swap(): return lax.ppermute(rows, 'dp', [(i, i ^ k) for i in members])  16 us
    ppermute x7, waiting for transfers between devices, shards(): lax.ppermute(far[k], 'pair', [(i, i ^ k) for i in range(owners)])  12.3 us
    pallas_call x1, Pallas kernels, mat_grad_of(): pl.pallas_call(functools.partial(mat_grad_kernel, ways, chunk, len(raw)),...  9.39 us
    all_to_all x2, starting transfers between devices, exchange(): lax.all_to_all(lines, 'pair', split_axis=0, concat_axis=0, tiled=True)  9.17 us
    pallas_call x1, Pallas kernels, forward(): pl.pallas_call(functools.partial(forward_kernel, group), out_shape=jax.Sh...  8.52 us
    ppermute x7, starting transfers between devices, shards(): lax.ppermute(far[k], 'pair', [(i, i ^ k) for i in range(owners)])  5.75 us
    pallas_call x1, Pallas kernels, far_rows(): pl.pallas_call(functools.partial(far_rows_kernel, ways, len(sources)), ou...  3.88 us
  transfers between devices with their start and end apart: 18, of which 6 were waited for; matrix products, arithmetic and copies ran while one was open for 4% of the time, Pallas kernels for 13%

profile of v6, /device:TPU:0, one launch (start us, length us, event | category | flops | bytes accessed | tf_op | source)
XLA Modules:
  0.0 121.6 jit_solution(4290872444309644320)
XLA Ops:
  0.6 3.8 %shard_map.76 = (bf16[8,384,256]{2,1,0:T(8,128)(2,1)}, s32[8,128]{1,0:T(8,128)}) custom-call(s32[1]{0:T(128)} %bitcast.owner_ref, s32[2,384]{1,0:T(2,128)} %bitcast.15, bf16[16,128,256]{2,1,0:T(8,128)(2,1)} %rows_ref.1), custom_call_target="tpu_custom_call" | custom-call | tf_op jit(solution)/shard_map/pallas_call | solution.py:72
  4.5 5.3 %all-to-all-start = ((bf16[8,384,256]{2,1,0:T(8,128)(2,1)}), bf16[8,384,256]{2,1,0:T(8,128)(2,1)S(1)}, u32[]{:S(2)}, u32[]{:S(2)}) async-start(bf16[8,384,256]{2,1,0:T(8,128)(2,1)} %get-tuple-element.30), calls=%async_computation | async-start | bytes 3145728 | tf_op jit(solution)/shard_map/all_to_all | solution.py:415
  9.9 1.6 %collective-permute-start = (bf16[16,64,256]{2,1,0:T(8,128)(2,1)S(1)}, bf16[16,64,256]{2,1,0:T(8,128)(2,1)}, u32[]{:S(2)}, u32[]{:S(2)}) collective-permute-start(bf16[16,64,256]{2,1,0:T(8,128)(2,1)S(1)} %slice.6), channel_id=1, source_target_pairs={{0,8},{8,0},{16,24},{24,16},{1,9},{9,1},{17,25},{25,17},{2,10},{10... | collective-permute-start | bytes 1572872 | tf_op jit(solution)/shard_map/ppermute | solution.py:401
  11.5 2.5 %collective-permute-start.1 = (bf16[16,64,256]{2,1,0:T(8,128)(2,1)S(1)}, bf16[16,64,256]{2,1,0:T(8,128)(2,1)}, u32[]{:S(2)}, u32[]{:S(2)}) collective-permute-start(bf16[16,64,256]{2,1,0:T(8,128)(2,1)S(1)} %slice.6), channel_id=1, source_target_pairs={{0,24},{8,16},{16,8},{24,0},{1,25},{9,17},{17,9},{25,1},{2,26},{10... | collective-permute-start | bytes 1572872 | tf_op jit(solution)/shard_map/ppermute | solution.py:401
  14.0 0.8 constant_dynamic-slice_fusion
  15.4 9.0 %collective-permute-done.refs_0_ = bf16[16,64,256]{2,1,0:T(8,128)(2,1)} collective-permute-done((bf16[16,64,256]{2,1,0:T(8,128)(2,1)S(1)}, bf16[16,64,256]{2,1,0:T(8,128)(2,1)}, u32[]{:S(2)}, u32[]{:S(2)}) %collective-permute-start) | collective-permute-done | bytes 524320 | tf_op jit(solution)/shard_map/ppermute | solution.py:401
  24.4 1.5 %collective-permute-start.2 = (bf16[16,64,256]{2,1,0:T(8,128)(2,1)}, bf16[16,64,256]{2,1,0:T(8,128)(2,1)}, u32[]{:S(2)}, u32[]{:S(2)}) collective-permute-start(bf16[16,64,256]{2,1,0:T(8,128)(2,1)} %collective-permute-done.refs_0_), channel_id=1, source_target_pairs={{8,16},{16,8},{9,17},{17,9},{10,18},{18,10},{11,19},{19,11},{12,20... | collective-permute-start | bytes 1572872 | tf_op jit(solution)/shard_map/ppermute | solution.py:401
  25.8 11.9 %collective-permute-done.1.refs_1_ = bf16[16,64,256]{2,1,0:T(8,128)(2,1)} collective-permute-done((bf16[16,64,256]{2,1,0:T(8,128)(2,1)S(1)}, bf16[16,64,256]{2,1,0:T(8,128)(2,1)}, u32[]{:S(2)}, u32[]{:S(2)}) %collective-permute-start.1) | collective-permute-done | bytes 524320 | tf_op jit(solution)/shard_map/ppermute | solution.py:401
  37.8 1.3 %collective-permute-start.3 = (bf16[16,64,256]{2,1,0:T(8,128)(2,1)}, bf16[16,64,256]{2,1,0:T(8,128)(2,1)}, u32[]{:S(2)}, u32[]{:S(2)}) collective-permute-start(bf16[16,64,256]{2,1,0:T(8,128)(2,1)} %collective-permute-done.1.refs_1_), channel_id=1, source_target_pairs={{8,0},{16,24},{9,1},{17,25},{10,2},{18,26},{11,3},{19,27},{12,4},{... | collective-permute-start | bytes 1572872 | tf_op jit(solution)/shard_map/ppermute | solution.py:401
  39.3 0.8 select_reduce_fusion.1.slot_ref
  40.1 1.0 slice.7
  41.1 3.4 %collective-permute-start.4 = (bf16[24,64,256]{2,1,0:T(8,128)(2,1)}, bf16[24,64,256]{2,1,0:T(8,128)(2,1)S(1)}, u32[]{:S(2)}, u32[]{:S(2)}) collective-permute-start(bf16[24,64,256]{2,1,0:T(8,128)(2,1)} %slice.7), channel_id=1, source_target_pairs={{0,8},{8,0},{16,24},{24,16},{1,9},{9,1},{17,25},{25,17},{2,10},{10... | collective-permute-start | bytes 2359304 | tf_op jit(solution)/shard_map/ppermute | solution.py:401
  44.5 2.9 %collective-permute-start.5 = (bf16[24,64,256]{2,1,0:T(8,128)(2,1)}, bf16[24,64,256]{2,1,0:T(8,128)(2,1)S(1)}, u32[]{:S(2)}, u32[]{:S(2)}) collective-permute-start(bf16[24,64,256]{2,1,0:T(8,128)(2,1)} %slice.7), channel_id=1, source_target_pairs={{0,24},{8,16},{16,8},{24,0},{1,25},{9,17},{17,9},{25,1},{2,26},{10... | collective-permute-start | bytes 2359304 | tf_op jit(solution)/shard_map/ppermute | solution.py:401
  47.6 0.7 reshape.63.width_ref
  48.3 8.5 %shard_map.77 = bf16[8,400,256]{2,1,0:T(8,128)(2,1)} custom-call(s32[96]{0:T(128)} %select_reduce_fusion.1.slot_ref, s32[24]{0:T(128)} %reshape.63.width_ref, bf16[24,128,256]{2,1,0:T(8,128)(2,1)} %bitcast.13, bf16[48,256,256]{2,1,0:T(8,128)(2,1)} %mats_ref.1), custom_call_target="tpu_custom_call" | custom-call | tf_op jit(solution)/shard_map/pallas_call | solution.py:196
  56.8 3.9 %all-to-all-start.1 = ((bf16[8,400,256]{2,1,0:T(8,128)(2,1)}), bf16[8,400,256]{2,1,0:T(8,128)(2,1)S(1)}, u32[]{:S(2)}, u32[]{:S(2)}) async-start(bf16[8,400,256]{2,1,0:T(8,128)(2,1)} %shard_map.77), calls=%async_computation.1 | async-start | bytes 3276800 | tf_op jit(solution)/shard_map/all_to_all | solution.py:415
  60.7 3.9 %shard_map.79 = (bf16[3,192,256]{2,1,0:T(8,128)(2,1)}, bf16[3,192,256]{2,1,0:T(8,128)(2,1)}, bf16[3,192,256]{2,1,0:T(8,128)(2,1)}, bf16[3,192,256]{2,1,0:T(8,128...) custom-call(s32[1]{0:T(128)} %bitcast.owner_ref, ...), custom_call_target="tpu_custom_call" | custom-call | tf_op jit(solution)/shard_map/pallas_call | solution.py:125
  64.6 2.1 %collective-permute-start.6 = (bf16[3,192,256]{2,1,0:T(8,128)(2,1)}, bf16[3,192,256]{2,1,0:T(8,128)(2,1)S(1)}, u32[]{:S(2)}, u32[]{:S(2)}) collective-permute-start(bf16[3,192,256]{2,1,0:T(8,128)(2,1)} %get-tuple-element.41), channel_id=1, source_target_pairs={{0,2},{1,3},{2,0},{3,1},{4,6},{5,7},{6,4},{7,5},{8,10},{9,11},{10,... | collective-permute-start | bytes 884744 | tf_op jit(solution)/shard_map/ppermute | solution.py:435
  66.7 1.5 %collective-permute-start.7 = (bf16[3,192,256]{2,1,0:T(8,128)(2,1)}, bf16[3,192,256]{2,1,0:T(8,128)(2,1)}, u32[]{:S(2)}, u32[]{:S(2)}) collective-permute-start(bf16[3,192,256]{2,1,0:T(8,128)(2,1)} %get-tuple-element.42), channel_id=1, source_target_pairs={{0,4},{1,5},{2,6},{3,7},{4,0},{5,1},{6,2},{7,3},{8,12},{9,13},{10,... | collective-permute-start | bytes 884744 | tf_op jit(solution)/shard_map/ppermute | solution.py:435
  68.3 18.8 %collective-permute-done.4.refs_8_ = bf16[24,64,256]{2,1,0:T(8,128)(2,1)S(1)} collective-permute-done((bf16[24,64,256]{2,1,0:T(8,128)(2,1)}, bf16[24,64,256]{2,1,0:T(8,128)(2,1)S(1)}, u32[]{:S(2)}, u32[]{:S(2)}) %collective-permute-start.4) | collective-permute-done | bytes 786464 | tf_op jit(solution)/shard_map/ppermute | solution.py:401
  87.0 1.5 %collective-permute-start.13 = (bf16[24,64,256]{2,1,0:T(8,128)(2,1)S(1)}, bf16[24,64,256]{2,1,0:T(8,128)(2,1)}, u32[]{:S(2)}, u32[]{:S(2)}) collective-permute-start(bf16[24,64,256]{2,1,0:T(8,128)(2,1)S(1)} %collective-permute-done.4.refs_8_), channel_id=1, source_target_pairs={{8,16},{16,8},{9,17},{17,9},{10,18},{18,10},{11,19},{19,11},{12,20... | collective-permute-start | bytes 2359304 | tf_op jit(solution)/shard_map/ppermute | solution.py:401
  88.6 1.3 %collective-permute-start.14 = (bf16[24,64,256]{2,1,0:T(8,128)(2,1)S(1)}, bf16[24,64,256]{2,1,0:T(8,128)(2,1)}, u32[]{:S(2)}, u32[]{:S(2)}) collective-permute-start(bf16[24,64,256]{2,1,0:T(8,128)(2,1)S(1)} %collective-permute-done.5.refs_9_), channel_id=1, source_target_pairs={{8,0},{16,24},{9,1},{17,25},{10,2},{18,26},{11,3},{19,27},{12,4},{... | collective-permute-start | bytes 2359304 | tf_op jit(solution)/shard_map/ppermute | solution.py:401
  89.9 5.3 %collective-permute-done.8.refs_6_ = bf16[3,192,256]{2,1,0:T(8,128)(2,1)} collective-permute-done((bf16[3,192,256]{2,1,0:T(8,128)(2,1)}, bf16[3,192,256]{2,1,0:T(8,128)(2,1)}, u32[]{:S(2)}, u32[]{:S(2)}) %collective-permute-start.8) | collective-permute-done | bytes 294944 | tf_op jit(solution)/shard_map/ppermute | solution.py:435
  95.2 0.7 collective-permute-start.10
  95.9 1.2 %collective-permute-done.9.refs_1_ = bf16[3,192,256]{2,1,0:T(8,128)(2,1)} collective-permute-done((bf16[3,192,256]{2,1,0:T(8,128)(2,1)}, bf16[3,192,256]{2,1,0:T(8,128)(2,1)}, u32[]{:S(2)}, u32[]{:S(2)}) %collective-permute-start.9) | collective-permute-done | bytes 294944 | tf_op jit(solution)/shard_map/ppermute | solution.py:439
  97.1 1.4 %collective-permute-start.12 = (bf16[3,192,256]{2,1,0:T(8,128)(2,1)}, bf16[3,192,256]{2,1,0:T(8,128)(2,1)}, u32[]{:S(2)}, u32[]{:S(2)}) collective-permute-start(bf16[3,192,256]{2,1,0:T(8,128)(2,1)} %get-tuple-element.56), channel_id=1, source_target_pairs={{0,7},{1,6},{2,5},{3,4},{4,3},{5,2},{6,1},{7,0},{8,15},{9,14},{10,... | collective-permute-start | bytes 884744 | tf_op jit(solution)/shard_map/ppermute | solution.py:439
  98.5 0.6 shard_map.78
  99.1 3.2 %all-to-all-start.2 = ((f32[4,1,128]{2,1,0:T(1,128)}), f32[4,1,128]{2,1,0:T(1,128)S(1)}, u32[]{:S(2)}, u32[]{:S(2)}) async-start(f32[4,1,128]{2,1,0:T(1,128)} %get-tuple-element.35.grad_ref), calls=%async_computation.2 | async-start | bytes 4096 | tf_op jit(solution)/shard_map/all_to_all | solution.py:445
  102.4 0.6 pad_add_fusion.source_ref
  103.1 2.8 %shard_map.81 = f32[16,128,256]{2,1,0:T(8,128)} custom-call(s32[8,128]{1,0:T(8,128)S(1)} %copy-done, s32[16]{0:T(128)S(1)} %dynamic_slice.4.width_ref, bf16[8,400,256]{2,1,0:T(8,128)(2,1)S(1)} %all-to-all-done.1.back_ref, f32[4,1,128]{2,1,0:T(1,128)} %get-tuple-element.35.grad_ref), custom_call_target="tpu_custom_call" | custom-call | tf_op jit(solution)/shard_map/pallas_call | solution.py:261
  105.9 5.8 %collective-permute-done.11.refs_5_ = bf16[3,192,256]{2,1,0:T(8,128)(2,1)} collective-permute-done((bf16[3,192,256]{2,1,0:T(8,128)(2,1)}, bf16[3,192,256]{2,1,0:T(8,128)(2,1)}, u32[]{:S(2)}, u32[]{:S(2)}) %collective-permute-start.11) | collective-permute-done | bytes 294944 | tf_op jit(solution)/shard_map/ppermute | solution.py:439
  112.2 9.4 %shard_map.80 = bf16[48,64,256]{2,1,0:T(8,128)(2,1)} custom-call(s32[96]{0:T(128)} %select_reduce_fusion.1.slot_ref, s32[24]{0:T(128)} %reshape.63.width_ref, s32[1]{0:T(128)} %bitcast.5.which_ref, s32[4]{0:T(128)} %pad_add_fusion.source_ref, s32[1]{0:T(128)} %bitcast.10.first_ref, s32[1]{0:T(128)} %bitcast.owner_ref, f32[4,1,128]{2,1,0:T(1,128)} %copy-done.7, ...), custom_call_target="tpu_custom_call" | custom-call | tf_op jit(solution)/shard_map/pallas_call | solution.py:357
  (49 shorter events, 1.9 us)
Async XLA Ops:
  4.5 5.3 %copy-start.3 = (bf16[16,128,256]{2,1,0:T(8,128)(2,1)S(1)}, bf16[16,128,256]{2,1,0:T(8,128)(2,1)}, u32[]{:S(2)}) copy-start(bf16[16,128,256]{2,1,0:T(8,128)(2,1)} %rows_ref.1) | copy-start | bytes 3145732
  4.5 34.7 %copy-start.8 = (s32[128]{0:T(128)S(1)}, s32[128]{0:T(128)}, u32[]{:S(2)}) copy-start(s32[128]{0:T(128)} %param.6) | copy-start | bytes 1540
  4.5 35.5 %all-to-all-start = ((bf16[8,384,256]{2,1,0:T(8,128)(2,1)}), bf16[8,384,256]{2,1,0:T(8,128)(2,1)S(1)}, u32[]{:S(2)}, u32[]{:S(2)}) async-start(bf16[8,384,256]{2,1,0:T(8,128)(2,1)} %get-tuple-element.30), calls=%async_computation | async-start | bytes 3145728 | tf_op jit(solution)/shard_map/all_to_all | solution.py:415
  9.9 14.5 %collective-permute-start = (bf16[16,64,256]{2,1,0:T(8,128)(2,1)S(1)}, bf16[16,64,256]{2,1,0:T(8,128)(2,1)}, u32[]{:S(2)}, u32[]{:S(2)}) collective-permute-start(bf16[16,64,256]{2,1,0:T(8,128)(2,1)S(1)} %slice.6), channel_id=1, source_target_pairs={{0,8},{8,0},{16,24},{24,16},{1,9},{9,1},{17,25},{25,17},{2,10},{10... | collective-permute-start | bytes 1572872 | tf_op jit(solution)/shard_map/ppermute | solution.py:401
  11.5 26.2 %collective-permute-start.1 = (bf16[16,64,256]{2,1,0:T(8,128)(2,1)S(1)}, bf16[16,64,256]{2,1,0:T(8,128)(2,1)}, u32[]{:S(2)}, u32[]{:S(2)}) collective-permute-start(bf16[16,64,256]{2,1,0:T(8,128)(2,1)S(1)} %slice.6), channel_id=1, source_target_pairs={{0,24},{8,16},{16,8},{24,0},{1,25},{9,17},{17,9},{25,1},{2,26},{10... | collective-permute-start | bytes 1572872 | tf_op jit(solution)/shard_map/ppermute | solution.py:401
  24.4 32.4 %collective-permute-start.2 = (bf16[16,64,256]{2,1,0:T(8,128)(2,1)}, bf16[16,64,256]{2,1,0:T(8,128)(2,1)}, u32[]{:S(2)}, u32[]{:S(2)}) collective-permute-start(bf16[16,64,256]{2,1,0:T(8,128)(2,1)} %collective-permute-done.refs_0_), channel_id=1, source_target_pairs={{8,16},{16,8},{9,17},{17,9},{10,18},{18,10},{11,19},{19,11},{12,20... | collective-permute-start | bytes 1572872 | tf_op jit(solution)/shard_map/ppermute | solution.py:401
  37.8 19.1 %collective-permute-start.3 = (bf16[16,64,256]{2,1,0:T(8,128)(2,1)}, bf16[16,64,256]{2,1,0:T(8,128)(2,1)}, u32[]{:S(2)}, u32[]{:S(2)}) collective-permute-start(bf16[16,64,256]{2,1,0:T(8,128)(2,1)} %collective-permute-done.1.refs_1_), channel_id=1, source_target_pairs={{8,0},{16,24},{9,1},{17,25},{10,2},{18,26},{11,3},{19,27},{12,4},{... | collective-permute-start | bytes 1572872 | tf_op jit(solution)/shard_map/ppermute | solution.py:401
  40.1 8.2 %copy-start.2 = (bf16[8,384,256]{2,1,0:T(8,128)(2,1)}, bf16[8,384,256]{2,1,0:T(8,128)(2,1)S(1)}, u32[]{:S(2)}) copy-start(bf16[8,384,256]{2,1,0:T(8,128)(2,1)S(1)} %all-to-all-done) | copy-start | bytes 4718596
  41.1 46.0 %collective-permute-start.4 = (bf16[24,64,256]{2,1,0:T(8,128)(2,1)}, bf16[24,64,256]{2,1,0:T(8,128)(2,1)S(1)}, u32[]{:S(2)}, u32[]{:S(2)}) collective-permute-start(bf16[24,64,256]{2,1,0:T(8,128)(2,1)} %slice.7), channel_id=1, source_target_pairs={{0,8},{8,0},{16,24},{24,16},{1,9},{9,1},{17,25},{25,17},{2,10},{10... | collective-permute-start | bytes 2359304 | tf_op jit(solution)/shard_map/ppermute | solution.py:401
  44.5 44.1 %collective-permute-start.5 = (bf16[24,64,256]{2,1,0:T(8,128)(2,1)}, bf16[24,64,256]{2,1,0:T(8,128)(2,1)S(1)}, u32[]{:S(2)}, u32[]{:S(2)}) collective-permute-start(bf16[24,64,256]{2,1,0:T(8,128)(2,1)} %slice.7), channel_id=1, source_target_pairs={{0,24},{8,16},{16,8},{24,0},{1,25},{9,17},{17,9},{25,1},{2,26},{10... | collective-permute-start | bytes 2359304 | tf_op jit(solution)/shard_map/ppermute | solution.py:401
  56.8 41.7 %all-to-all-start.1 = ((bf16[8,400,256]{2,1,0:T(8,128)(2,1)}), bf16[8,400,256]{2,1,0:T(8,128)(2,1)S(1)}, u32[]{:S(2)}, u32[]{:S(2)}) async-start(bf16[8,400,256]{2,1,0:T(8,128)(2,1)} %shard_map.77), calls=%async_computation.1 | async-start | bytes 3276800 | tf_op jit(solution)/shard_map/all_to_all | solution.py:415
  60.7 37.9 %copy-start.1 = (s32[128]{0:T(128)S(1)}, s32[128]{0:T(128)}, u32[]{:S(2)}) copy-start(s32[128]{0:T(128)} %param.9) | copy-start | bytes 1540
  60.7 42.3 %copy-start = (s32[8,128]{1,0:T(8,128)S(1)}, s32[8,128]{1,0:T(8,128)}, u32[]{:S(2)}) copy-start(s32[8,128]{1,0:T(8,128)} %get-tuple-element.36.table_ref) | copy-start | bytes 12292
  64.6 25.3 %collective-permute-start.6 = (bf16[3,192,256]{2,1,0:T(8,128)(2,1)}, bf16[3,192,256]{2,1,0:T(8,128)(2,1)S(1)}, u32[]{:S(2)}, u32[]{:S(2)}) collective-permute-start(bf16[3,192,256]{2,1,0:T(8,128)(2,1)} %get-tuple-element.41), channel_id=1, source_target_pairs={{0,2},{1,3},{2,0},{3,1},{4,6},{5,7},{6,4},{7,5},{8,10},{9,11},{10,... | collective-permute-start | bytes 884744 | tf_op jit(solution)/shard_map/ppermute | solution.py:435
  66.7 23.2 %collective-permute-start.7 = (bf16[3,192,256]{2,1,0:T(8,128)(2,1)}, bf16[3,192,256]{2,1,0:T(8,128)(2,1)}, u32[]{:S(2)}, u32[]{:S(2)}) collective-permute-start(bf16[3,192,256]{2,1,0:T(8,128)(2,1)} %get-tuple-element.42), channel_id=1, source_target_pairs={{0,4},{1,5},{2,6},{3,7},{4,0},{5,1},{6,2},{7,3},{8,12},{9,13},{10,... | collective-permute-start | bytes 884744 | tf_op jit(solution)/shard_map/ppermute | solution.py:435
  68.2 27.0 %collective-permute-start.8 = (bf16[3,192,256]{2,1,0:T(8,128)(2,1)}, bf16[3,192,256]{2,1,0:T(8,128)(2,1)}, u32[]{:S(2)}, u32[]{:S(2)}) collective-permute-start(bf16[3,192,256]{2,1,0:T(8,128)(2,1)} %get-tuple-element.43), channel_id=1, source_target_pairs={{0,6},{1,7},{2,4},{3,5},{4,2},{5,3},{6,0},{7,1},{8,14},{9,15},{10,... | collective-permute-start | bytes 884744 | tf_op jit(solution)/shard_map/ppermute | solution.py:435
  87.0 18.8 %copy-start.4 = (bf16[24,64,256]{2,1,0:T(8,128)(2,1)}, bf16[24,64,256]{2,1,0:T(8,128)(2,1)S(1)}, u32[]{:S(2)}) copy-start(bf16[24,64,256]{2,1,0:T(8,128)(2,1)S(1)} %collective-permute-done.4.refs_8_) | copy-start | bytes 2359300
  87.0 24.6 %collective-permute-start.13 = (bf16[24,64,256]{2,1,0:T(8,128)(2,1)S(1)}, bf16[24,64,256]{2,1,0:T(8,128)(2,1)}, u32[]{:S(2)}, u32[]{:S(2)}) collective-permute-start(bf16[24,64,256]{2,1,0:T(8,128)(2,1)S(1)} %collective-permute-done.4.refs_8_), channel_id=1, source_target_pairs={{8,16},{16,8},{9,17},{17,9},{10,18},{18,10},{11,19},{19,11},{12,20... | collective-permute-start | bytes 2359304 | tf_op jit(solution)/shard_map/ppermute | solution.py:401
  88.6 17.3 %copy-start.5 = (bf16[24,64,256]{2,1,0:T(8,128)(2,1)}, bf16[24,64,256]{2,1,0:T(8,128)(2,1)S(1)}, u32[]{:S(2)}) copy-start(bf16[24,64,256]{2,1,0:T(8,128)(2,1)S(1)} %collective-permute-done.5.refs_9_) | copy-start | bytes 2359300
  88.6 23.1 %collective-permute-start.14 = (bf16[24,64,256]{2,1,0:T(8,128)(2,1)S(1)}, bf16[24,64,256]{2,1,0:T(8,128)(2,1)}, u32[]{:S(2)}, u32[]{:S(2)}) collective-permute-start(bf16[24,64,256]{2,1,0:T(8,128)(2,1)S(1)} %collective-permute-done.5.refs_9_), channel_id=1, source_target_pairs={{8,0},{16,24},{9,1},{17,25},{10,2},{18,26},{11,3},{19,27},{12,4},{... | collective-permute-start | bytes 2359304 | tf_op jit(solution)/shard_map/ppermute | solution.py:401
  89.9 16.0 %copy-start.6 = (bf16[3,192,256]{2,1,0:T(8,128)(2,1)}, bf16[3,192,256]{2,1,0:T(8,128)(2,1)S(1)}, u32[]{:S(2)}) copy-start(bf16[3,192,256]{2,1,0:T(8,128)(2,1)S(1)} %collective-permute-done.6.refs_2_) | copy-start | bytes 884740
  95.2 1.9 %collective-permute-start.9 = (bf16[3,192,256]{2,1,0:T(8,128)(2,1)}, bf16[3,192,256]{2,1,0:T(8,128)(2,1)}, u32[]{:S(2)}, u32[]{:S(2)}) collective-permute-start(bf16[3,192,256]{2,1,0:T(8,128)(2,1)} %get-tuple-element.50), channel_id=1, source_target_pairs={{0,1},{1,0},{2,3},{3,2},{4,5},{5,4},{6,7},{7,6},{8,9},{9,8},{10,11... | collective-permute-start | bytes 884744 | tf_op jit(solution)/shard_map/ppermute | solution.py:439
  95.2 10.6 %collective-permute-start.10 = (bf16[3,192,256]{2,1,0:T(8,128)(2,1)}, bf16[3,192,256]{2,1,0:T(8,128)(2,1)}, u32[]{:S(2)}, u32[]{:S(2)}) collective-permute-start(bf16[3,192,256]{2,1,0:T(8,128)(2,1)} %get-tuple-element.52), channel_id=1, source_target_pairs={{0,3},{1,2},{2,1},{3,0},{4,7},{5,6},{6,5},{7,4},{8,11},{9,10},{10,... | collective-permute-start | bytes 884744 | tf_op jit(solution)/shard_map/ppermute | solution.py:439
  95.9 15.8 %collective-permute-start.11 = (bf16[3,192,256]{2,1,0:T(8,128)(2,1)}, bf16[3,192,256]{2,1,0:T(8,128)(2,1)}, u32[]{:S(2)}, u32[]{:S(2)}) collective-permute-start(bf16[3,192,256]{2,1,0:T(8,128)(2,1)} %get-tuple-element.54), channel_id=1, source_target_pairs={{0,5},{1,4},{2,7},{3,6},{4,1},{5,0},{6,3},{7,2},{8,13},{9,12},{10,... | collective-permute-start | bytes 884744 | tf_op jit(solution)/shard_map/ppermute | solution.py:439
  97.1 14.5 %collective-permute-start.12 = (bf16[3,192,256]{2,1,0:T(8,128)(2,1)}, bf16[3,192,256]{2,1,0:T(8,128)(2,1)}, u32[]{:S(2)}, u32[]{:S(2)}) collective-permute-start(bf16[3,192,256]{2,1,0:T(8,128)(2,1)} %get-tuple-element.56), channel_id=1, source_target_pairs={{0,7},{1,6},{2,5},{3,4},{4,3},{5,2},{6,1},{7,0},{8,15},{9,14},{10,... | collective-permute-start | bytes 884744 | tf_op jit(solution)/shard_map/ppermute | solution.py:439
  99.1 12.5 %all-to-all-start.2 = ((f32[4,1,128]{2,1,0:T(1,128)}), f32[4,1,128]{2,1,0:T(1,128)S(1)}, u32[]{:S(2)}, u32[]{:S(2)}) async-start(f32[4,1,128]{2,1,0:T(1,128)} %get-tuple-element.35.grad_ref), calls=%async_computation.2 | async-start | bytes 4096 | tf_op jit(solution)/shard_map/all_to_all | solution.py:445
  111.6 0.6 copy-start.7

commit v7 on v6

--- a/solution.py
+++ b/solution.py
@@ -314,7 +314,7 @@
                 copy.wait()
             grad = grads_ref[source_ref[start + k]]
 
-            @pl.loop(0, slots, unroll=12)
+            @pl.loop(0, slots, unroll=24)
             def _(j, k=k, grad=grad):
                 x = x_ref[j, k * samples : (k + 1) * samples, :]
                 turned = lax.dot_general(pick, x, (((1,), (1,)), ((), ())), preferred_element_type=F32)
@@ -365,7 +365,7 @@
             pltpu.VMEM((pairs, rows, width), F32),
             pltpu.VMEM((pairs, rows, width), BF16),
             pltpu.SemaphoreType.DMA((chunk, 2 + len(raw))),
-            pltpu.SemaphoreType.DMA((pairs // 8,)),
+            pltpu.SemaphoreType.DMA((pairs // 16,)),
         ],
         compiler_params=limit(56 << 20),
         cost_estimate=CHEAP,

time: 122 us -> 121 us (level)
  no operation moved by 1% of the time
where the time goes in v7:
time: 121 us
  waiting for transfers between devices  52 us (43%)
  starting transfers between devices  34.2 us (28%)
  Pallas kernels  28.2 us (23%)
  local copies, waits for them, and re-layouts  3.66 us (3%)
  other arithmetic  1.92 us (2%)
    ppermute x8, waiting for transfers between devices, swap(): return lax.ppermute(rows, 'dp', [(i, i ^ k) for i in members])  39.7 us
    ppermute x8, starting transfers between devices, swap(): return lax.ppermute(rows, 'dp', [(i, i ^ k) for i in members])  16 us
    ppermute x7, waiting for transfers between devices, shards(): lax.ppermute(far[k], 'pair', [(i, i ^ k) for i in range(owners)])  12.3 us
    all_to_all x2, starting transfers between devices, exchange(): lax.all_to_all(lines, 'pair', split_axis=0, concat_axis=0, tiled=True)  9.17 us
    pallas_call x1, Pallas kernels, mat_grad_of(): pl.pallas_call(functools.partial(mat_grad_kernel, ways, chunk, len(raw)),...  8.61 us
    pallas_call x1, Pallas kernels, forward(): pl.pallas_call(functools.partial(forward_kernel, group), out_shape=jax.Sh...  8.52 us
    ppermute x7, starting transfers between devices, shards(): lax.ppermute(far[k], 'pair', [(i, i ^ k) for i in range(owners)])  5.75 us
    pallas_call x1, Pallas kernels, far_rows(): pl.pallas_call(functools.partial(far_rows_kernel, ways, len(sources)), ou...  3.88 us
  transfers between devices with their start and end apart: 18, of which 6 were waited for; matrix products, arithmetic and copies ran while one was open for 4% of the time, Pallas kernels for 13%

profile of v7, /device:TPU:0, one launch (start us, length us, event | category | flops | bytes accessed | tf_op | source)
XLA Modules:
  0.0 120.9 jit_solution(16813389185595492063)
XLA Ops:
  0.6 3.8 %shard_map.76 = (bf16[8,384,256]{2,1,0:T(8,128)(2,1)}, s32[8,128]{1,0:T(8,128)}) custom-call(s32[1]{0:T(128)} %bitcast.owner_ref, s32[2,384]{1,0:T(2,128)} %bitcast.15, bf16[16,128,256]{2,1,0:T(8,128)(2,1)} %rows_ref.1), custom_call_target="tpu_custom_call" | custom-call | tf_op jit(solution)/shard_map/pallas_call | solution.py:72
  4.5 5.3 %all-to-all-start = ((bf16[8,384,256]{2,1,0:T(8,128)(2,1)}), bf16[8,384,256]{2,1,0:T(8,128)(2,1)S(1)}, u32[]{:S(2)}, u32[]{:S(2)}) async-start(bf16[8,384,256]{2,1,0:T(8,128)(2,1)} %get-tuple-element.30), calls=%async_computation | async-start | bytes 3145728 | tf_op jit(solution)/shard_map/all_to_all | solution.py:415
  9.9 1.6 %collective-permute-start = (bf16[16,64,256]{2,1,0:T(8,128)(2,1)S(1)}, bf16[16,64,256]{2,1,0:T(8,128)(2,1)}, u32[]{:S(2)}, u32[]{:S(2)}) collective-permute-start(bf16[16,64,256]{2,1,0:T(8,128)(2,1)S(1)} %slice.6), channel_id=1, source_target_pairs={{0,8},{8,0},{16,24},{24,16},{1,9},{9,1},{17,25},{25,17},{2,10},{10... | collective-permute-start | bytes 1572872 | tf_op jit(solution)/shard_map/ppermute | solution.py:401
  11.5 2.5 %collective-permute-start.1 = (bf16[16,64,256]{2,1,0:T(8,128)(2,1)S(1)}, bf16[16,64,256]{2,1,0:T(8,128)(2,1)}, u32[]{:S(2)}, u32[]{:S(2)}) collective-permute-start(bf16[16,64,256]{2,1,0:T(8,128)(2,1)S(1)} %slice.6), channel_id=1, source_target_pairs={{0,24},{8,16},{16,8},{24,0},{1,25},{9,17},{17,9},{25,1},{2,26},{10... | collective-permute-start | bytes 1572872 | tf_op jit(solution)/shard_map/ppermute | solution.py:401
  14.0 0.8 constant_dynamic-slice_fusion
  15.4 9.0 %collective-permute-done.refs_0_ = bf16[16,64,256]{2,1,0:T(8,128)(2,1)} collective-permute-done((bf16[16,64,256]{2,1,0:T(8,128)(2,1)S(1)}, bf16[16,64,256]{2,1,0:T(8,128)(2,1)}, u32[]{:S(2)}, u32[]{:S(2)}) %collective-permute-start) | collective-permute-done | bytes 524320 | tf_op jit(solution)/shard_map/ppermute | solution.py:401
  24.4 1.5 %collective-permute-start.2 = (bf16[16,64,256]{2,1,0:T(8,128)(2,1)}, bf16[16,64,256]{2,1,0:T(8,128)(2,1)}, u32[]{:S(2)}, u32[]{:S(2)}) collective-permute-start(bf16[16,64,256]{2,1,0:T(8,128)(2,1)} %collective-permute-done.refs_0_), channel_id=1, source_target_pairs={{8,16},{16,8},{9,17},{17,9},{10,18},{18,10},{11,19},{19,11},{12,20... | collective-permute-start | bytes 1572872 | tf_op jit(solution)/shard_map/ppermute | solution.py:401
  25.8 11.9 %collective-permute-done.1.refs_1_ = bf16[16,64,256]{2,1,0:T(8,128)(2,1)} collective-permute-done((bf16[16,64,256]{2,1,0:T(8,128)(2,1)S(1)}, bf16[16,64,256]{2,1,0:T(8,128)(2,1)}, u32[]{:S(2)}, u32[]{:S(2)}) %collective-permute-start.1) | collective-permute-done | bytes 524320 | tf_op jit(solution)/shard_map/ppermute | solution.py:401
  37.8 1.3 %collective-permute-start.3 = (bf16[16,64,256]{2,1,0:T(8,128)(2,1)}, bf16[16,64,256]{2,1,0:T(8,128)(2,1)}, u32[]{:S(2)}, u32[]{:S(2)}) collective-permute-start(bf16[16,64,256]{2,1,0:T(8,128)(2,1)} %collective-permute-done.1.refs_1_), channel_id=1, source_target_pairs={{8,0},{16,24},{9,1},{17,25},{10,2},{18,26},{11,3},{19,27},{12,4},{... | collective-permute-start | bytes 1572872 | tf_op jit(solution)/shard_map/ppermute | solution.py:401
  39.3 0.8 select_reduce_fusion.1.slot_ref
  40.1 1.0 slice.7
  41.1 3.4 %collective-permute-start.4 = (bf16[24,64,256]{2,1,0:T(8,128)(2,1)}, bf16[24,64,256]{2,1,0:T(8,128)(2,1)S(1)}, u32[]{:S(2)}, u32[]{:S(2)}) collective-permute-start(bf16[24,64,256]{2,1,0:T(8,128)(2,1)} %slice.7), channel_id=1, source_target_pairs={{0,8},{8,0},{16,24},{24,16},{1,9},{9,1},{17,25},{25,17},{2,10},{10... | collective-permute-start | bytes 2359304 | tf_op jit(solution)/shard_map/ppermute | solution.py:401
  44.5 2.9 %collective-permute-start.5 = (bf16[24,64,256]{2,1,0:T(8,128)(2,1)}, bf16[24,64,256]{2,1,0:T(8,128)(2,1)S(1)}, u32[]{:S(2)}, u32[]{:S(2)}) collective-permute-start(bf16[24,64,256]{2,1,0:T(8,128)(2,1)} %slice.7), channel_id=1, source_target_pairs={{0,24},{8,16},{16,8},{24,0},{1,25},{9,17},{17,9},{25,1},{2,26},{10... | collective-permute-start | bytes 2359304 | tf_op jit(solution)/shard_map/ppermute | solution.py:401
  47.6 0.7 reshape.63.width_ref
  48.3 8.5 %shard_map.77 = bf16[8,400,256]{2,1,0:T(8,128)(2,1)} custom-call(s32[96]{0:T(128)} %select_reduce_fusion.1.slot_ref, s32[24]{0:T(128)} %reshape.63.width_ref, bf16[24,128,256]{2,1,0:T(8,128)(2,1)} %bitcast.13, bf16[48,256,256]{2,1,0:T(8,128)(2,1)} %mats_ref.1), custom_call_target="tpu_custom_call" | custom-call | tf_op jit(solution)/shard_map/pallas_call | solution.py:196
  56.8 3.9 %all-to-all-start.1 = ((bf16[8,400,256]{2,1,0:T(8,128)(2,1)}), bf16[8,400,256]{2,1,0:T(8,128)(2,1)S(1)}, u32[]{:S(2)}, u32[]{:S(2)}) async-start(bf16[8,400,256]{2,1,0:T(8,128)(2,1)} %shard_map.77), calls=%async_computation.1 | async-start | bytes 3276800 | tf_op jit(solution)/shard_map/all_to_all | solution.py:415
  60.7 3.9 %shard_map.79 = (bf16[3,192,256]{2,1,0:T(8,128)(2,1)}, bf16[3,192,256]{2,1,0:T(8,128)(2,1)}, bf16[3,192,256]{2,1,0:T(8,128)(2,1)}, bf16[3,192,256]{2,1,0:T(8,128...) custom-call(s32[1]{0:T(128)} %bitcast.owner_ref, ...), custom_call_target="tpu_custom_call" | custom-call | tf_op jit(solution)/shard_map/pallas_call | solution.py:125
  64.6 2.1 %collective-permute-start.6 = (bf16[3,192,256]{2,1,0:T(8,128)(2,1)}, bf16[3,192,256]{2,1,0:T(8,128)(2,1)S(1)}, u32[]{:S(2)}, u32[]{:S(2)}) collective-permute-start(bf16[3,192,256]{2,1,0:T(8,128)(2,1)} %get-tuple-element.41), channel_id=1, source_target_pairs={{0,2},{1,3},{2,0},{3,1},{4,6},{5,7},{6,4},{7,5},{8,10},{9,11},{10,... | collective-permute-start | bytes 884744 | tf_op jit(solution)/shard_map/ppermute | solution.py:435
  66.7 1.5 %collective-permute-start.7 = (bf16[3,192,256]{2,1,0:T(8,128)(2,1)}, bf16[3,192,256]{2,1,0:T(8,128)(2,1)}, u32[]{:S(2)}, u32[]{:S(2)}) collective-permute-start(bf16[3,192,256]{2,1,0:T(8,128)(2,1)} %get-tuple-element.42), channel_id=1, source_target_pairs={{0,4},{1,5},{2,6},{3,7},{4,0},{5,1},{6,2},{7,3},{8,12},{9,13},{10,... | collective-permute-start | bytes 884744 | tf_op jit(solution)/shard_map/ppermute | solution.py:435
  68.3 18.8 %collective-permute-done.4.refs_8_ = bf16[24,64,256]{2,1,0:T(8,128)(2,1)S(1)} collective-permute-done((bf16[24,64,256]{2,1,0:T(8,128)(2,1)}, bf16[24,64,256]{2,1,0:T(8,128)(2,1)S(1)}, u32[]{:S(2)}, u32[]{:S(2)}) %collective-permute-start.4) | collective-permute-done | bytes 786464 | tf_op jit(solution)/shard_map/ppermute | solution.py:401
  87.0 1.5 %collective-permute-start.13 = (bf16[24,64,256]{2,1,0:T(8,128)(2,1)S(1)}, bf16[24,64,256]{2,1,0:T(8,128)(2,1)}, u32[]{:S(2)}, u32[]{:S(2)}) collective-permute-start(bf16[24,64,256]{2,1,0:T(8,128)(2,1)S(1)} %collective-permute-done.4.refs_8_), channel_id=1, source_target_pairs={{8,16},{16,8},{9,17},{17,9},{10,18},{18,10},{11,19},{19,11},{12,20... | collective-permute-start | bytes 2359304 | tf_op jit(solution)/shard_map/ppermute | solution.py:401
  88.6 1.3 %collective-permute-start.14 = (bf16[24,64,256]{2,1,0:T(8,128)(2,1)S(1)}, bf16[24,64,256]{2,1,0:T(8,128)(2,1)}, u32[]{:S(2)}, u32[]{:S(2)}) collective-permute-start(bf16[24,64,256]{2,1,0:T(8,128)(2,1)S(1)} %collective-permute-done.5.refs_9_), channel_id=1, source_target_pairs={{8,0},{16,24},{9,1},{17,25},{10,2},{18,26},{11,3},{19,27},{12,4},{... | collective-permute-start | bytes 2359304 | tf_op jit(solution)/shard_map/ppermute | solution.py:401
  89.9 5.3 %collective-permute-done.8.refs_6_ = bf16[3,192,256]{2,1,0:T(8,128)(2,1)} collective-permute-done((bf16[3,192,256]{2,1,0:T(8,128)(2,1)}, bf16[3,192,256]{2,1,0:T(8,128)(2,1)}, u32[]{:S(2)}, u32[]{:S(2)}) %collective-permute-start.8) | collective-permute-done | bytes 294944 | tf_op jit(solution)/shard_map/ppermute | solution.py:435
  95.2 0.7 collective-permute-start.10
  95.9 1.2 %collective-permute-done.9.refs_1_ = bf16[3,192,256]{2,1,0:T(8,128)(2,1)} collective-permute-done((bf16[3,192,256]{2,1,0:T(8,128)(2,1)}, bf16[3,192,256]{2,1,0:T(8,128)(2,1)}, u32[]{:S(2)}, u32[]{:S(2)}) %collective-permute-start.9) | collective-permute-done | bytes 294944 | tf_op jit(solution)/shard_map/ppermute | solution.py:439
  97.1 1.4 %collective-permute-start.12 = (bf16[3,192,256]{2,1,0:T(8,128)(2,1)}, bf16[3,192,256]{2,1,0:T(8,128)(2,1)}, u32[]{:S(2)}, u32[]{:S(2)}) collective-permute-start(bf16[3,192,256]{2,1,0:T(8,128)(2,1)} %get-tuple-element.56), channel_id=1, source_target_pairs={{0,7},{1,6},{2,5},{3,4},{4,3},{5,2},{6,1},{7,0},{8,15},{9,14},{10,... | collective-permute-start | bytes 884744 | tf_op jit(solution)/shard_map/ppermute | solution.py:439
  98.5 0.6 shard_map.78
  99.1 3.2 %all-to-all-start.2 = ((f32[4,1,128]{2,1,0:T(1,128)}), f32[4,1,128]{2,1,0:T(1,128)S(1)}, u32[]{:S(2)}, u32[]{:S(2)}) async-start(f32[4,1,128]{2,1,0:T(1,128)} %get-tuple-element.35.grad_ref), calls=%async_computation.2 | async-start | bytes 4096 | tf_op jit(solution)/shard_map/all_to_all | solution.py:445
  102.4 0.6 pad_add_fusion.source_ref
  103.1 2.8 %shard_map.81 = f32[16,128,256]{2,1,0:T(8,128)} custom-call(s32[8,128]{1,0:T(8,128)S(1)} %copy-done, s32[16]{0:T(128)S(1)} %dynamic_slice.4.width_ref, bf16[8,400,256]{2,1,0:T(8,128)(2,1)S(1)} %all-to-all-done.1.back_ref, f32[4,1,128]{2,1,0:T(1,128)} %get-tuple-element.35.grad_ref), custom_call_target="tpu_custom_call" | custom-call | tf_op jit(solution)/shard_map/pallas_call | solution.py:261
  105.9 5.8 %collective-permute-done.11.refs_5_ = bf16[3,192,256]{2,1,0:T(8,128)(2,1)} collective-permute-done((bf16[3,192,256]{2,1,0:T(8,128)(2,1)}, bf16[3,192,256]{2,1,0:T(8,128)(2,1)}, u32[]{:S(2)}, u32[]{:S(2)}) %collective-permute-start.11) | collective-permute-done | bytes 294944 | tf_op jit(solution)/shard_map/ppermute | solution.py:439
  112.2 8.6 %shard_map.80 = bf16[48,64,256]{2,1,0:T(8,128)(2,1)} custom-call(s32[96]{0:T(128)} %select_reduce_fusion.1.slot_ref, s32[24]{0:T(128)} %reshape.63.width_ref, s32[1]{0:T(128)} %bitcast.5.which_ref, s32[4]{0:T(128)} %pad_add_fusion.source_ref, s32[1]{0:T(128)} %bitcast.10.first_ref, s32[1]{0:T(128)} %bitcast.owner_ref, f32[4,1,128]{2,1,0:T(1,128)} %copy-done.7, ...), custom_call_target="tpu_custom_call" | custom-call | tf_op jit(solution)/shard_map/pallas_call | solution.py:357
  (49 shorter events, 1.9 us)
Async XLA Ops:
  4.5 5.3 %copy-start.3 = (bf16[16,128,256]{2,1,0:T(8,128)(2,1)S(1)}, bf16[16,128,256]{2,1,0:T(8,128)(2,1)}, u32[]{:S(2)}) copy-start(bf16[16,128,256]{2,1,0:T(8,128)(2,1)} %rows_ref.1) | copy-start | bytes 3145732
  4.5 34.7 %copy-start.8 = (s32[128]{0:T(128)S(1)}, s32[128]{0:T(128)}, u32[]{:S(2)}) copy-start(s32[128]{0:T(128)} %param.6) | copy-start | bytes 1540
  4.5 35.5 %all-to-all-start = ((bf16[8,384,256]{2,1,0:T(8,128)(2,1)}), bf16[8,384,256]{2,1,0:T(8,128)(2,1)S(1)}, u32[]{:S(2)}, u32[]{:S(2)}) async-start(bf16[8,384,256]{2,1,0:T(8,128)(2,1)} %get-tuple-element.30), calls=%async_computation | async-start | bytes 3145728 | tf_op jit(solution)/shard_map/all_to_all | solution.py:415
  9.9 14.5 %collective-permute-start = (bf16[16,64,256]{2,1,0:T(8,128)(2,1)S(1)}, bf16[16,64,256]{2,1,0:T(8,128)(2,1)}, u32[]{:S(2)}, u32[]{:S(2)}) collective-permute-start(bf16[16,64,256]{2,1,0:T(8,128)(2,1)S(1)} %slice.6), channel_id=1, source_target_pairs={{0,8},{8,0},{16,24},{24,16},{1,9},{9,1},{17,25},{25,17},{2,10},{10... | collective-permute-start | bytes 1572872 | tf_op jit(solution)/shard_map/ppermute | solution.py:401
  11.5 26.2 %collective-permute-start.1 = (bf16[16,64,256]{2,1,0:T(8,128)(2,1)S(1)}, bf16[16,64,256]{2,1,0:T(8,128)(2,1)}, u32[]{:S(2)}, u32[]{:S(2)}) collective-permute-start(bf16[16,64,256]{2,1,0:T(8,128)(2,1)S(1)} %slice.6), channel_id=1, source_target_pairs={{0,24},{8,16},{16,8},{24,0},{1,25},{9,17},{17,9},{25,1},{2,26},{10... | collective-permute-start | bytes 1572872 | tf_op jit(solution)/shard_map/ppermute | solution.py:401
  24.4 32.4 %collective-permute-start.2 = (bf16[16,64,256]{2,1,0:T(8,128)(2,1)}, bf16[16,64,256]{2,1,0:T(8,128)(2,1)}, u32[]{:S(2)}, u32[]{:S(2)}) collective-permute-start(bf16[16,64,256]{2,1,0:T(8,128)(2,1)} %collective-permute-done.refs_0_), channel_id=1, source_target_pairs={{8,16},{16,8},{9,17},{17,9},{10,18},{18,10},{11,19},{19,11},{12,20... | collective-permute-start | bytes 1572872 | tf_op jit(solution)/shard_map/ppermute | solution.py:401
  37.8 19.1 %collective-permute-start.3 = (bf16[16,64,256]{2,1,0:T(8,128)(2,1)}, bf16[16,64,256]{2,1,0:T(8,128)(2,1)}, u32[]{:S(2)}, u32[]{:S(2)}) collective-permute-start(bf16[16,64,256]{2,1,0:T(8,128)(2,1)} %collective-permute-done.1.refs_1_), channel_id=1, source_target_pairs={{8,0},{16,24},{9,1},{17,25},{10,2},{18,26},{11,3},{19,27},{12,4},{... | collective-permute-start | bytes 1572872 | tf_op jit(solution)/shard_map/ppermute | solution.py:401
  40.1 8.2 %copy-start.2 = (bf16[8,384,256]{2,1,0:T(8,128)(2,1)}, bf16[8,384,256]{2,1,0:T(8,128)(2,1)S(1)}, u32[]{:S(2)}) copy-start(bf16[8,384,256]{2,1,0:T(8,128)(2,1)S(1)} %all-to-all-done) | copy-start | bytes 4718596
  41.1 46.0 %collective-permute-start.4 = (bf16[24,64,256]{2,1,0:T(8,128)(2,1)}, bf16[24,64,256]{2,1,0:T(8,128)(2,1)S(1)}, u32[]{:S(2)}, u32[]{:S(2)}) collective-permute-start(bf16[24,64,256]{2,1,0:T(8,128)(2,1)} %slice.7), channel_id=1, source_target_pairs={{0,8},{8,0},{16,24},{24,16},{1,9},{9,1},{17,25},{25,17},{2,10},{10... | collective-permute-start | bytes 2359304 | tf_op jit(solution)/shard_map/ppermute | solution.py:401
  44.5 44.1 %collective-permute-start.5 = (bf16[24,64,256]{2,1,0:T(8,128)(2,1)}, bf16[24,64,256]{2,1,0:T(8,128)(2,1)S(1)}, u32[]{:S(2)}, u32[]{:S(2)}) collective-permute-start(bf16[24,64,256]{2,1,0:T(8,128)(2,1)} %slice.7), channel_id=1, source_target_pairs={{0,24},{8,16},{16,8},{24,0},{1,25},{9,17},{17,9},{25,1},{2,26},{10... | collective-permute-start | bytes 2359304 | tf_op jit(solution)/shard_map/ppermute | solution.py:401
  56.8 41.7 %all-to-all-start.1 = ((bf16[8,400,256]{2,1,0:T(8,128)(2,1)}), bf16[8,400,256]{2,1,0:T(8,128)(2,1)S(1)}, u32[]{:S(2)}, u32[]{:S(2)}) async-start(bf16[8,400,256]{2,1,0:T(8,128)(2,1)} %shard_map.77), calls=%async_computation.1 | async-start | bytes 3276800 | tf_op jit(solution)/shard_map/all_to_all | solution.py:415
  60.7 37.9 %copy-start.1 = (s32[128]{0:T(128)S(1)}, s32[128]{0:T(128)}, u32[]{:S(2)}) copy-start(s32[128]{0:T(128)} %param.9) | copy-start | bytes 1540
  60.7 42.3 %copy-start = (s32[8,128]{1,0:T(8,128)S(1)}, s32[8,128]{1,0:T(8,128)}, u32[]{:S(2)}) copy-start(s32[8,128]{1,0:T(8,128)} %get-tuple-element.36.table_ref) | copy-start | bytes 12292
  64.6 25.3 %collective-permute-start.6 = (bf16[3,192,256]{2,1,0:T(8,128)(2,1)}, bf16[3,192,256]{2,1,0:T(8,128)(2,1)S(1)}, u32[]{:S(2)}, u32[]{:S(2)}) collective-permute-start(bf16[3,192,256]{2,1,0:T(8,128)(2,1)} %get-tuple-element.41), channel_id=1, source_target_pairs={{0,2},{1,3},{2,0},{3,1},{4,6},{5,7},{6,4},{7,5},{8,10},{9,11},{10,... | collective-permute-start | bytes 884744 | tf_op jit(solution)/shard_map/ppermute | solution.py:435
  66.7 23.2 %collective-permute-start.7 = (bf16[3,192,256]{2,1,0:T(8,128)(2,1)}, bf16[3,192,256]{2,1,0:T(8,128)(2,1)}, u32[]{:S(2)}, u32[]{:S(2)}) collective-permute-start(bf16[3,192,256]{2,1,0:T(8,128)(2,1)} %get-tuple-element.42), channel_id=1, source_target_pairs={{0,4},{1,5},{2,6},{3,7},{4,0},{5,1},{6,2},{7,3},{8,12},{9,13},{10,... | collective-permute-start | bytes 884744 | tf_op jit(solution)/shard_map/ppermute | solution.py:435
  68.2 27.0 %collective-permute-start.8 = (bf16[3,192,256]{2,1,0:T(8,128)(2,1)}, bf16[3,192,256]{2,1,0:T(8,128)(2,1)}, u32[]{:S(2)}, u32[]{:S(2)}) collective-permute-start(bf16[3,192,256]{2,1,0:T(8,128)(2,1)} %get-tuple-element.43), channel_id=1, source_target_pairs={{0,6},{1,7},{2,4},{3,5},{4,2},{5,3},{6,0},{7,1},{8,14},{9,15},{10,... | collective-permute-start | bytes 884744 | tf_op jit(solution)/shard_map/ppermute | solution.py:435
  87.0 18.8 %copy-start.4 = (bf16[24,64,256]{2,1,0:T(8,128)(2,1)}, bf16[24,64,256]{2,1,0:T(8,128)(2,1)S(1)}, u32[]{:S(2)}) copy-start(bf16[24,64,256]{2,1,0:T(8,128)(2,1)S(1)} %collective-permute-done.4.refs_8_) | copy-start | bytes 2359300
  87.0 24.6 %collective-permute-start.13 = (bf16[24,64,256]{2,1,0:T(8,128)(2,1)S(1)}, bf16[24,64,256]{2,1,0:T(8,128)(2,1)}, u32[]{:S(2)}, u32[]{:S(2)}) collective-permute-start(bf16[24,64,256]{2,1,0:T(8,128)(2,1)S(1)} %collective-permute-done.4.refs_8_), channel_id=1, source_target_pairs={{8,16},{16,8},{9,17},{17,9},{10,18},{18,10},{11,19},{19,11},{12,20... | collective-permute-start | bytes 2359304 | tf_op jit(solution)/shard_map/ppermute | solution.py:401
  88.6 17.3 %copy-start.5 = (bf16[24,64,256]{2,1,0:T(8,128)(2,1)}, bf16[24,64,256]{2,1,0:T(8,128)(2,1)S(1)}, u32[]{:S(2)}) copy-start(bf16[24,64,256]{2,1,0:T(8,128)(2,1)S(1)} %collective-permute-done.5.refs_9_) | copy-start | bytes 2359300
  88.6 23.1 %collective-permute-start.14 = (bf16[24,64,256]{2,1,0:T(8,128)(2,1)S(1)}, bf16[24,64,256]{2,1,0:T(8,128)(2,1)}, u32[]{:S(2)}, u32[]{:S(2)}) collective-permute-start(bf16[24,64,256]{2,1,0:T(8,128)(2,1)S(1)} %collective-permute-done.5.refs_9_), channel_id=1, source_target_pairs={{8,0},{16,24},{9,1},{17,25},{10,2},{18,26},{11,3},{19,27},{12,4},{... | collective-permute-start | bytes 2359304 | tf_op jit(solution)/shard_map/ppermute | solution.py:401
  89.9 16.0 %copy-start.6 = (bf16[3,192,256]{2,1,0:T(8,128)(2,1)}, bf16[3,192,256]{2,1,0:T(8,128)(2,1)S(1)}, u32[]{:S(2)}) copy-start(bf16[3,192,256]{2,1,0:T(8,128)(2,1)S(1)} %collective-permute-done.6.refs_2_) | copy-start | bytes 884740
  95.2 1.9 %collective-permute-start.9 = (bf16[3,192,256]{2,1,0:T(8,128)(2,1)}, bf16[3,192,256]{2,1,0:T(8,128)(2,1)}, u32[]{:S(2)}, u32[]{:S(2)}) collective-permute-start(bf16[3,192,256]{2,1,0:T(8,128)(2,1)} %get-tuple-element.50), channel_id=1, source_target_pairs={{0,1},{1,0},{2,3},{3,2},{4,5},{5,4},{6,7},{7,6},{8,9},{9,8},{10,11... | collective-permute-start | bytes 884744 | tf_op jit(solution)/shard_map/ppermute | solution.py:439
  95.2 10.6 %collective-permute-start.10 = (bf16[3,192,256]{2,1,0:T(8,128)(2,1)}, bf16[3,192,256]{2,1,0:T(8,128)(2,1)}, u32[]{:S(2)}, u32[]{:S(2)}) collective-permute-start(bf16[3,192,256]{2,1,0:T(8,128)(2,1)} %get-tuple-element.52), channel_id=1, source_target_pairs={{0,3},{1,2},{2,1},{3,0},{4,7},{5,6},{6,5},{7,4},{8,11},{9,10},{10,... | collective-permute-start | bytes 884744 | tf_op jit(solution)/shard_map/ppermute | solution.py:439
  95.9 15.8 %collective-permute-start.11 = (bf16[3,192,256]{2,1,0:T(8,128)(2,1)}, bf16[3,192,256]{2,1,0:T(8,128)(2,1)}, u32[]{:S(2)}, u32[]{:S(2)}) collective-permute-start(bf16[3,192,256]{2,1,0:T(8,128)(2,1)} %get-tuple-element.54), channel_id=1, source_target_pairs={{0,5},{1,4},{2,7},{3,6},{4,1},{5,0},{6,3},{7,2},{8,13},{9,12},{10,... | collective-permute-start | bytes 884744 | tf_op jit(solution)/shard_map/ppermute | solution.py:439
  97.1 14.5 %collective-permute-start.12 = (bf16[3,192,256]{2,1,0:T(8,128)(2,1)}, bf16[3,192,256]{2,1,0:T(8,128)(2,1)}, u32[]{:S(2)}, u32[]{:S(2)}) collective-permute-start(bf16[3,192,256]{2,1,0:T(8,128)(2,1)} %get-tuple-element.56), channel_id=1, source_target_pairs={{0,7},{1,6},{2,5},{3,4},{4,3},{5,2},{6,1},{7,0},{8,15},{9,14},{10,... | collective-permute-start | bytes 884744 | tf_op jit(solution)/shard_map/ppermute | solution.py:439
  99.1 12.5 %all-to-all-start.2 = ((f32[4,1,128]{2,1,0:T(1,128)}), f32[4,1,128]{2,1,0:T(1,128)S(1)}, u32[]{:S(2)}, u32[]{:S(2)}) async-start(f32[4,1,128]{2,1,0:T(1,128)} %get-tuple-element.35.grad_ref), calls=%async_computation.2 | async-start | bytes 4096 | tf_op jit(solution)/shard_map/all_to_all | solution.py:445
  111.6 0.6 copy-start.7

commit v8 on v7

--- a/solution.py
+++ b/solution.py
@@ -190,7 +190,7 @@
         sums_ref[o, lines : lines + NOTE, :] = note.astype(BF16)
 
 
-def forward(slot_index, slot_width, rows, mats, group=8):
+def forward(slot_index, slot_width, rows, mats, group=12):
     slots, samples, width = rows.shape
     sums = (slots // CAP, CAP * samples + NOTE, width)
     return pl.pallas_call(
@@ -423,7 +423,6 @@
     raw_steps = chain(embeddings[:, :RAW])
     close = next(raw_steps)
     received = exchange(picked).reshape(owners * CAP, samples, width)
-    received, close[:] = tie((received, close))
     raw = next(raw_steps)
     kept_steps = chain(received[:, RAW:])
     sums = forward(slot_index, slot_width, received, pair_mats)

time: 121 us -> 121 us (level)
  no operation moved by 1% of the time
where the time goes in v8:
time: 121 us
  waiting for transfers between devices  52 us (43%)
  starting transfers between devices  34.2 us (28%)
  Pallas kernels  28.1 us (23%)
  local copies, waits for them, and re-layouts  3.66 us (3%)
  other arithmetic  1.92 us (2%)
    ppermute x8, waiting for transfers between devices, swap(): return lax.ppermute(rows, 'dp', [(i, i ^ k) for i in members])  39.8 us
    ppermute x8, starting transfers between devices, swap(): return lax.ppermute(rows, 'dp', [(i, i ^ k) for i in members])  16 us
    ppermute x7, waiting for transfers between devices, shards(): lax.ppermute(far[k], 'pair', [(i, i ^ k) for i in range(owners)])  12.2 us
    all_to_all x2, starting transfers between devices, exchange(): lax.all_to_all(lines, 'pair', split_axis=0, concat_axis=0, tiled=True)  9.17 us
    pallas_call x1, Pallas kernels, mat_grad_of(): pl.pallas_call(functools.partial(mat_grad_kernel, ways, chunk, len(raw)),...  8.61 us
    pallas_call x1, Pallas kernels, forward(): pl.pallas_call(functools.partial(forward_kernel, group), out_shape=jax.Sh...  8.35 us
    ppermute x7, starting transfers between devices, shards(): lax.ppermute(far[k], 'pair', [(i, i ^ k) for i in range(owners)])  5.75 us
    pallas_call x1, Pallas kernels, far_rows(): pl.pallas_call(functools.partial(far_rows_kernel, ways, len(sources)), ou...  3.88 us
  transfers between devices with their start and end apart: 18, of which 6 were waited for; matrix products, arithmetic and copies ran while one was open for 4% of the time, Pallas kernels for 13%

profile of v8, /device:TPU:0, one launch (start us, length us, event | category | flops | bytes accessed | tf_op | source)
XLA Modules:
  0.0 120.7 jit_solution(12612662743805538640)
XLA Ops:
  0.6 3.8 %shard_map.76 = (bf16[8,384,256]{2,1,0:T(8,128)(2,1)}, s32[8,128]{1,0:T(8,128)}) custom-call(s32[1]{0:T(128)} %bitcast.owner_ref, s32[2,384]{1,0:T(2,128)} %bitcast.15, bf16[16,128,256]{2,1,0:T(8,128)(2,1)} %rows_ref.1), custom_call_target="tpu_custom_call" | custom-call | tf_op jit(solution)/shard_map/pallas_call | solution.py:72
  4.5 5.3 %all-to-all-start = ((bf16[8,384,256]{2,1,0:T(8,128)(2,1)}), bf16[8,384,256]{2,1,0:T(8,128)(2,1)S(1)}, u32[]{:S(2)}, u32[]{:S(2)}) async-start(bf16[8,384,256]{2,1,0:T(8,128)(2,1)} %get-tuple-element.29), calls=%async_computation | async-start | bytes 3145728 | tf_op jit(solution)/shard_map/all_to_all | solution.py:415
  9.9 1.6 %collective-permute-start = (bf16[16,64,256]{2,1,0:T(8,128)(2,1)S(1)}, bf16[16,64,256]{2,1,0:T(8,128)(2,1)}, u32[]{:S(2)}, u32[]{:S(2)}) collective-permute-start(bf16[16,64,256]{2,1,0:T(8,128)(2,1)S(1)} %slice.6), channel_id=1, source_target_pairs={{0,8},{8,0},{16,24},{24,16},{1,9},{9,1},{17,25},{25,17},{2,10},{10... | collective-permute-start | bytes 1572872 | tf_op jit(solution)/shard_map/ppermute | solution.py:401
  11.5 2.5 %collective-permute-start.1 = (bf16[16,64,256]{2,1,0:T(8,128)(2,1)S(1)}, bf16[16,64,256]{2,1,0:T(8,128)(2,1)}, u32[]{:S(2)}, u32[]{:S(2)}) collective-permute-start(bf16[16,64,256]{2,1,0:T(8,128)(2,1)S(1)} %slice.6), channel_id=1, source_target_pairs={{0,24},{8,16},{16,8},{24,0},{1,25},{9,17},{17,9},{25,1},{2,26},{10... | collective-permute-start | bytes 1572872 | tf_op jit(solution)/shard_map/ppermute | solution.py:401
  14.0 0.8 constant_dynamic-slice_fusion
  15.4 9.0 %collective-permute-done.refs_0_ = bf16[16,64,256]{2,1,0:T(8,128)(2,1)} collective-permute-done((bf16[16,64,256]{2,1,0:T(8,128)(2,1)S(1)}, bf16[16,64,256]{2,1,0:T(8,128)(2,1)}, u32[]{:S(2)}, u32[]{:S(2)}) %collective-permute-start) | collective-permute-done | bytes 524320 | tf_op jit(solution)/shard_map/ppermute | solution.py:401
  24.4 1.5 %collective-permute-start.2 = (bf16[16,64,256]{2,1,0:T(8,128)(2,1)}, bf16[16,64,256]{2,1,0:T(8,128)(2,1)}, u32[]{:S(2)}, u32[]{:S(2)}) collective-permute-start(bf16[16,64,256]{2,1,0:T(8,128)(2,1)} %collective-permute-done.refs_0_), channel_id=1, source_target_pairs={{8,16},{16,8},{9,17},{17,9},{10,18},{18,10},{11,19},{19,11},{12,20... | collective-permute-start | bytes 1572872 | tf_op jit(solution)/shard_map/ppermute | solution.py:401
  25.8 11.9 %collective-permute-done.1.refs_1_ = bf16[16,64,256]{2,1,0:T(8,128)(2,1)} collective-permute-done((bf16[16,64,256]{2,1,0:T(8,128)(2,1)S(1)}, bf16[16,64,256]{2,1,0:T(8,128)(2,1)}, u32[]{:S(2)}, u32[]{:S(2)}) %collective-permute-start.1) | collective-permute-done | bytes 524320 | tf_op jit(solution)/shard_map/ppermute | solution.py:401
  37.8 1.3 %collective-permute-start.3 = (bf16[16,64,256]{2,1,0:T(8,128)(2,1)}, bf16[16,64,256]{2,1,0:T(8,128)(2,1)}, u32[]{:S(2)}, u32[]{:S(2)}) collective-permute-start(bf16[16,64,256]{2,1,0:T(8,128)(2,1)} %collective-permute-done.1.refs_1_), channel_id=1, source_target_pairs={{8,0},{16,24},{9,1},{17,25},{10,2},{18,26},{11,3},{19,27},{12,4},{... | collective-permute-start | bytes 1572872 | tf_op jit(solution)/shard_map/ppermute | solution.py:401
  39.3 0.8 select_reduce_fusion.1.slot_ref
  40.1 1.0 slice.8
  41.1 3.4 %collective-permute-start.4 = (bf16[24,64,256]{2,1,0:T(8,128)(2,1)}, bf16[24,64,256]{2,1,0:T(8,128)(2,1)S(1)}, u32[]{:S(2)}, u32[]{:S(2)}) collective-permute-start(bf16[24,64,256]{2,1,0:T(8,128)(2,1)} %slice.8), channel_id=1, source_target_pairs={{0,8},{8,0},{16,24},{24,16},{1,9},{9,1},{17,25},{25,17},{2,10},{10... | collective-permute-start | bytes 2359304 | tf_op jit(solution)/shard_map/ppermute | solution.py:401
  44.5 2.9 %collective-permute-start.5 = (bf16[24,64,256]{2,1,0:T(8,128)(2,1)}, bf16[24,64,256]{2,1,0:T(8,128)(2,1)S(1)}, u32[]{:S(2)}, u32[]{:S(2)}) collective-permute-start(bf16[24,64,256]{2,1,0:T(8,128)(2,1)} %slice.8), channel_id=1, source_target_pairs={{0,24},{8,16},{16,8},{24,0},{1,25},{9,17},{17,9},{25,1},{2,26},{10... | collective-permute-start | bytes 2359304 | tf_op jit(solution)/shard_map/ppermute | solution.py:401
  47.6 0.7 reshape.63.width_ref
  48.3 8.4 %shard_map.77 = bf16[8,400,256]{2,1,0:T(8,128)(2,1)} custom-call(s32[96]{0:T(128)} %select_reduce_fusion.1.slot_ref, s32[24]{0:T(128)} %reshape.63.width_ref, bf16[24,128,256]{2,1,0:T(8,128)(2,1)} %bitcast.13, bf16[48,256,256]{2,1,0:T(8,128)(2,1)} %mats_ref.1), custom_call_target="tpu_custom_call" | custom-call | tf_op jit(solution)/shard_map/pallas_call | solution.py:196
  56.7 3.9 %all-to-all-start.1 = ((bf16[8,400,256]{2,1,0:T(8,128)(2,1)}), bf16[8,400,256]{2,1,0:T(8,128)(2,1)S(1)}, u32[]{:S(2)}, u32[]{:S(2)}) async-start(bf16[8,400,256]{2,1,0:T(8,128)(2,1)} %shard_map.77), calls=%async_computation.1 | async-start | bytes 3276800 | tf_op jit(solution)/shard_map/all_to_all | solution.py:415
  60.6 3.9 %shard_map.79 = (bf16[3,192,256]{2,1,0:T(8,128)(2,1)}, bf16[3,192,256]{2,1,0:T(8,128)(2,1)}, bf16[3,192,256]{2,1,0:T(8,128)(2,1)}, bf16[3,192,256]{2,1,0:T(8,128...) custom-call(s32[1]{0:T(128)} %bitcast.owner_ref, ...), custom_call_target="tpu_custom_call" | custom-call | tf_op jit(solution)/shard_map/pallas_call | solution.py:125
  64.4 2.1 %collective-permute-start.6 = (bf16[3,192,256]{2,1,0:T(8,128)(2,1)}, bf16[3,192,256]{2,1,0:T(8,128)(2,1)S(1)}, u32[]{:S(2)}, u32[]{:S(2)}) collective-permute-start(bf16[3,192,256]{2,1,0:T(8,128)(2,1)} %get-tuple-element.39), channel_id=1, source_target_pairs={{0,2},{1,3},{2,0},{3,1},{4,6},{5,7},{6,4},{7,5},{8,10},{9,11},{10,... | collective-permute-start | bytes 884744 | tf_op jit(solution)/shard_map/ppermute | solution.py:434
  66.6 1.5 %collective-permute-start.7 = (bf16[3,192,256]{2,1,0:T(8,128)(2,1)}, bf16[3,192,256]{2,1,0:T(8,128)(2,1)}, u32[]{:S(2)}, u32[]{:S(2)}) collective-permute-start(bf16[3,192,256]{2,1,0:T(8,128)(2,1)} %get-tuple-element.40), channel_id=1, source_target_pairs={{0,4},{1,5},{2,6},{3,7},{4,0},{5,1},{6,2},{7,3},{8,12},{9,13},{10,... | collective-permute-start | bytes 884744 | tf_op jit(solution)/shard_map/ppermute | solution.py:434
  68.1 18.9 %collective-permute-done.4.refs_8_ = bf16[24,64,256]{2,1,0:T(8,128)(2,1)S(1)} collective-permute-done((bf16[24,64,256]{2,1,0:T(8,128)(2,1)}, bf16[24,64,256]{2,1,0:T(8,128)(2,1)S(1)}, u32[]{:S(2)}, u32[]{:S(2)}) %collective-permute-start.4) | collective-permute-done | bytes 786464 | tf_op jit(solution)/shard_map/ppermute | solution.py:401
  87.0 1.5 %collective-permute-start.13 = (bf16[24,64,256]{2,1,0:T(8,128)(2,1)S(1)}, bf16[24,64,256]{2,1,0:T(8,128)(2,1)}, u32[]{:S(2)}, u32[]{:S(2)}) collective-permute-start(bf16[24,64,256]{2,1,0:T(8,128)(2,1)S(1)} %collective-permute-done.4.refs_8_), channel_id=1, source_target_pairs={{8,16},{16,8},{9,17},{17,9},{10,18},{18,10},{11,19},{19,11},{12,20... | collective-permute-start | bytes 2359304 | tf_op jit(solution)/shard_map/ppermute | solution.py:401
  88.6 1.3 %collective-permute-start.14 = (bf16[24,64,256]{2,1,0:T(8,128)(2,1)S(1)}, bf16[24,64,256]{2,1,0:T(8,128)(2,1)}, u32[]{:S(2)}, u32[]{:S(2)}) collective-permute-start(bf16[24,64,256]{2,1,0:T(8,128)(2,1)S(1)} %collective-permute-done.5.refs_9_), channel_id=1, source_target_pairs={{8,0},{16,24},{9,1},{17,25},{10,2},{18,26},{11,3},{19,27},{12,4},{... | collective-permute-start | bytes 2359304 | tf_op jit(solution)/shard_map/ppermute | solution.py:401
  89.9 5.1 %collective-permute-done.8.refs_6_ = bf16[3,192,256]{2,1,0:T(8,128)(2,1)} collective-permute-done((bf16[3,192,256]{2,1,0:T(8,128)(2,1)}, bf16[3,192,256]{2,1,0:T(8,128)(2,1)}, u32[]{:S(2)}, u32[]{:S(2)}) %collective-permute-start.8) | collective-permute-done | bytes 294944 | tf_op jit(solution)/shard_map/ppermute | solution.py:434
  95.1 0.7 collective-permute-start.10
  95.7 1.2 %collective-permute-done.9.refs_1_ = bf16[3,192,256]{2,1,0:T(8,128)(2,1)} collective-permute-done((bf16[3,192,256]{2,1,0:T(8,128)(2,1)}, bf16[3,192,256]{2,1,0:T(8,128)(2,1)}, u32[]{:S(2)}, u32[]{:S(2)}) %collective-permute-start.9) | collective-permute-done | bytes 294944 | tf_op jit(solution)/shard_map/ppermute | solution.py:438
  97.0 1.4 %collective-permute-start.12 = (bf16[3,192,256]{2,1,0:T(8,128)(2,1)}, bf16[3,192,256]{2,1,0:T(8,128)(2,1)}, u32[]{:S(2)}, u32[]{:S(2)}) collective-permute-start(bf16[3,192,256]{2,1,0:T(8,128)(2,1)} %get-tuple-element.54), channel_id=1, source_target_pairs={{0,7},{1,6},{2,5},{3,4},{4,3},{5,2},{6,1},{7,0},{8,15},{9,14},{10,... | collective-permute-start | bytes 884744 | tf_op jit(solution)/shard_map/ppermute | solution.py:438
  98.4 0.6 shard_map.78
  99.0 3.2 %all-to-all-start.2 = ((f32[4,1,128]{2,1,0:T(1,128)}), f32[4,1,128]{2,1,0:T(1,128)S(1)}, u32[]{:S(2)}, u32[]{:S(2)}) async-start(f32[4,1,128]{2,1,0:T(1,128)} %get-tuple-element.33.grad_ref), calls=%async_computation.2 | async-start | bytes 4096 | tf_op jit(solution)/shard_map/all_to_all | solution.py:444
  102.2 0.6 pad_add_fusion.source_ref
  102.9 2.8 %shard_map.81 = f32[16,128,256]{2,1,0:T(8,128)} custom-call(s32[8,128]{1,0:T(8,128)S(1)} %copy-done, s32[16]{0:T(128)S(1)} %dynamic_slice.4.width_ref, bf16[8,400,256]{2,1,0:T(8,128)(2,1)S(1)} %all-to-all-done.1.back_ref, f32[4,1,128]{2,1,0:T(1,128)} %get-tuple-element.33.grad_ref), custom_call_target="tpu_custom_call" | custom-call | tf_op jit(solution)/shard_map/pallas_call | solution.py:261
  105.7 5.8 %collective-permute-done.11.refs_5_ = bf16[3,192,256]{2,1,0:T(8,128)(2,1)} collective-permute-done((bf16[3,192,256]{2,1,0:T(8,128)(2,1)}, bf16[3,192,256]{2,1,0:T(8,128)(2,1)}, u32[]{:S(2)}, u32[]{:S(2)}) %collective-permute-start.11) | collective-permute-done | bytes 294944 | tf_op jit(solution)/shard_map/ppermute | solution.py:438
  112.1 8.6 %shard_map.80 = bf16[48,64,256]{2,1,0:T(8,128)(2,1)} custom-call(s32[96]{0:T(128)} %select_reduce_fusion.1.slot_ref, s32[24]{0:T(128)} %reshape.63.width_ref, s32[1]{0:T(128)} %bitcast.5.which_ref, s32[4]{0:T(128)} %pad_add_fusion.source_ref, s32[1]{0:T(128)} %bitcast.10.first_ref, s32[1]{0:T(128)} %bitcast.owner_ref, f32[4,1,128]{2,1,0:T(1,128)} %copy-done.7, ...), custom_call_target="tpu_custom_call" | custom-call | tf_op jit(solution)/shard_map/pallas_call | solution.py:357
  (49 shorter events, 1.9 us)
Async XLA Ops:
  4.5 5.3 %copy-start.3 = (bf16[16,128,256]{2,1,0:T(8,128)(2,1)S(1)}, bf16[16,128,256]{2,1,0:T(8,128)(2,1)}, u32[]{:S(2)}) copy-start(bf16[16,128,256]{2,1,0:T(8,128)(2,1)} %rows_ref.1) | copy-start | bytes 3145732
  4.5 34.7 %copy-start.8 = (s32[128]{0:T(128)S(1)}, s32[128]{0:T(128)}, u32[]{:S(2)}) copy-start(s32[128]{0:T(128)} %param.6) | copy-start | bytes 1540
  4.5 35.5 %all-to-all-start = ((bf16[8,384,256]{2,1,0:T(8,128)(2,1)}), bf16[8,384,256]{2,1,0:T(8,128)(2,1)S(1)}, u32[]{:S(2)}, u32[]{:S(2)}) async-start(bf16[8,384,256]{2,1,0:T(8,128)(2,1)} %get-tuple-element.29), calls=%async_computation | async-start | bytes 3145728 | tf_op jit(solution)/shard_map/all_to_all | solution.py:415
  9.9 14.5 %collective-permute-start = (bf16[16,64,256]{2,1,0:T(8,128)(2,1)S(1)}, bf16[16,64,256]{2,1,0:T(8,128)(2,1)}, u32[]{:S(2)}, u32[]{:S(2)}) collective-permute-start(bf16[16,64,256]{2,1,0:T(8,128)(2,1)S(1)} %slice.6), channel_id=1, source_target_pairs={{0,8},{8,0},{16,24},{24,16},{1,9},{9,1},{17,25},{25,17},{2,10},{10... | collective-permute-start | bytes 1572872 | tf_op jit(solution)/shard_map/ppermute | solution.py:401
  11.5 26.2 %collective-permute-start.1 = (bf16[16,64,256]{2,1,0:T(8,128)(2,1)S(1)}, bf16[16,64,256]{2,1,0:T(8,128)(2,1)}, u32[]{:S(2)}, u32[]{:S(2)}) collective-permute-start(bf16[16,64,256]{2,1,0:T(8,128)(2,1)S(1)} %slice.6), channel_id=1, source_target_pairs={{0,24},{8,16},{16,8},{24,0},{1,25},{9,17},{17,9},{25,1},{2,26},{10... | collective-permute-start | bytes 1572872 | tf_op jit(solution)/shard_map/ppermute | solution.py:401
  24.4 32.3 %collective-permute-start.2 = (bf16[16,64,256]{2,1,0:T(8,128)(2,1)}, bf16[16,64,256]{2,1,0:T(8,128)(2,1)}, u32[]{:S(2)}, u32[]{:S(2)}) collective-permute-start(bf16[16,64,256]{2,1,0:T(8,128)(2,1)} %collective-permute-done.refs_0_), channel_id=1, source_target_pairs={{8,16},{16,8},{9,17},{17,9},{10,18},{18,10},{11,19},{19,11},{12,20... | collective-permute-start | bytes 1572872 | tf_op jit(solution)/shard_map/ppermute | solution.py:401
  37.8 18.9 %collective-permute-start.3 = (bf16[16,64,256]{2,1,0:T(8,128)(2,1)}, bf16[16,64,256]{2,1,0:T(8,128)(2,1)}, u32[]{:S(2)}, u32[]{:S(2)}) collective-permute-start(bf16[16,64,256]{2,1,0:T(8,128)(2,1)} %collective-permute-done.1.refs_1_), channel_id=1, source_target_pairs={{8,0},{16,24},{9,1},{17,25},{10,2},{18,26},{11,3},{19,27},{12,4},{... | collective-permute-start | bytes 1572872 | tf_op jit(solution)/shard_map/ppermute | solution.py:401
  40.1 8.2 %copy-start.2 = (bf16[8,384,256]{2,1,0:T(8,128)(2,1)}, bf16[8,384,256]{2,1,0:T(8,128)(2,1)S(1)}, u32[]{:S(2)}) copy-start(bf16[8,384,256]{2,1,0:T(8,128)(2,1)S(1)} %all-to-all-done) | copy-start | bytes 4718596
  41.1 46.0 %collective-permute-start.4 = (bf16[24,64,256]{2,1,0:T(8,128)(2,1)}, bf16[24,64,256]{2,1,0:T(8,128)(2,1)S(1)}, u32[]{:S(2)}, u32[]{:S(2)}) collective-permute-start(bf16[24,64,256]{2,1,0:T(8,128)(2,1)} %slice.8), channel_id=1, source_target_pairs={{0,8},{8,0},{16,24},{24,16},{1,9},{9,1},{17,25},{25,17},{2,10},{10... | collective-permute-start | bytes 2359304 | tf_op jit(solution)/shard_map/ppermute | solution.py:401
  44.5 44.1 %collective-permute-start.5 = (bf16[24,64,256]{2,1,0:T(8,128)(2,1)}, bf16[24,64,256]{2,1,0:T(8,128)(2,1)S(1)}, u32[]{:S(2)}, u32[]{:S(2)}) collective-permute-start(bf16[24,64,256]{2,1,0:T(8,128)(2,1)} %slice.8), channel_id=1, source_target_pairs={{0,24},{8,16},{16,8},{24,0},{1,25},{9,17},{17,9},{25,1},{2,26},{10... | collective-permute-start | bytes 2359304 | tf_op jit(solution)/shard_map/ppermute | solution.py:401
  56.7 41.7 %all-to-all-start.1 = ((bf16[8,400,256]{2,1,0:T(8,128)(2,1)}), bf16[8,400,256]{2,1,0:T(8,128)(2,1)S(1)}, u32[]{:S(2)}, u32[]{:S(2)}) async-start(bf16[8,400,256]{2,1,0:T(8,128)(2,1)} %shard_map.77), calls=%async_computation.1 | async-start | bytes 3276800 | tf_op jit(solution)/shard_map/all_to_all | solution.py:415
  60.5 37.9 %copy-start.1 = (s32[128]{0:T(128)S(1)}, s32[128]{0:T(128)}, u32[]{:S(2)}) copy-start(s32[128]{0:T(128)} %param.9) | copy-start | bytes 1540
  60.5 42.3 %copy-start = (s32[8,128]{1,0:T(8,128)S(1)}, s32[8,128]{1,0:T(8,128)}, u32[]{:S(2)}) copy-start(s32[8,128]{1,0:T(8,128)} %get-tuple-element.34.table_ref) | copy-start | bytes 12292
  64.4 25.4 %collective-permute-start.6 = (bf16[3,192,256]{2,1,0:T(8,128)(2,1)}, bf16[3,192,256]{2,1,0:T(8,128)(2,1)S(1)}, u32[]{:S(2)}, u32[]{:S(2)}) collective-permute-start(bf16[3,192,256]{2,1,0:T(8,128)(2,1)} %get-tuple-element.39), channel_id=1, source_target_pairs={{0,2},{1,3},{2,0},{3,1},{4,6},{5,7},{6,4},{7,5},{8,10},{9,11},{10,... | collective-permute-start | bytes 884744 | tf_op jit(solution)/shard_map/ppermute | solution.py:434
  66.6 23.3 %collective-permute-start.7 = (bf16[3,192,256]{2,1,0:T(8,128)(2,1)}, bf16[3,192,256]{2,1,0:T(8,128)(2,1)}, u32[]{:S(2)}, u32[]{:S(2)}) collective-permute-start(bf16[3,192,256]{2,1,0:T(8,128)(2,1)} %get-tuple-element.40), channel_id=1, source_target_pairs={{0,4},{1,5},{2,6},{3,7},{4,0},{5,1},{6,2},{7,3},{8,12},{9,13},{10,... | collective-permute-start | bytes 884744 | tf_op jit(solution)/shard_map/ppermute | solution.py:434
  68.0 27.0 %collective-permute-start.8 = (bf16[3,192,256]{2,1,0:T(8,128)(2,1)}, bf16[3,192,256]{2,1,0:T(8,128)(2,1)}, u32[]{:S(2)}, u32[]{:S(2)}) collective-permute-start(bf16[3,192,256]{2,1,0:T(8,128)(2,1)} %get-tuple-element.41), channel_id=1, source_target_pairs={{0,6},{1,7},{2,4},{3,5},{4,2},{5,3},{6,0},{7,1},{8,14},{9,15},{10,... | collective-permute-start | bytes 884744 | tf_op jit(solution)/shard_map/ppermute | solution.py:434
  87.0 18.6 %copy-start.4 = (bf16[24,64,256]{2,1,0:T(8,128)(2,1)}, bf16[24,64,256]{2,1,0:T(8,128)(2,1)S(1)}, u32[]{:S(2)}) copy-start(bf16[24,64,256]{2,1,0:T(8,128)(2,1)S(1)} %collective-permute-done.4.refs_8_) | copy-start | bytes 2359300
  87.0 24.5 %collective-permute-start.13 = (bf16[24,64,256]{2,1,0:T(8,128)(2,1)S(1)}, bf16[24,64,256]{2,1,0:T(8,128)(2,1)}, u32[]{:S(2)}, u32[]{:S(2)}) collective-permute-start(bf16[24,64,256]{2,1,0:T(8,128)(2,1)S(1)} %collective-permute-done.4.refs_8_), channel_id=1, source_target_pairs={{8,16},{16,8},{9,17},{17,9},{10,18},{18,10},{11,19},{19,11},{12,20... | collective-permute-start | bytes 2359304 | tf_op jit(solution)/shard_map/ppermute | solution.py:401
  88.6 17.1 %copy-start.5 = (bf16[24,64,256]{2,1,0:T(8,128)(2,1)}, bf16[24,64,256]{2,1,0:T(8,128)(2,1)S(1)}, u32[]{:S(2)}) copy-start(bf16[24,64,256]{2,1,0:T(8,128)(2,1)S(1)} %collective-permute-done.5.refs_9_) | copy-start | bytes 2359300
  88.6 22.9 %collective-permute-start.14 = (bf16[24,64,256]{2,1,0:T(8,128)(2,1)S(1)}, bf16[24,64,256]{2,1,0:T(8,128)(2,1)}, u32[]{:S(2)}, u32[]{:S(2)}) collective-permute-start(bf16[24,64,256]{2,1,0:T(8,128)(2,1)S(1)} %collective-permute-done.5.refs_9_), channel_id=1, source_target_pairs={{8,0},{16,24},{9,1},{17,25},{10,2},{18,26},{11,3},{19,27},{12,4},{... | collective-permute-start | bytes 2359304 | tf_op jit(solution)/shard_map/ppermute | solution.py:401
  89.9 15.8 %copy-start.6 = (bf16[3,192,256]{2,1,0:T(8,128)(2,1)}, bf16[3,192,256]{2,1,0:T(8,128)(2,1)S(1)}, u32[]{:S(2)}) copy-start(bf16[3,192,256]{2,1,0:T(8,128)(2,1)S(1)} %collective-permute-done.6.refs_2_) | copy-start | bytes 884740
  95.0 1.9 %collective-permute-start.9 = (bf16[3,192,256]{2,1,0:T(8,128)(2,1)}, bf16[3,192,256]{2,1,0:T(8,128)(2,1)}, u32[]{:S(2)}, u32[]{:S(2)}) collective-permute-start(bf16[3,192,256]{2,1,0:T(8,128)(2,1)} %get-tuple-element.48), channel_id=1, source_target_pairs={{0,1},{1,0},{2,3},{3,2},{4,5},{5,4},{6,7},{7,6},{8,9},{9,8},{10,11... | collective-permute-start | bytes 884744 | tf_op jit(solution)/shard_map/ppermute | solution.py:438
  95.1 10.6 %collective-permute-start.10 = (bf16[3,192,256]{2,1,0:T(8,128)(2,1)}, bf16[3,192,256]{2,1,0:T(8,128)(2,1)}, u32[]{:S(2)}, u32[]{:S(2)}) collective-permute-start(bf16[3,192,256]{2,1,0:T(8,128)(2,1)} %get-tuple-element.50), channel_id=1, source_target_pairs={{0,3},{1,2},{2,1},{3,0},{4,7},{5,6},{6,5},{7,4},{8,11},{9,10},{10,... | collective-permute-start | bytes 884744 | tf_op jit(solution)/shard_map/ppermute | solution.py:438
  95.7 15.8 %collective-permute-start.11 = (bf16[3,192,256]{2,1,0:T(8,128)(2,1)}, bf16[3,192,256]{2,1,0:T(8,128)(2,1)}, u32[]{:S(2)}, u32[]{:S(2)}) collective-permute-start(bf16[3,192,256]{2,1,0:T(8,128)(2,1)} %get-tuple-element.52), channel_id=1, source_target_pairs={{0,5},{1,4},{2,7},{3,6},{4,1},{5,0},{6,3},{7,2},{8,13},{9,12},{10,... | collective-permute-start | bytes 884744 | tf_op jit(solution)/shard_map/ppermute | solution.py:438
  97.0 14.5 %collective-permute-start.12 = (bf16[3,192,256]{2,1,0:T(8,128)(2,1)}, bf16[3,192,256]{2,1,0:T(8,128)(2,1)}, u32[]{:S(2)}, u32[]{:S(2)}) collective-permute-start(bf16[3,192,256]{2,1,0:T(8,128)(2,1)} %get-tuple-element.54), channel_id=1, source_target_pairs={{0,7},{1,6},{2,5},{3,4},{4,3},{5,2},{6,1},{7,0},{8,15},{9,14},{10,... | collective-permute-start | bytes 884744 | tf_op jit(solution)/shard_map/ppermute | solution.py:438
  99.0 12.5 %all-to-all-start.2 = ((f32[4,1,128]{2,1,0:T(1,128)}), f32[4,1,128]{2,1,0:T(1,128)S(1)}, u32[]{:S(2)}, u32[]{:S(2)}) async-start(f32[4,1,128]{2,1,0:T(1,128)} %get-tuple-element.33.grad_ref), calls=%async_computation.2 | async-start | bytes 4096 | tf_op jit(solution)/shard_map/all_to_all | solution.py:444
  111.5 0.6 copy-start.7
